TPU v7x, 128 devices: a whole 4x4x4 slice. The times are simulated.
128 devices in a mesh: row: 16 (over y, x), col: 8 (over z, core).
Axes of the slice: x: 4, y: 4, z: 4, core: 2. Of those that a mesh axis runs over, the one named last changes fastest.
Arguments:
- a_blocks: bfloat16 [4096, 16, 128, 128], P(('row', 'col')), may hold values from -0.0625 to 0.0625
- omega: bfloat16 [32768, 256], P('col'), may hold values from -6 to 6
- route_dest: int32 [4096, 1], P(('row', 'col')), may hold values from 0 to 15; in each aligned block of 32 rows (0 to 31, 32 to 63, ...) at most 4 rows name the same one
- row_target: int32 [4096], P(('row', 'col')), may hold values from 0 to 63
- col_target: int32 [4096, 16], P(('row', 'col')), may hold values from 0 to 31
Outputs:
- basis: float32 [131072, 256], P(('row', 'col'))
- factor: float32 [256, 256], replicated
Inputs may be any that keep to these rules, and one draw needn't show every extreme that they name: `route_dest`: among the 32 rows of one device no value appears more than 4 times, and in some device's rows one value appears exactly 4 times.
All inputs are finite; a program needn't handle non-finite values.
Results may differ from a plain program's by a relative error of at most 0.003.
Values may be sent and summed in bfloat16 or wider, within the bound.
No kernel may reach another device: no remote copies, remote signals or barrier semaphores. Data moves between devices by JAX's collectives and lax.ppermute only.
A program may use at most 192 MiB of HBM per device.

v0:
```python
import jax
import jax.numpy as jnp
from jax import lax
from jax.sharding import PartitionSpec as P

RB_DEV = 8
CAP = 4


def swapped(value, axis, bit):
    mask = 2**bit
    pairs = [(source, source ^ mask) for source in range(lax.axis_size(axis))]
    return lax.ppermute(value, axis, pairs)


def product(left, right):
    return jnp.dot(left, right, precision=lax.Precision.HIGHEST, preferred_element_type=jnp.float32)


def upper_factor(gram):
    order = gram.shape[0]
    lower = jnp.linalg.cholesky(gram)
    identity = jnp.eye(order, dtype=jnp.float32)
    inverse = jax.scipy.linalg.solve_triangular(lower, identity, lower=True)
    return (lower.T, inverse.T)


def cholesky_twice(matrix):
    first, first_inv = upper_factor(product(matrix.T, matrix))
    once = product(matrix, first_inv)
    second, second_inv = upper_factor(product(once.T, once))
    return (product(once, second_inv), product(second, first))


def merge_pair(own_factor, peer_factor):
    first, first_inv = upper_factor(
        product(own_factor.T, own_factor) + product(peer_factor.T, peer_factor)
    )
    own_once = product(own_factor, first_inv)
    peer_once = product(peer_factor, first_inv)
    second, second_inv = upper_factor(
        product(own_once.T, own_once) + product(peer_once.T, peer_once)
    )
    return (product(second, first), product(own_once, second_inv))


def body(a_blocks, omega, route_dest, row_target, col_target):
    targets_here, group_size, block_order, _ = a_blocks.shape
    sketch_width = omega.shape[1]
    row_count = lax.axis_size("row")
    slab = omega.reshape(omega.shape[0] // block_order, block_order, sketch_width)
    picked = slab[col_target]
    partial_value = jnp.einsum(
        "tgij,tgjk->tik", a_blocks, picked, preferred_element_type=jnp.float32
    ).astype(jnp.bfloat16)
    destination = route_dest[:, 0]
    positions = jnp.arange(targets_here, dtype=jnp.int32)
    same_owner = destination[:, None] == destination[None, :]
    earlier = positions[None, :] < positions[:, None]
    rank = jnp.sum(jnp.logical_and(same_owner, earlier), axis=1)
    slot_of = destination * CAP + rank
    slot_ids = jnp.arange(row_count * CAP, dtype=jnp.int32)
    matches = slot_of[None, :] == slot_ids[:, None]
    filled = jnp.any(matches, axis=1)
    source = jnp.sum(jnp.where(matches, positions[None, :], 0), axis=1)
    send_values = jnp.where(
        filled[:, None, None], partial_value[source], jnp.zeros((), jnp.bfloat16)
    )
    send_values = send_values.reshape(row_count, CAP, block_order, sketch_width)
    send_rows = jnp.where(filled, row_target[source], -1).reshape(row_count, CAP)
    got_values, got_rows = (
        lax.all_to_all(send_values, "row", split_axis=0, concat_axis=0, tiled=True),
        lax.all_to_all(send_rows, "row", split_axis=0, concat_axis=0, tiled=True),
    )
    flat_values = got_values.reshape(row_count * CAP, block_order, sketch_width)
    flat_rows = got_rows.reshape(row_count * CAP)
    count = lax.axis_size("col") * (RB_DEV * block_order)
    block_total = count // block_order
    wanted = jnp.arange(block_total, dtype=jnp.int32)
    selector = (flat_rows[None, :] == wanted[:, None]).astype(jnp.bfloat16)
    term = jnp.einsum("bs,sik->bik", selector, flat_values, preferred_element_type=jnp.float32)
    sketch = lax.psum_scatter(
        term.reshape(count, sketch_width), "col", scatter_dimension=0, tiled=True
    )
    basis, factor = cholesky_twice(sketch)
    depth_total = lax.axis_size(("row", "col")).bit_length() - 1
    for depth_level in range(depth_total):
        peer_factor = swapped(factor, ("row", "col"), depth_level)
        factor, own_half = merge_pair(factor, peer_factor)
        basis = product(basis, own_half)
    total_rows = float(sketch.shape[0] * lax.axis_size(("row", "col")))
    scale_root = jnp.sqrt(jnp.float32(total_rows))
    return (basis * scale_root, factor / scale_root)


def solution(mesh):
    return jax.shard_map(
        body,
        mesh=mesh,
        in_specs=(
            P(("row", "col"), None, None, None),
            P("col", None),
            P(("row", "col"), None),
            P(("row", "col")),
            P(("row", "col"), None),
        ),
        out_specs=(P(("row", "col"), None), P()),
        check_vma=False,
    )
```

profile of v0, /device:TPU:1, one launch (start us, length us, event | category | flops | bytes accessed | tf_op | source)
XLA Modules:
  0.0 1277.4 jit_solution(8655472719050406391)
XLA Ops:
  19.8 16.1 %gather_fusion.1 = bf16[512,128,256]{2,1,0:T(8,128)(2,1)} fusion(bf16[32,128,256]{2,1,0:T(8,128)(2,1)S(1)} %bitcast.619, s32[1024]{0:T(1024)S(1)} %pad_clamp_fusion), kind=kCustom, calls=%fused_computation.1 | custom fusion | bytes 67110912 | tf_op jit(solution)/shard_map/gather | solution.py:52
  35.8 18.2 %fusion = bf16[32,128,256]{1,2,0:T(8,128)(2,1)S(1)} fusion(bf16[32,16,128,256]{3,2,1,0:T(8,128)(2,1)} %bitcast.620, bf16[32,16,128,128]{3,2,1,0:T(8,128)(2,1)} %param.8), kind=kOutput, calls=%fused_computation.37 | convolution fusion | flops 4296015872 | bytes 52428800 | tf_op jit(solution)/shard_map/tgij,tgjk->tik/dot_general | solution.py:53
  69.6 59.3 %all-to-all-done.1 = bf16[16,4,128,256]{2,3,1,0:T(8,128)(2,1)} async-done(((bf16[16,4,128,256]{2,3,1,0:T(8,128)(2,1)}), bf16[16,4,128,256]{2,3,1,0:T(8,128)(2,1)}, u32[]{:S(2)}, u32[]{:S(2)}) %all-to-all-start.1) | async-done | bytes 4194336 | tf_op jit(solution)/shard_map/all_to_all | solution.py:72
  147.5 53.9 %reduce-scatter.2.cloned.1.call-done = f32[1024,256]{1,0:T(8,128)} async-done(((f32[8192,256]{1,0:T(8,128)}), f32[1024,256]{1,0:T(8,128)}) %reduce-scatter.2.cloned.1.call-update) | async-done | bytes 1048592 | tf_op jit(solution)/shard_map/reduce_scatter | solution.py:82
  205.3 11.7 cholesky.718
  227.6 11.7 cholesky.735
  245.6 20.1 %custom-call.42 = f32[2,128,128]{1,2,0:T(8,128)S(1)} custom-call(f32[2,128,128]{2,1,0:T(8,128)S(1)} %get-tuple-element.102), custom_call_target="InvertDiagBlocksLowerTriangular" | custom-call | tf_op jit(solution)/shard_map/jit(_solve_triangular)/triangular_solve | solution.py:24
  269.8 11.7 cholesky.752
  291.8 11.9 cholesky.769
  313.7 19.7 %custom-call.44 = f32[2,128,128]{1,2,0:T(8,128)S(1)} custom-call(f32[2,128,128]{2,1,0:T(8,128)S(1)} %get-tuple-element.103), custom_call_target="InvertDiagBlocksLowerTriangular" | custom-call | tf_op jit(solution)/shard_map/jit(_solve_triangular)/triangular_solve | solution.py:24
  337.1 11.7 cholesky.786
  359.1 12.1 cholesky.803
  377.9 19.7 %custom-call.46 = f32[2,128,128]{1,2,0:T(8,128)S(1)} custom-call(f32[2,128,128]{2,1,0:T(8,128)S(1)} %get-tuple-element.104), custom_call_target="InvertDiagBlocksLowerTriangular" | custom-call | tf_op jit(solution)/shard_map/jit(_solve_triangular)/triangular_solve | solution.py:24
  400.7 11.7 cholesky.820
  422.8 11.8 cholesky.837
  441.8 19.7 %custom-call.48 = f32[2,128,128]{1,2,0:T(8,128)S(1)} custom-call(f32[2,128,128]{2,1,0:T(8,128)S(1)} %get-tuple-element.105), custom_call_target="InvertDiagBlocksLowerTriangular" | custom-call | tf_op jit(solution)/shard_map/jit(_solve_triangular)/triangular_solve | solution.py:24
  471.6 11.7 cholesky.854
  493.7 12.1 cholesky.871
  512.5 19.7 %custom-call.50 = f32[2,128,128]{1,2,0:T(8,128)S(1)} custom-call(f32[2,128,128]{2,1,0:T(8,128)S(1)} %get-tuple-element.106), custom_call_target="InvertDiagBlocksLowerTriangular" | custom-call | tf_op jit(solution)/shard_map/jit(_solve_triangular)/triangular_solve | solution.py:24
  535.3 11.7 cholesky.888
  557.4 11.8 cholesky.905
  576.4 19.7 %custom-call.52 = f32[2,128,128]{1,2,0:T(8,128)S(1)} custom-call(f32[2,128,128]{2,1,0:T(8,128)S(1)} %get-tuple-element.107), custom_call_target="InvertDiagBlocksLowerTriangular" | custom-call | tf_op jit(solution)/shard_map/jit(_solve_triangular)/triangular_solve | solution.py:24
  606.8 11.7 cholesky.922
  628.9 12.1 cholesky.939
  647.7 19.7 %custom-call.54 = f32[2,128,128]{1,2,0:T(8,128)S(1)} custom-call(f32[2,128,128]{2,1,0:T(8,128)S(1)} %get-tuple-element.108), custom_call_target="InvertDiagBlocksLowerTriangular" | custom-call | tf_op jit(solution)/shard_map/jit(_solve_triangular)/triangular_solve | solution.py:24
  670.5 11.7 cholesky.956
  692.6 11.8 cholesky.973
  711.6 19.7 %custom-call.56 = f32[2,128,128]{1,2,0:T(8,128)S(1)} custom-call(f32[2,128,128]{2,1,0:T(8,128)S(1)} %get-tuple-element.109), custom_call_target="InvertDiagBlocksLowerTriangular" | custom-call | tf_op jit(solution)/shard_map/jit(_solve_triangular)/triangular_solve | solution.py:24
  739.6 11.7 cholesky.990
  761.7 12.1 cholesky.1007
  780.4 19.7 %custom-call.58 = f32[2,128,128]{1,2,0:T(8,128)S(1)} custom-call(f32[2,128,128]{2,1,0:T(8,128)S(1)} %get-tuple-element.110), custom_call_target="InvertDiagBlocksLowerTriangular" | custom-call | tf_op jit(solution)/shard_map/jit(_solve_triangular)/triangular_solve | solution.py:24
  803.3 11.7 cholesky.1024
  825.3 11.8 cholesky.1041
  844.4 19.7 %custom-call.60 = f32[2,128,128]{1,2,0:T(8,128)S(1)} custom-call(f32[2,128,128]{2,1,0:T(8,128)S(1)} %get-tuple-element.111), custom_call_target="InvertDiagBlocksLowerTriangular" | custom-call | tf_op jit(solution)/shard_map/jit(_solve_triangular)/triangular_solve | solution.py:24
  873.0 11.7 cholesky.1058
  895.0 12.1 cholesky.1075
  913.8 19.7 %custom-call.62 = f32[2,128,128]{1,2,0:T(8,128)S(1)} custom-call(f32[2,128,128]{2,1,0:T(8,128)S(1)} %get-tuple-element.112), custom_call_target="InvertDiagBlocksLowerTriangular" | custom-call | tf_op jit(solution)/shard_map/jit(_solve_triangular)/triangular_solve | solution.py:24
  936.6 11.7 cholesky.1092
  958.7 11.8 cholesky.1109
  977.7 19.7 %custom-call.64 = f32[2,128,128]{1,2,0:T(8,128)S(1)} custom-call(f32[2,128,128]{2,1,0:T(8,128)S(1)} %get-tuple-element.113), custom_call_target="InvertDiagBlocksLowerTriangular" | custom-call | tf_op jit(solution)/shard_map/jit(_solve_triangular)/triangular_solve | solution.py:24
  1026.9 12.1 cholesky.1143
  1045.7 19.7 %custom-call.66 = f32[2,128,128]{1,2,0:T(8,128)S(1)} custom-call(f32[2,128,128]{2,1,0:T(8,128)S(1)} %get-tuple-element.114), custom_call_target="InvertDiagBlocksLowerTriangular" | custom-call | tf_op jit(solution)/shard_map/jit(_solve_triangular)/triangular_solve | solution.py:24
  1090.6 11.8 cholesky.1177
  1109.6 19.7 %custom-call.68 = f32[2,128,128]{1,2,0:T(8,128)S(1)} custom-call(f32[2,128,128]{2,1,0:T(8,128)S(1)} %get-tuple-element.115), custom_call_target="InvertDiagBlocksLowerTriangular" | custom-call | tf_op jit(solution)/shard_map/jit(_solve_triangular)/triangular_solve | solution.py:24
  1160.3 12.1 cholesky.1211
  1179.0 19.7 %custom-call.70 = f32[2,128,128]{1,2,0:T(8,128)S(1)} custom-call(f32[2,128,128]{2,1,0:T(8,128)S(1)} %get-tuple-element.116), custom_call_target="InvertDiagBlocksLowerTriangular" | custom-call | tf_op jit(solution)/shard_map/jit(_solve_triangular)/triangular_solve | solution.py:24
  1226.3 11.9 cholesky.1245
  1246.2 19.7 %custom-call.72 = f32[2,128,128]{1,2,0:T(8,128)S(1)} custom-call(f32[2,128,128]{2,1,0:T(8,128)S(1)} %get-tuple-element.117), custom_call_target="InvertDiagBlocksLowerTriangular" | custom-call | tf_op jit(solution)/shard_map/jit(_solve_triangular)/triangular_solve | solution.py:24
  (491 shorter events, 509.1 us)
Async XLA Ops:
  7.2 12.6 copy-start
  11.2 50.4 %all-to-all-start = ((s32[16,1,4]{2,1,0:T(1,128)}), s32[16,1,4]{2,1,0:T(1,128)S(1)}, u32[]{:S(2)}, u32[]{:S(2)}) async-start(s32[16,1,4]{2,1,0:T(1,128)} %bitcast.3), calls=%async_computation | async-start | bytes 16384 | tf_op jit(solution)/shard_map/all_to_all | solution.py:73
  61.5 67.4 %all-to-all-start.1 = ((bf16[16,4,128,256]{2,3,1,0:T(8,128)(2,1)}), bf16[16,4,128,256]{2,3,1,0:T(8,128)(2,1)}, u32[]{:S(2)}, u32[]{:S(2)}) async-start(bf16[16,4,128,256]{2,3,1,0:T(8,128)(2,1)} %broadcast_select_fusion), calls=%async_computation.1 | async-start | bytes 8388608 | tf_op jit(solution)/shard_map/all_to_all | solution.py:72
  68.3 133.1 %reduce-scatter.2.cloned.1.call-start = ((), (), s32[]{:S(2)}) async-start(), calls=%async_computation.3 | async-start | bytes 9437184 | tf_op jit(solution)/shard_map/reduce_scatter | solution.py:82
  201.4 65.3 %copy-start.2 = (f32[1024,256]{1,0:T(8,128)S(1)}, f32[1024,256]{1,0:T(8,128)}, u32[]{:S(2)}) copy-start(f32[1024,256]{1,0:T(8,128)} %reduce-scatter.2.cloned.1.call-done) | copy-start | bytes 3145732
  308.2 27.1 %collective-permute-start = (f32[256,256]{1,0:T(8,128)S(1)}, f32[256,256]{1,0:T(8,128)S(1)}, u32[]{:S(2)}, u32[]{:S(2)}) collective-permute-start(f32[256,256]{1,0:T(8,128)S(1)} %fusion.71), channel_id=1, source_target_pairs={{0,1},{1,0},{2,3},{3,2},{4,5},{5,4},{6,7},{7,6},{8,9},{9,8},{10,11... | collective-permute-start | bytes 786440 | tf_op jit(solution)/shard_map/ppermute | solution.py:13
  462.8 8.0 collective-permute-start.1
  597.4 8.6 collective-permute-start.2
  732.6 6.2 collective-permute-start.3
  865.4 6.8 collective-permute-start.4
  998.7 5.3 collective-permute-start.5
  1130.6 6.8 collective-permute-start.6
  1201.7 68.7 %copy-start.1 = (bf16[4096,256]{1,0:T(8,128)(2,1)S(1)}, bf16[4096,256]{1,0:T(8,128)(2,1)}, u32[]{:S(2)}) copy-start(bf16[4096,256]{1,0:T(8,128)(2,1)} %param.9) | copy-start | bytes 6291460
  1201.9 0.7 copy-start.3
Sparse Core Ops, SparseCore 0:
  147.6 53.8 reduce-scatter.1
where the time goes:
time: 1290 us; the launch traced here: 1280 us
  other arithmetic  881 us (68%)
  waiting for transfers between devices  135 us (10%)
  local copies, waits for them, and re-layouts  104 us (8%)
  matrix products  94.2 us (7%)
  between operations  37.3 us (3%)
  starting transfers between devices  25.1 us (2%)
    another operation x111, other arithmetic, upper_factor(): lower = jnp.linalg.cholesky(gram)  556 us
    another operation x33, other arithmetic, upper_factor(): inverse = jax.scipy.linalg.solve_triangular(lower, identity, lower=True)  316 us
    another operation x113, local copies, waits for them, and re-layouts, upper_factor(): inverse = jax.scipy.linalg.solve_triangular(lower, identity, lower=True)  63.8 us
    all_to_all x1, waiting for transfers between devices, body(): lax.all_to_all(send_values, 'row', split_axis=0, concat_axis=0, tiled=True)  59.3 us
    reduce_scatter x1, waiting for transfers between devices, body(): lax.psum_scatter(term.reshape(count, sketch_width), 'col', scatter_dimens...  53.9 us
    dot_general x68, matrix products, product(): jnp.dot(left, right, precision=lax.Precision.HIGHEST, preferred_element_t...  49.3 us
  transfers between devices with their start and end apart: 10, of which 8 were waited for; matrix products, arithmetic and copies ran while one was open for 6% of the time, Pallas kernels for 0%

commit v1 on v0

v1 whole, which is shorter than its diff:
```python
import functools

import jax
import jax.numpy as jnp
from jax import lax
from jax.experimental import pallas as pl
from jax.experimental.pallas import tpu as pltpu
from jax.sharding import PartitionSpec as P

RB_DEV = 8
CAP = 4
BS = 128
META = 16
PANEL = 32
F32 = jnp.float32
BF16 = jnp.bfloat16
HIGHEST = lax.Precision.HIGHEST
VMEM_LIMIT = 48 * 1024 * 1024


def partial_kernel(col_ref, dest_ref, row_ref, a_ref, omega_ref, out_ref, stage, meta, count, sems, meta_sem):
    step = pl.program_id(0)
    steps = pl.num_programs(0)
    group = a_ref.shape[1]
    width = omega_ref.shape[-1]

    @pl.when(step == 0)
    def _():
        meta[...] = jnp.full(meta.shape, -1.0, meta.dtype)
        for d in range(count.shape[0]):
            count[d] = 0

    dest = dest_ref[step]
    rank = count[dest]
    count[dest] = rank + 1
    here = jnp.logical_and(
        lax.broadcasted_iota(jnp.int32, (META, width), 0) == 0,
        lax.broadcasted_iota(jnp.int32, (META, width), 1) == rank,
    )
    value = jnp.full((META, width), row_ref[step], jnp.int32).astype(F32)
    meta[dest] = jnp.where(here, value, meta[dest].astype(F32)).astype(BF16)

    total = jnp.zeros((BS, width), F32)
    for g in range(0, group, 2):
        left = jnp.concatenate([a_ref[0, g], a_ref[0, g + 1]], axis=1)
        right = jnp.concatenate(
            [omega_ref[col_ref[step, g]], omega_ref[col_ref[step, g + 1]]], axis=0
        )
        total = total + jnp.dot(left, right, preferred_element_type=F32)

    slot = lax.rem(step, 2)

    def copy_out(which, d, r):
        return pltpu.make_async_copy(
            stage.at[which],
            out_ref.at[d, pl.ds(pl.multiple_of(r * BS, BS), BS), :],
            sems.at[which],
        )

    @pl.when(step >= 2)
    def _():
        copy_out(slot, 0, 0).wait()

    stage[slot] = total.astype(BF16)
    copy_out(slot, dest, rank).start()

    @pl.when(step == steps - 1)
    def _():
        last = pltpu.make_async_copy(meta, out_ref.at[:, pl.ds(CAP * BS, META), :], meta_sem)
        last.start()
        copy_out(1 - slot, 0, 0).wait()
        copy_out(slot, 0, 0).wait()
        last.wait()


def partials(a_blocks, omega, route_dest, row_target, col_target, owners):
    targets, group = col_target.shape
    width = omega.shape[1]
    slab = omega.reshape(-1, BS, width)
    return pl.pallas_call(
        partial_kernel,
        grid_spec=pltpu.PrefetchScalarGridSpec(
            num_scalar_prefetch=3,
            grid=(targets,),
            in_specs=[
                pl.BlockSpec((1, group, BS, BS), lambda t, *_: (t, 0, 0, 0)),
                pl.BlockSpec(slab.shape, lambda t, *_: (0, 0, 0)),
            ],
            out_specs=pl.BlockSpec(memory_space=pl.ANY),
            scratch_shapes=[
                pltpu.VMEM((2, BS, width), BF16),
                pltpu.VMEM((owners, META, width), BF16),
                pltpu.SMEM((owners,), jnp.int32),
                pltpu.SemaphoreType.DMA((2,)),
                pltpu.SemaphoreType.DMA,
            ],
        ),
        out_shape=jax.ShapeDtypeStruct((owners, CAP * BS + META, width), BF16),
        compiler_params=pltpu.CompilerParams(vmem_limit_bytes=VMEM_LIMIT),
        name="partials",
    )(col_target, route_dest[:, 0], row_target, a_blocks, slab)


def slot_sum_kernel(rows_ref, place_ref, got_ref, send_ref, keep_ref, acc):
    step = pl.program_id(0)
    blocks = acc.shape[0]

    @pl.when(step == 0)
    def _():
        def clear(b, carry):
            acc[b] = jnp.zeros(acc.shape[1:], F32)
            return carry

        lax.fori_loop(0, blocks, clear, 0)

    for r in range(CAP):
        row = rows_ref[step * CAP + r]

        @pl.when(row >= 0)
        def _():
            acc[row] = acc[row] + got_ref[0, r * BS : (r + 1) * BS, :].astype(F32)

    @pl.when(step == pl.num_programs(0) - 1)
    def _():
        z, core = place_ref[0], place_ref[1]

        def write(k, carry):
            d = k // RB_DEV
            chip = lax.rem(z + d, 4)
            base = chip * (2 * RB_DEV) + lax.rem(k, RB_DEV)
            send_ref[k] = acc[base + (1 - core) * RB_DEV].astype(BF16)
            keep_ref[k] = acc[base + core * RB_DEV]
            return carry

        lax.fori_loop(0, 4 * RB_DEV, write, 0)


def slot_sums(rows, place, got):
    owners, _, width = got.shape
    half = 4 * RB_DEV
    return pl.pallas_call(
        slot_sum_kernel,
        grid_spec=pltpu.PrefetchScalarGridSpec(
            num_scalar_prefetch=2,
            grid=(owners,),
            in_specs=[pl.BlockSpec((1, CAP * BS + META, width), lambda s, *_: (s, 0, 0))],
            out_specs=[
                pl.BlockSpec((half, BS, width), lambda s, *_: (0, 0, 0)),
                pl.BlockSpec((half, BS, width), lambda s, *_: (0, 0, 0)),
            ],
            scratch_shapes=[pltpu.VMEM((2 * half, BS, width), F32)],
        ),
        out_shape=[
            jax.ShapeDtypeStruct((half, BS, width), BF16),
            jax.ShapeDtypeStruct((half, BS, width), F32),
        ],
        compiler_params=pltpu.CompilerParams(vmem_limit_bytes=VMEM_LIMIT),
        name="slot_sums",
    )(rows, place, got)


def gram_kernel(place_ref, own_ref, core_ref, z1_ref, z2_ref, z3_ref, sketch_ref, send_ref, keep_ref, gram):
    z, core = place_ref[0], place_ref[1]
    sketch_ref[...] = (
        (own_ref[...] + core_ref[...].astype(F32))
        + (z1_ref[...].astype(F32) + z2_ref[...].astype(F32))
        + z3_ref[...].astype(F32)
    )
    sketch = sketch_ref[...]
    gram[...] = lax.dot_general(
        sketch, sketch, (((0,), (0,)), ((), ())), precision=HIGHEST, preferred_element_type=F32
    )
    part = send_ref.shape[0] // 4
    half = send_ref.shape[0]
    for d in range(4):
        chip = lax.rem(z + d, 4)
        send_ref[d * part : (d + 1) * part, :] = gram[
            pl.ds(pl.multiple_of((1 - core) * half + chip * part, part), part), :
        ]
        keep_ref[d * part : (d + 1) * part, :] = gram[
            pl.ds(pl.multiple_of(core * half + chip * part, part), part), :
        ]


def gram_halves(place, own, core_part, others):
    rows, width = own.shape
    whole = pl.BlockSpec(memory_space=pltpu.VMEM)
    return pl.pallas_call(
        gram_kernel,
        in_specs=[pl.BlockSpec(memory_space=pltpu.SMEM)] + [whole] * 5,
        out_specs=[whole] * 3,
        out_shape=[
            jax.ShapeDtypeStruct((rows, width), F32),
            jax.ShapeDtypeStruct((width // 2, width), F32),
            jax.ShapeDtypeStruct((width // 2, width), F32),
        ],
        scratch_shapes=[pltpu.VMEM((width, width), F32)],
        compiler_params=pltpu.CompilerParams(vmem_limit_bytes=VMEM_LIMIT),
        name="sum_gram",
    )(place, own, core_part, *others)


def factor_kernel(scale, place_ref, *refs):
    pieces, (sketch_ref, basis_ref, factor_ref, work) = refs[:8], refs[8:]
    z, core = place_ref[0], place_ref[1]
    part, n = pieces[0].shape
    for c in range(2):
        side = core if c == 0 else 1 - core
        for d in range(4):
            chip = lax.rem(z - d + 4, 4)
            work[pl.ds(pl.multiple_of((side * 4 + chip) * part, part), part), 0:n] = pieces[c * 4 + d][...]
    work[:, n : 2 * n] = (
        lax.broadcasted_iota(jnp.int32, (n, n), 0) == lax.broadcasted_iota(jnp.int32, (n, n), 1)
    ).astype(F32)
    below = lax.broadcasted_iota(jnp.int32, (PANEL, 1), 0)
    for j in range(0, n, PANEL):
        first, last = (j // BS) * BS, n + (j // BS) * BS + BS
        panel = [work[j : j + PANEL, t : t + BS] for t in range(first, last, BS)]
        lane = j - first
        for k in range(PANEL):
            column = panel[0][:, lane + k : lane + k + 1]
            inv_root = lax.rsqrt(column[k : k + 1, :])
            ratio = jnp.where(below > k, column * inv_root, 0.0)
            for i in range(len(panel)):
                row = panel[i][k : k + 1, :] * inv_root
                panel[i] = jnp.where(below == k, row, panel[i] - ratio * row)
        for i, t in enumerate(range(first, last, BS)):
            work[j : j + PANEL, t : t + BS] = panel[i]
        if j + PANEL < n:
            done = work[j : j + PANEL, first:last]
            work[j + PANEL : n, first:last] -= lax.dot_general(
                work[j : j + PANEL, j + PANEL : n],
                done,
                (((0,), (0,)), ((), ())),
                precision=HIGHEST,
                preferred_element_type=F32,
            )
    upper = lax.broadcasted_iota(jnp.int32, (n, n), 0) <= lax.broadcasted_iota(jnp.int32, (n, n), 1)
    factor_ref[...] = jnp.where(upper, work[:, 0:n], 0.0) * (1.0 / scale)
    inverse = work[:, n : 2 * n] * scale
    basis_ref[...] = lax.dot_general(
        sketch_ref[...], inverse, (((1,), (1,)), ((), ())), precision=HIGHEST, preferred_element_type=F32
    )


def factors(scale, place, pieces, sketch):
    rows, width = sketch.shape
    whole = pl.BlockSpec(memory_space=pltpu.VMEM)
    return pl.pallas_call(
        functools.partial(factor_kernel, scale),
        in_specs=[pl.BlockSpec(memory_space=pltpu.SMEM)] + [whole] * 9,
        out_specs=[whole] * 2,
        out_shape=[
            jax.ShapeDtypeStruct((rows, width), F32),
            jax.ShapeDtypeStruct((width, width), F32),
        ],
        scratch_shapes=[pltpu.VMEM((width, 2 * width), F32)],
        compiler_params=pltpu.CompilerParams(vmem_limit_bytes=VMEM_LIMIT),
        name="factor_basis",
    )(place, *pieces, sketch)


def other_core(value):
    return lax.ppermute(value, "col", [(i, i ^ 1) for i in range(8)])


def along_z(value, d):
    return lax.ppermute(value, "col", [(i, (i + 2 * d) % 8) for i in range(8)])


def along_y(value, d):
    return lax.ppermute(value, "row", [(i, (i + 4 * d) % 16) for i in range(16)])


def along_x(value, d):
    return lax.ppermute(value, "row", [(i, i // 4 * 4 + (i + d) % 4) for i in range(16)])


def summed(value, along):
    one, two, three = (along(value, d) for d in (1, 2, 3))
    return (value + two) + (one + three)


def body(scale, a_blocks, omega, route_dest, row_target, col_target):
    width = omega.shape[1]
    owners = lax.axis_size("row")
    col = lax.axis_index("col")
    place = jnp.stack([col // 2, col % 2]).astype(jnp.int32)
    send = partials(a_blocks, omega, route_dest, row_target, col_target, owners)
    got = lax.all_to_all(send, "row", split_axis=0, concat_axis=0, tiled=True)
    rows = got[:, CAP * BS, :CAP].reshape(-1).astype(jnp.int32)
    to_core, own = slot_sums(rows, place, got)
    from_core = other_core(to_core)
    per_chip = RB_DEV
    half = 4 * RB_DEV
    others = [
        along_z(
            (
                own[d * per_chip : (d + 1) * per_chip]
                + from_core[d * per_chip : (d + 1) * per_chip].astype(F32)
            ).astype(BF16),
            d,
        ).reshape(-1, width)
        for d in (1, 2, 3)
    ]
    sketch, gram_send, gram_keep = gram_halves(
        place,
        own[:per_chip].reshape(-1, width),
        from_core[:per_chip].reshape(-1, width),
        others,
    )
    gram = gram_keep + other_core(gram_send)
    part = gram.shape[0] // 4
    piece = gram[:part]
    moved = [along_z(gram[d * part : (d + 1) * part], d) for d in (1, 2, 3)]
    piece = (piece + moved[1]) + (moved[0] + moved[2])
    piece = summed(summed(piece, along_y), along_x)
    mine = [piece] + [along_z(piece, d) for d in (1, 2, 3)]
    pieces = mine + [other_core(p) for p in mine]
    return tuple(factors(scale, place, pieces, sketch))


def solution(mesh):
    rows_total = mesh.shape["row"] * mesh.shape["col"] * RB_DEV * BS
    return jax.shard_map(
        functools.partial(body, float(rows_total) ** 0.5),
        mesh=mesh,
        in_specs=(
            P(("row", "col"), None, None, None),
            P("col", None),
            P(("row", "col"), None),
            P(("row", "col")),
            P(("row", "col"), None),
        ),
        out_specs=(P(("row", "col"), None), P()),
        check_vma=False,
    )
```

time: 1290 us -> 216 us (0.17)
  other arithmetic: 881 us -> 3.68 us
  local copies, waits for them, and re-layouts: 104 us -> 3.8 us
  matrix products: 94.2 us -> 0 us
  Pallas kernels: 0 us -> 65.9 us
  between operations: 37.3 us -> 0.74 us
  waiting for transfers between devices: 135 us -> 106 us
    another operation x144 -> x1, other arithmetic: 872 us -> 0.08 us  [body(): place = jnp.stack([col // 2, col % 2]).astype(jnp.int32)]
    dot_general x70 -> x0, matrix products: 70.9 us -> none  [the longest x68 49.3 us: product(): jnp.dot(left, right, precision=lax.Precision.HIGHEST, preferred_element_t...]
    pallas_call x0 -> x4, Pallas kernels: none -> 65.9 us  [the longest x1 26.6 us: factors(): pl.pallas_call(functools.partial(factor_kernel, scale), in_specs=[pl.Bloc...]
    another operation x145 -> x0, local copies, waits for them, and re-layouts: 64.4 us -> none  [the longest x113 63.8 us: upper_factor(): inverse = jax.scipy.linalg.solve_triangular(lower, identity, lower=True)]
    reduce_scatter x1 -> x0, waiting for transfers between devices: 53.9 us -> none  [body(): lax.psum_scatter(term.reshape(count, sketch_width), 'col', scatter_dimens...]
    another operation x80 -> x0, matrix products: 23.3 us -> none  [the longest x48 14.1 us: upper_factor(): inverse = jax.scipy.linalg.solve_triangular(lower, identity, lower=True)]
    gather x3 -> x0, local copies, waits for them, and re-layouts: 20.5 us -> none  [the longest x1 16.1 us: body(): picked = slab[col_target]]
    ppermute x7 -> x21, waiting for transfers between devices: 21.8 us -> 42.1 us  [the longest x9 29.2 us: along_z(): return lax.ppermute(value, 'col', [(i, (i + 2 * d) % 8) for i in range(8)])]
  transfers between devices with their start and end apart: 10 -> 22, of which waited for: 8 -> 15; matrix products, arithmetic and copies ran while one was open for 6% -> 0% of each run, Pallas kernels for 0% -> 0%
where the time goes in v1:
time: 216 us; the launch traced here: 215 us
  waiting for transfers between devices  106 us (49%)
  Pallas kernels  65.9 us (31%)
  starting transfers between devices  34.5 us (16%)
  local copies, waits for them, and re-layouts  3.8 us (2%)
  other arithmetic  3.68 us (2%)
    all_to_all x1, waiting for transfers between devices, body(): got = lax.all_to_all(send, 'row', split_axis=0, concat_axis=0, tiled=True)  64.1 us
    ppermute x9, waiting for transfers between devices, along_z(): return lax.ppermute(value, 'col', [(i, (i + 2 * d) % 8) for i in range(8)])  29.2 us
    pallas_call x1, Pallas kernels, factors(): pl.pallas_call(functools.partial(factor_kernel, scale), in_specs=[pl.Bloc...  26.6 us
    pallas_call x1, Pallas kernels, partials(): pl.pallas_call(partial_kernel, grid_spec=pltpu.PrefetchScalarGridSpec(num...  24.9 us
    ppermute x6, starting transfers between devices, other_core(): return lax.ppermute(value, 'col', [(i, i ^ 1) for i in range(8)])  13.1 us
    pallas_call x1, Pallas kernels, slot_sums(): pl.pallas_call(slot_sum_kernel, grid_spec=pltpu.PrefetchScalarGridSpec(nu...  12.5 us
    ppermute x9, starting transfers between devices, along_z(): return lax.ppermute(value, 'col', [(i, (i + 2 * d) % 8) for i in range(8)])  8.92 us
    all_to_all x1, starting transfers between devices, body(): got = lax.all_to_all(send, 'row', split_axis=0, concat_axis=0, tiled=True)  7.65 us
  transfers between devices with their start and end apart: 22, of which 15 were waited for; matrix products, arithmetic and copies ran while one was open for 0% of the time, Pallas kernels for 0%

profile of v1, /device:TPU:1, one launch (start us, length us, event | category | flops | bytes accessed | tf_op | source)
XLA Modules:
  0.0 214.9 jit_solution(10388801196081298727)
XLA Ops:
  0.6 0.8 copy.8.col_ref
  1.4 1.6 copy-done
  3.0 0.7 copy-done.1
  3.7 0.7 copy-done.2
  4.3 24.9 %partials.1 = bf16[16,528,256]{2,1,0:T(8,128)(2,1)} custom-call(s32[32,16]{1,0:T(8,128)S(1)} %copy.8.col_ref, s32[32]{0:T(128)S(1)} %bitcast.15, s32[32]{0:T(128)S(1)} %copy-done.2, bf16[32,16,128,128]{3,2,1,0:T(8,128)(2,1)} %a_ref.1, bf16[32,128,256]{2,1,0:T(8,128)(2,1)S(1)} %bitcast.10), custom_call_target="tpu_custom_call" | custom-call | tf_op jit(solution)/shard_map/partials/pallas_call | solution.py:80
  29.2 7.7 %all-to-all-start = ((bf16[16,528,256]{2,1,0:T(8,128)(2,1)}), bf16[16,528,256]{2,1,0:T(8,128)(2,1)}, u32[]{:S(2)}, u32[]{:S(2)}) async-start(bf16[16,528,256]{2,1,0:T(8,128)(2,1)} %partials.1), calls=%async_computation | async-start | bytes 8650752 | tf_op jit(solution)/shard_map/all_to_all | solution.py:290
  36.8 0.1 pad_add_fusion.place_ref
  36.9 64.1 %all-to-all-done.got_ref = bf16[16,528,256]{2,1,0:T(8,128)(2,1)} async-done(((bf16[16,528,256]{2,1,0:T(8,128)(2,1)}), bf16[16,528,256]{2,1,0:T(8,128)(2,1)}, u32[]{:S(2)}, u32[]{:S(2)}) %all-to-all-start) | async-done | bytes 4325408 | tf_op jit(solution)/shard_map/all_to_all | solution.py:290
  101.1 0.8 fusion.1
  101.8 0.1 reshape.30.rows_ref
  101.9 12.5 %slot_sums.1 = (bf16[32,128,256]{2,1,0:T(8,128)(2,1)S(1)}, f32[32,128,256]{2,1,0:T(8,128)}) custom-call(s32[64]{0:T(128)S(1)} %reshape.30.rows_ref, s32[2]{0:T(128)S(1)} %pad_add_fusion.place_ref, bf16[16,528,256]{2,1,0:T(8,128)(2,1)} %all-to-all-done.got_ref), custom_call_target="tpu_custom_call" | custom-call | tf_op jit(solution)/shard_map/slot_sums/pallas_call | solution.py:141
  114.4 1.8 collective-permute-start
  116.2 3.8 %collective-permute-done = bf16[32,128,256]{2,1,0:T(8,128)(2,1)S(1)} collective-permute-done((bf16[32,128,256]{2,1,0:T(8,128)(2,1)S(1)}, bf16[32,128,256]{2,1,0:T(8,128)(2,1)S(1)}, u32[]{:S(2)}, u32[]{:S(2)}) %collective-permute-start) | collective-permute-done | bytes 2097184 | tf_op jit(solution)/shard_map/ppermute | solution.py:264
  120.0 2.8 %add_convert_fusion = (bf16[8,128,256]{2,1,0:T(8,128)(2,1)S(1)}, bf16[8,128,256]{2,1,0:T(8,128)(2,1)S(1)}, bf16[8,128,256]{2,1,0:T(8,128)(2,1)S(1)}, f32[8,128,256]{2,1,0:T(8,128)S(1)}) fusion(f32[32,128,256]{2,1,0:T(8,128)} %get-tuple-element.7, bf16[32,128,256]{2,1,0:T(8,128)(2,1)S(1)} %collective-permute-done), kind=kLoop, calls=%fused_computation | loop fusion | flops 2359296 | bytes 8388608 | tf_op jit(solution)/shard_map/convert_element_type | solution.py:301
  122.8 3.8 %collective-permute-start.3 = (bf16[8,128,256]{2,1,0:T(8,128)(2,1)S(1)}, bf16[8,128,256]{2,1,0:T(8,128)(2,1)S(1)}, u32[]{:S(2)}, u32[]{:S(2)}) collective-permute-start(bf16[8,128,256]{2,1,0:T(8,128)(2,1)S(1)} %get-tuple-element.12), channel_id=1, source_target_pairs={{0,6},{1,7},{2,0},{3,1},{4,2},{5,3},{6,4},{7,5},{8,14},{9,15},{10,... | collective-permute-start | bytes 1572872 | tf_op jit(solution)/shard_map/ppermute | solution.py:268
  126.6 0.0 collective-permute-start.2
  126.6 0.7 collective-permute-start.1
  127.3 21.4 %collective-permute-done.3 = bf16[8,128,256]{2,1,0:T(8,128)(2,1)S(1)} collective-permute-done((bf16[8,128,256]{2,1,0:T(8,128)(2,1)S(1)}, bf16[8,128,256]{2,1,0:T(8,128)(2,1)S(1)}, u32[]{:S(2)}, u32[]{:S(2)}) %collective-permute-start.3) | collective-permute-done | bytes 524320 | tf_op jit(solution)/shard_map/ppermute | solution.py:268
  148.8 0.0 collective-permute-done.2
  148.8 3.8 %collective-permute-done.1 = bf16[8,128,256]{2,1,0:T(8,128)(2,1)S(1)} collective-permute-done((bf16[8,128,256]{2,1,0:T(8,128)(2,1)S(1)}, bf16[8,128,256]{2,1,0:T(8,128)(2,1)S(1)}, u32[]{:S(2)}, u32[]{:S(2)}) %collective-permute-start.1) | collective-permute-done | bytes 524320 | tf_op jit(solution)/shard_map/ppermute | solution.py:268
  152.6 2.0 sum_gram.1
  154.6 0.9 collective-permute-start.4
  155.5 1.0 collective-permute-done.4
  156.5 0.7 collective-permute-start.7
  157.2 0.8 collective-permute-start.6
  158.0 0.4 collective-permute-start.5
  158.5 0.9 collective-permute-done.7
  159.3 1.8 collective-permute-done.6
  161.2 1.2 collective-permute-done.5
  162.4 1.6 collective-permute-start.10
  164.1 1.3 collective-permute-start.8
  165.3 2.7 %collective-permute-done.9 = f32[32,256]{1,0:T(8,128)S(1)} collective-permute-done((f32[32,256]{1,0:T(8,128)S(1)}, f32[32,256]{1,0:T(8,128)S(1)}, u32[]{:S(2)}, u32[]{:S(2)}) %collective-permute-start.9) | collective-permute-done | bytes 32800 | tf_op jit(solution)/shard_map/ppermute | solution.py:272
  168.0 0.3 collective-permute-done.8
  168.4 0.6 collective-permute-start.13
  169.0 0.9 collective-permute-start.12
  169.9 0.4 collective-permute-start.11
  170.3 1.2 collective-permute-done.13
  171.5 1.5 collective-permute-done.12
  173.0 1.2 collective-permute-done.11
  174.2 1.8 collective-permute-start.16
  176.0 0.7 collective-permute-start.14
  176.7 5.9 %collective-permute-start.17 = (f32[32,256]{1,0:T(8,128)S(1)}, f32[32,256]{1,0:T(8,128)S(1)}, u32[]{:S(2)}, u32[]{:S(2)}) collective-permute-start(f32[32,256]{1,0:T(8,128)S(1)} %add_add_fusion.refs_0_), channel_id=1, source_target_pairs={{0,1},{1,0},{2,3},{3,2},{4,5},{5,4},{6,7},{7,6},{8,9},{9,8},{10,11... | collective-permute-start | bytes 98312 | tf_op jit(solution)/shard_map/ppermute | solution.py:264
  182.6 0.9 collective-permute-start.20
  183.4 3.7 %collective-permute-start.19 = (f32[32,256]{1,0:T(8,128)S(1)}, f32[32,256]{1,0:T(8,128)S(1)}, u32[]{:S(2)}, u32[]{:S(2)}) collective-permute-start(f32[32,256]{1,0:T(8,128)S(1)} %collective-permute-done.15.refs_2_), channel_id=1, source_target_pairs={{0,1},{1,0},{2,3},{3,2},{4,5},{5,4},{6,7},{7,6},{8,9},{9,8},{10,11... | collective-permute-start | bytes 98312 | tf_op jit(solution)/shard_map/ppermute | solution.py:264
  187.1 0.0 collective-permute-start.18
  187.1 0.8 collective-permute-done.19.refs_6_
  188.0 0.4 collective-permute-done.18.refs_5_
  188.3 26.6 %factor_basis.1 = (f32[1024,256]{1,0:T(8,128)}, f32[256,256]{1,0:T(8,128)}) custom-call(s32[2]{0:T(128)S(1)} %pad_add_fusion.place_ref, f32[32,256]{1,0:T(8,128)S(1)} %add_add_fusion.refs_0_, f32[32,256]{1,0:T(8,128)S(1)} %collective-permute-done.14.refs_1_, f32[32,256]{1,0:T(8,128)S(1)} %collective-permute-done.15.refs_2_, ...), custom_call_target="tpu_custom_call" | custom-call | tf_op jit(solution)/shard_map/factor_basis/pallas_call | solution.py:249
  (17 shorter events, 0.1 us)
Async XLA Ops:
  1.4 1.6 copy-start
  3.0 0.7 copy-start.1
  3.6 0.7 copy-start.2
  29.2 71.9 %all-to-all-start = ((bf16[16,528,256]{2,1,0:T(8,128)(2,1)}), bf16[16,528,256]{2,1,0:T(8,128)(2,1)}, u32[]{:S(2)}, u32[]{:S(2)}) async-start(bf16[16,528,256]{2,1,0:T(8,128)(2,1)} %partials.1), calls=%async_computation | async-start | bytes 8650752 | tf_op jit(solution)/shard_map/all_to_all | solution.py:290
  114.4 5.6 %collective-permute-start = (bf16[32,128,256]{2,1,0:T(8,128)(2,1)S(1)}, bf16[32,128,256]{2,1,0:T(8,128)(2,1)S(1)}, u32[]{:S(2)}, u32[]{:S(2)}) collective-permute-start(bf16[32,128,256]{2,1,0:T(8,128)(2,1)S(1)} %get-tuple-element.8), channel_id=1, source_target_pairs={{0,1},{1,0},{2,3},{3,2},{4,5},{5,4},{6,7},{7,6},{8,9},{9,8},{10,11... | collective-permute-start | bytes 6291464 | tf_op jit(solution)/shard_map/ppermute | solution.py:264
  122.8 26.0 %collective-permute-start.3 = (bf16[8,128,256]{2,1,0:T(8,128)(2,1)S(1)}, bf16[8,128,256]{2,1,0:T(8,128)(2,1)S(1)}, u32[]{:S(2)}, u32[]{:S(2)}) collective-permute-start(bf16[8,128,256]{2,1,0:T(8,128)(2,1)S(1)} %get-tuple-element.12), channel_id=1, source_target_pairs={{0,6},{1,7},{2,0},{3,1},{4,2},{5,3},{6,4},{7,5},{8,14},{9,15},{10,... | collective-permute-start | bytes 1572872 | tf_op jit(solution)/shard_map/ppermute | solution.py:268
  126.6 22.2 %collective-permute-start.2 = (bf16[8,128,256]{2,1,0:T(8,128)(2,1)S(1)}, bf16[8,128,256]{2,1,0:T(8,128)(2,1)S(1)}, u32[]{:S(2)}, u32[]{:S(2)}) collective-permute-start(bf16[8,128,256]{2,1,0:T(8,128)(2,1)S(1)} %get-tuple-element.13), channel_id=1, source_target_pairs={{0,4},{1,5},{2,6},{3,7},{4,0},{5,1},{6,2},{7,3},{8,12},{9,13},{10,... | collective-permute-start | bytes 1572872 | tf_op jit(solution)/shard_map/ppermute | solution.py:268
  126.6 26.0 %collective-permute-start.1 = (bf16[8,128,256]{2,1,0:T(8,128)(2,1)S(1)}, bf16[8,128,256]{2,1,0:T(8,128)(2,1)S(1)}, u32[]{:S(2)}, u32[]{:S(2)}) collective-permute-start(bf16[8,128,256]{2,1,0:T(8,128)(2,1)S(1)} %get-tuple-element.14), channel_id=1, source_target_pairs={{0,2},{1,3},{2,4},{3,5},{4,6},{5,7},{6,0},{7,1},{8,10},{9,11},{10,... | collective-permute-start | bytes 1572872 | tf_op jit(solution)/shard_map/ppermute | solution.py:268
  154.6 1.9 collective-permute-start.4
  156.5 2.8 %collective-permute-start.7 = (f32[32,256]{1,0:T(8,128)S(1)}, f32[32,256]{1,0:T(8,128)S(1)}, u32[]{:S(2)}, u32[]{:S(2)}) collective-permute-start(f32[32,256]{1,0:T(8,128)S(1)} %get-tuple-element.16), channel_id=1, source_target_pairs={{0,6},{1,7},{2,0},{3,1},{4,2},{5,3},{6,4},{7,5},{8,14},{9,15},{10,... | collective-permute-start | bytes 98312 | tf_op jit(solution)/shard_map/ppermute | solution.py:268
  157.2 4.0 %collective-permute-start.6 = (f32[32,256]{1,0:T(8,128)S(1)}, f32[32,256]{1,0:T(8,128)S(1)}, u32[]{:S(2)}, u32[]{:S(2)}) collective-permute-start(f32[32,256]{1,0:T(8,128)S(1)} %get-tuple-element.17), channel_id=1, source_target_pairs={{0,2},{1,3},{2,4},{3,5},{4,6},{5,7},{6,0},{7,1},{8,10},{9,11},{10,... | collective-permute-start | bytes 98312 | tf_op jit(solution)/shard_map/ppermute | solution.py:268
  158.0 4.4 %collective-permute-start.5 = (f32[32,256]{1,0:T(8,128)S(1)}, f32[32,256]{1,0:T(8,128)S(1)}, u32[]{:S(2)}, u32[]{:S(2)}) collective-permute-start(f32[32,256]{1,0:T(8,128)S(1)} %get-tuple-element.18), channel_id=1, source_target_pairs={{0,4},{1,5},{2,6},{3,7},{4,0},{5,1},{6,2},{7,3},{8,12},{9,13},{10,... | collective-permute-start | bytes 98312 | tf_op jit(solution)/shard_map/ppermute | solution.py:268
  162.4 2.9 %collective-permute-start.10 = (f32[32,256]{1,0:T(8,128)S(1)}, f32[32,256]{1,0:T(8,128)S(1)}, u32[]{:S(2)}, u32[]{:S(2)}) collective-permute-start(f32[32,256]{1,0:T(8,128)S(1)} %fusion), channel_id=1, source_target_pairs={{0,96},{8,104},{16,112},{24,120},{32,0},{40,8},{48,16},{56,24},{64... | collective-permute-start | bytes 98312 | tf_op jit(solution)/shard_map/ppermute | solution.py:272
  164.1 4.0 %collective-permute-start.9 = (f32[32,256]{1,0:T(8,128)S(1)}, f32[32,256]{1,0:T(8,128)S(1)}, u32[]{:S(2)}, u32[]{:S(2)}) collective-permute-start(f32[32,256]{1,0:T(8,128)S(1)} %fusion), channel_id=1, source_target_pairs={{0,32},{8,40},{16,48},{24,56},{32,64},{40,72},{48,80},{56,88},{64,... | collective-permute-start | bytes 98312 | tf_op jit(solution)/shard_map/ppermute | solution.py:272
  164.1 4.3 %collective-permute-start.8 = (f32[32,256]{1,0:T(8,128)S(1)}, f32[32,256]{1,0:T(8,128)S(1)}, u32[]{:S(2)}, u32[]{:S(2)}) collective-permute-start(f32[32,256]{1,0:T(8,128)S(1)} %fusion), channel_id=1, source_target_pairs={{0,64},{8,72},{16,80},{24,88},{32,96},{40,104},{48,112},{56,120},{... | collective-permute-start | bytes 98312 | tf_op jit(solution)/shard_map/ppermute | solution.py:272
  168.4 3.1 %collective-permute-start.13 = (f32[32,256]{1,0:T(8,128)S(1)}, f32[32,256]{1,0:T(8,128)S(1)}, u32[]{:S(2)}, u32[]{:S(2)}) collective-permute-start(f32[32,256]{1,0:T(8,128)S(1)} %add_add_fusion.1), channel_id=1, source_target_pairs={{0,24},{8,0},{16,8},{24,16},{32,56},{40,32},{48,40},{56,48},{64,88... | collective-permute-start | bytes 98312 | tf_op jit(solution)/shard_map/ppermute | solution.py:276
  169.0 4.0 %collective-permute-start.12 = (f32[32,256]{1,0:T(8,128)S(1)}, f32[32,256]{1,0:T(8,128)S(1)}, u32[]{:S(2)}, u32[]{:S(2)}) collective-permute-start(f32[32,256]{1,0:T(8,128)S(1)} %add_add_fusion.1), channel_id=1, source_target_pairs={{0,8},{8,16},{16,24},{24,0},{32,40},{40,48},{48,56},{56,32},{64,72... | collective-permute-start | bytes 98312 | tf_op jit(solution)/shard_map/ppermute | solution.py:276
  169.9 4.3 %collective-permute-start.11 = (f32[32,256]{1,0:T(8,128)S(1)}, f32[32,256]{1,0:T(8,128)S(1)}, u32[]{:S(2)}, u32[]{:S(2)}) collective-permute-start(f32[32,256]{1,0:T(8,128)S(1)} %add_add_fusion.1), channel_id=1, source_target_pairs={{0,16},{8,24},{16,0},{24,8},{32,48},{40,56},{48,32},{56,40},{64,80... | collective-permute-start | bytes 98312 | tf_op jit(solution)/shard_map/ppermute | solution.py:276
  174.2 8.4 %collective-permute-start.16 = (f32[32,256]{1,0:T(8,128)S(1)}, f32[32,256]{1,0:T(8,128)S(1)}, u32[]{:S(2)}, u32[]{:S(2)}) collective-permute-start(f32[32,256]{1,0:T(8,128)S(1)} %add_add_fusion.refs_0_), channel_id=1, source_target_pairs={{0,6},{1,7},{2,0},{3,1},{4,2},{5,3},{6,4},{7,5},{8,14},{9,15},{10,... | collective-permute-start | bytes 98312 | tf_op jit(solution)/shard_map/ppermute | solution.py:268
  176.0 7.4 %collective-permute-start.15 = (f32[32,256]{1,0:T(8,128)S(1)}, f32[32,256]{1,0:T(8,128)S(1)}, u32[]{:S(2)}, u32[]{:S(2)}) collective-permute-start(f32[32,256]{1,0:T(8,128)S(1)} %add_add_fusion.refs_0_), channel_id=1, source_target_pairs={{0,4},{1,5},{2,6},{3,7},{4,0},{5,1},{6,2},{7,3},{8,12},{9,13},{10,... | collective-permute-start | bytes 98312 | tf_op jit(solution)/shard_map/ppermute | solution.py:268
  176.0 11.1 %collective-permute-start.14 = (f32[32,256]{1,0:T(8,128)S(1)}, f32[32,256]{1,0:T(8,128)S(1)}, u32[]{:S(2)}, u32[]{:S(2)}) collective-permute-start(f32[32,256]{1,0:T(8,128)S(1)} %add_add_fusion.refs_0_), channel_id=1, source_target_pairs={{0,2},{1,3},{2,4},{3,5},{4,6},{5,7},{6,0},{7,1},{8,10},{9,11},{10,... | collective-permute-start | bytes 98312 | tf_op jit(solution)/shard_map/ppermute | solution.py:268
  176.7 10.4 %collective-permute-start.17 = (f32[32,256]{1,0:T(8,128)S(1)}, f32[32,256]{1,0:T(8,128)S(1)}, u32[]{:S(2)}, u32[]{:S(2)}) collective-permute-start(f32[32,256]{1,0:T(8,128)S(1)} %add_add_fusion.refs_0_), channel_id=1, source_target_pairs={{0,1},{1,0},{2,3},{3,2},{4,5},{5,4},{6,7},{7,6},{8,9},{9,8},{10,11... | collective-permute-start | bytes 98312 | tf_op jit(solution)/shard_map/ppermute | solution.py:264
  182.6 4.5 %collective-permute-start.20 = (f32[32,256]{1,0:T(8,128)S(1)}, f32[32,256]{1,0:T(8,128)S(1)}, u32[]{:S(2)}, u32[]{:S(2)}) collective-permute-start(f32[32,256]{1,0:T(8,128)S(1)} %collective-permute-done.16.refs_3_), channel_id=1, source_target_pairs={{0,1},{1,0},{2,3},{3,2},{4,5},{5,4},{6,7},{7,6},{8,9},{9,8},{10,11... | collective-permute-start | bytes 98312 | tf_op jit(solution)/shard_map/ppermute | solution.py:264
  183.4 4.5 %collective-permute-start.19 = (f32[32,256]{1,0:T(8,128)S(1)}, f32[32,256]{1,0:T(8,128)S(1)}, u32[]{:S(2)}, u32[]{:S(2)}) collective-permute-start(f32[32,256]{1,0:T(8,128)S(1)} %collective-permute-done.15.refs_2_), channel_id=1, source_target_pairs={{0,1},{1,0},{2,3},{3,2},{4,5},{5,4},{6,7},{7,6},{8,9},{9,8},{10,11... | collective-permute-start | bytes 98312 | tf_op jit(solution)/shard_map/ppermute | solution.py:264
  187.1 1.2 collective-permute-start.18

commit v2 on v0

v2 whole, which is shorter than its diff:
```python
import functools

import jax
import jax.numpy as jnp
from jax import lax
from jax.experimental import pallas as pl
from jax.experimental.pallas import tpu as pltpu
from jax.sharding import PartitionSpec as P

RB_DEV = 8
CAP = 4
BS = 128
META = 16
SLOT_ROWS = CAP * BS + META
CHUNKS = 2
PANEL = 32
UNROLL = 4
AHEAD = 3
SIDE = 4
OWNERS = SIDE * SIDE
HALF = SIDE * RB_DEV
F32 = jnp.float32
BF16 = jnp.bfloat16
HIGHEST = lax.Precision.HIGHEST
MIB = 1024 * 1024
WHOLE = pl.BlockSpec(memory_space=pltpu.VMEM)
SCALARS = pl.BlockSpec(memory_space=pltpu.SMEM)
IN_HBM = pl.BlockSpec(memory_space=pltpu.HBM)


def one_of(index, low, high, act):
    if high - low == 1:
        act(low)
        return
    middle = (low + high) // 2
    lax.cond(
        index < middle,
        lambda: one_of(index, low, middle, act),
        lambda: one_of(index, middle, high, act),
    )


def partial_kernel(index_ref, place_ref, a_ref, omega_ref, *refs):
    outs, scratch = refs[: CHUNKS * SIDE], refs[CHUNKS * SIDE :]
    blocks, slab, stage, meta, rows, count, a_sems, slab_sem, out_sems, meta_sems = scratch
    targets, group = blocks.shape[:2]
    width = slab.shape[-1] // CHUNKS
    core, y, x = place_ref[1], place_ref[2], place_ref[3]
    slab_copy = pltpu.make_async_copy(omega_ref, slab, slab_sem)
    slab_copy.start()

    def load(step):
        some = pl.ds(step * UNROLL, UNROLL)
        return pltpu.make_async_copy(a_ref.at[some], blocks.at[some], a_sems.at[step])

    for step in range(AHEAD):
        load(step).start()

    def clear(o, carry):
        count[o] = 0
        for r in range(CAP):
            rows[o, r] = -1
        return carry

    lax.fori_loop(0, OWNERS, clear, 0)
    slab_copy.wait()

    def copy_out(t, first, second, rank, c):
        return pltpu.make_async_copy(
            stage.at[t, :, pl.ds(c * width, width)],
            outs[c * SIDE + first].at[second, pl.ds(pl.multiple_of(rank * BS, BS), BS), :],
            out_sems.at[c, t],
        )

    def several(step, carry):
        @pl.when(step + AHEAD < targets // UNROLL)
        def _():
            load(step + AHEAD).start()

        load(step).wait()
        for i in range(UNROLL):
            t = step * UNROLL + i
            left = jnp.concatenate([blocks[t, g] for g in range(group)], axis=1)
            right = jnp.concatenate([slab[index_ref[g, t]] for g in range(group)], axis=0)
            stage[t] = jnp.dot(left, right, preferred_element_type=F32).astype(BF16)
        for i in range(UNROLL):
            t = step * UNROLL + i
            dest = index_ref[group, t]
            dy, dx = (dest // SIDE - y) & (SIDE - 1), (dest - x) & (SIDE - 1)
            first, second = jnp.where(core == 0, dy, dx), jnp.where(core == 0, dx, dy)
            owner = first * SIDE + second
            rank = count[owner]
            count[owner] = rank + 1
            rows[owner, rank] = index_ref[group + 1, t]

            def send(d, t=t, second=second, rank=rank):
                for c in range(CHUNKS):
                    copy_out(t, d, second, rank, c).start()

            one_of(first, 0, SIDE, send)
        return carry

    lax.fori_loop(0, targets // UNROLL, several, 0)
    lane = lax.broadcasted_iota(jnp.int32, (META, width), 1)
    for o in range(OWNERS):
        values = jnp.full((META, width), -1, jnp.int32)
        for r in range(CAP):
            values = jnp.where(lane == r, rows[o, r], values)
        meta[o] = values.astype(F32).astype(BF16)
    tails = [
        pltpu.make_async_copy(
            meta.at[pl.ds(d * SIDE, SIDE)],
            outs[c * SIDE + d].at[:, pl.ds(CAP * BS, META), :],
            meta_sems.at[c, d],
        )
        for c in range(CHUNKS)
        for d in range(SIDE)
    ]
    for tail in tails:
        tail.start()

    def finish(t, carry):
        for c in range(CHUNKS):
            copy_out(t, 0, 0, 0, c).wait()
        return carry

    lax.fori_loop(0, targets, finish, 0)
    for tail in tails:
        tail.wait()


def partials(a_blocks, omega, route_dest, row_target, col_target, place):
    targets = col_target.shape[0]
    width = omega.shape[1]
    slab = omega.reshape(-1, BS, width)
    indices = jnp.concatenate([col_target.T, route_dest.T, row_target[None, :]])
    out = jax.ShapeDtypeStruct((SIDE, SLOT_ROWS, width // CHUNKS), BF16)
    outs = pl.pallas_call(
        partial_kernel,
        in_specs=[SCALARS] * 2 + [IN_HBM] * 2,
        out_specs=[pl.BlockSpec(memory_space=pl.ANY)] * (CHUNKS * SIDE),
        out_shape=[out] * (CHUNKS * SIDE),
        scratch_shapes=[
            pltpu.VMEM(a_blocks.shape, BF16),
            pltpu.VMEM(slab.shape, BF16),
            pltpu.VMEM((targets, BS, width), BF16),
            pltpu.VMEM((OWNERS, META, width // CHUNKS), BF16),
            pltpu.SMEM((OWNERS, CAP), jnp.int32),
            pltpu.SMEM((OWNERS,), jnp.int32),
            pltpu.SemaphoreType.DMA((targets // UNROLL,)),
            pltpu.SemaphoreType.DMA,
            pltpu.SemaphoreType.DMA((CHUNKS, targets)),
            pltpu.SemaphoreType.DMA((CHUNKS, SIDE)),
        ],
        compiler_params=pltpu.CompilerParams(vmem_limit_bytes=48 * MIB),
        name="partials",
    )(indices, place, a_blocks, slab)
    return [outs[c * SIDE : (c + 1) * SIDE] for c in range(CHUNKS)]


def slot_sum_kernel(place_ref, *refs):
    got, (send_ref, acc, ints, rows, sem) = refs[: 2 * SIDE - 1], refs[2 * SIDE - 1 :]
    z, core = place_ref[0], place_ref[1]
    pieces = [(ref, 0) for ref in got[:SIDE]] + [(ref, i) for ref in got[SIDE:] for i in range(SIDE)]
    for s, (ref, i) in enumerate(pieces):
        tile = ref[i, CAP * BS : SLOT_ROWS, 0:BS].astype(F32)
        row = tile[0:1, :].astype(jnp.int32)
        side = (row // RB_DEV) & 1
        chip = (row // (2 * RB_DEV) - z) & (SIDE - 1)
        place = jnp.where(side == core, 0, HALF) + chip * RB_DEV + (row & (RB_DEV - 1))
        ints[s : s + 1, :] = jnp.where(row < 0, row, place)
    copy = pltpu.make_async_copy(ints, rows, sem)
    copy.start()

    def clear(b, carry):
        acc[b] = jnp.zeros(acc.shape[1:], F32)
        return carry

    lax.fori_loop(0, 2 * HALF, clear, 0, unroll=2)
    copy.wait()
    for s, (ref, i) in enumerate(pieces):
        for r in range(CAP):
            place = rows[s, r]

            @pl.when(place >= 0)
            def _():
                acc[place] = acc[place] + ref[i, r * BS : (r + 1) * BS, :].astype(F32)

    def write(k, carry):
        send_ref[k] = acc[HALF + k].astype(BF16)
        return carry

    lax.fori_loop(0, HALF, write, 0, unroll=2)


def slot_sums(place, got):
    width = got[0].shape[2]
    return pl.pallas_call(
        slot_sum_kernel,
        in_specs=[SCALARS] + [WHOLE] * len(got),
        out_specs=[WHOLE] * 2,
        out_shape=[
            jax.ShapeDtypeStruct((HALF, BS, width), BF16),
            jax.ShapeDtypeStruct((2 * HALF, BS, width), F32),
        ],
        scratch_shapes=[
            pltpu.VMEM((OWNERS, BS), jnp.int32),
            pltpu.SMEM((OWNERS, BS), jnp.int32),
            pltpu.SemaphoreType.DMA,
        ],
        compiler_params=pltpu.CompilerParams(vmem_limit_bytes=22 * MIB),
        name="slot_sums",
    )(place, *got)


def gram_kernel(place_ref, *refs):
    parts, (sketch_ref, send_ref, keep_ref, gram) = refs[: 5 * CHUNKS], refs[5 * CHUNKS :]
    core = place_ref[1]
    width = parts[0].shape[1]
    for c in range(CHUNKS):
        own, from_core, one, two, three = (ref[...].astype(F32) for ref in parts[5 * c : 5 * c + 5])
        sketch_ref[:, c * width : (c + 1) * width] = (own + from_core) + (one + three) + two
    sketch = sketch_ref[...]
    gram[...] = lax.dot_general(
        sketch, sketch, (((0,), (0,)), ((), ())), precision=HIGHEST, preferred_element_type=F32
    )
    half = send_ref.shape[0]
    send_ref[...] = gram[pl.ds(pl.multiple_of((1 - core) * half, half), half), :]
    keep_ref[...] = gram[pl.ds(pl.multiple_of(core * half, half), half), :]


def gram_halves(place, parts):
    rows = RB_DEV * BS
    width = CHUNKS * parts[0].shape[1]
    return pl.pallas_call(
        gram_kernel,
        in_specs=[SCALARS] + [WHOLE] * (5 * CHUNKS),
        out_specs=[WHOLE] * 3,
        out_shape=[
            jax.ShapeDtypeStruct((rows, width), F32),
            jax.ShapeDtypeStruct((width // 2, width), F32),
            jax.ShapeDtypeStruct((width // 2, width), F32),
        ],
        scratch_shapes=[pltpu.VMEM((width, width), F32)],
        compiler_params=pltpu.CompilerParams(vmem_limit_bytes=20 * MIB),
        name="sum_gram",
    )(place, *parts)


def small_factor(block):
    n = len(block)
    low = [list(row) for row in block]
    inv = [None] * n
    for k in range(n):
        inv[k] = lax.rsqrt(low[k][k])
        for i in range(k + 1, n):
            low[i][k] = low[i][k] * inv[k]
        for j in range(k + 1, n):
            for i in range(j, n):
                low[i][j] = low[i][j] - low[i][k] * low[j][k]
    out = [[None] * n for _ in range(n)]
    for j in range(n):
        out[j][j] = inv[j]
        for i in range(j + 1, n):
            s = low[i][j] * out[j][j]
            for m in range(j + 1, i):
                s = s + low[i][m] * out[m][j]
            out[i][j] = -(s * inv[i])
    return out


def wide(value):
    return jnp.broadcast_to(value, (8, BS))


def factor_panel(panel, lane):
    sub = lax.broadcasted_iota(jnp.int32, (8, BS), 0)
    for g in range(len(panel)):
        at = lane + 8 * g
        cols = [wide(panel[g][0][:, at + c : at + c + 1]) for c in range(8)]
        inverse = small_factor([[wide(cols[c][r : r + 1, :]) for c in range(r + 1)] for r in range(8)])
        spread = []
        for k in range(8):
            value = inverse[7][k]
            for r in range(6, k - 1, -1):
                value = jnp.where(sub == r, inverse[r][k], value)
            spread.append(jnp.where(sub >= k, value, 0.0))
        done = []
        for tile in panel[g]:
            total = spread[0] * wide(tile[0:1, :])
            for k in range(1, 8):
                total = total + spread[k] * wide(tile[k : k + 1, :])
            done.append(total)
        panel[g] = done
        done_rows = [[wide(tile[k : k + 1, :]) for k in range(8)] for tile in done]
        for h in range(g + 1, len(panel)):
            cols = [wide(panel[h][0][:, at + c : at + c + 1]) for c in range(8)]
            for k in range(8):
                ratio = cols[0] * inverse[k][0]
                for m in range(1, k + 1):
                    ratio = ratio + cols[m] * inverse[k][m]
                for t in range(len(done)):
                    panel[h][t] = panel[h][t] - ratio * done_rows[t][k]


def factor_kernel(scale, place_ref, mine_ref, other_ref, sketch_ref, basis_ref, factor_ref, work):
    core = place_ref[1]
    n = mine_ref.shape[1]
    half = n // 2
    work[pl.ds(pl.multiple_of(core * half, half), half), 0:n] = mine_ref[...]
    work[pl.ds(pl.multiple_of((1 - core) * half, half), half), 0:n] = other_ref[...]
    down = lax.broadcasted_iota(jnp.int32, (n, n), 0)
    across = lax.broadcasted_iota(jnp.int32, (n, n), 1)
    work[:, n : 2 * n] = (down == across).astype(F32)
    for j in range(0, n, PANEL):
        first, last = (j // BS) * BS, n + (j // BS) * BS + BS
        tiles = range(first, last, BS)
        panel = [[work[i : i + 8, t : t + BS] for t in tiles] for i in range(j, j + PANEL, 8)]
        factor_panel(panel, j - first)
        for g, group in enumerate(panel):
            for t, tile in zip(tiles, group):
                work[j + 8 * g : j + 8 * g + 8, t : t + BS] = tile
        if j + PANEL < n:
            work[j + PANEL : n, first:last] -= lax.dot_general(
                work[j : j + PANEL, j + PANEL : n],
                work[j : j + PANEL, first:last],
                (((0,), (0,)), ((), ())),
                precision=HIGHEST,
                preferred_element_type=F32,
            )
    factor_ref[...] = jnp.where(down <= across, work[:, 0:n], 0.0) * (1.0 / scale)
    inverse = work[:, n : 2 * n] * scale
    basis_ref[...] = lax.dot_general(
        sketch_ref[...], inverse, (((1,), (1,)), ((), ())), precision=HIGHEST, preferred_element_type=F32
    )


def factors(scale, place, mine, other, sketch):
    rows, width = sketch.shape
    return pl.pallas_call(
        functools.partial(factor_kernel, scale),
        in_specs=[SCALARS] + [WHOLE] * 3,
        out_specs=[WHOLE] * 2,
        out_shape=[
            jax.ShapeDtypeStruct((rows, width), F32),
            jax.ShapeDtypeStruct((width, width), F32),
        ],
        scratch_shapes=[pltpu.VMEM((width, 2 * width), F32)],
        compiler_params=pltpu.CompilerParams(vmem_limit_bytes=16 * MIB),
        name="factor_basis",
    )(place, mine, other, sketch)


def other_core(value):
    return lax.ppermute(value, "col", [(i, i ^ 1) for i in range(2 * SIDE)])


def moved(value, target):
    pairs = []
    for y in range(SIDE):
        for x in range(SIDE):
            for z in range(SIDE):
                for core in range(2):
                    to_y, to_x, to_z = target(core, (y, x, z))
                    source = ((y * SIDE + x) * SIDE + z) * 2 + core
                    pairs.append((source, ((to_y * SIDE + to_x) * SIDE + to_z) * 2 + core))
    return lax.ppermute(value, ("row", "col"), pairs)


def along(value, axes, step):
    def target(core, chip):
        return tuple(step(at) if axis == axes[core] else at for axis, at in enumerate(chip))

    return moved(value, target)


def ahead(value, axes, d):
    return along(value, axes, lambda at: (at + d) % SIDE)


def summed(value):
    for axes in ((2, 0), (0, 1), (1, 2)):
        one, three, two = (ahead(value, axes, d) for d in (1, 3, 2))
        value = (value + two) + (one + three)
    return value


def body(scale, a_blocks, omega, route_dest, row_target, col_target):
    row, col = lax.axis_index("row"), lax.axis_index("col")
    place = jnp.stack([col // 2, col % 2, row // SIDE, row % SIDE]).astype(jnp.int32)
    sends = partials(a_blocks, omega, route_dest, row_target, col_target, place)
    parts = []
    for c, send in enumerate(sends):
        near = [send[0]] + [ahead(send[d], (0, 1), d) for d in (1, 3, 2)]
        across = [jnp.stack([part[d] for part in near]) for d in (1, 3, 2)]
        far = [ahead(value, (1, 0), d) for d, value in zip((1, 3, 2), across)]
        kept, leaving = core_sums(place, near + far)
        parts = parts + kept + sent_along_z(leaving)
    sketch, gram_send, gram_keep = gram_halves(place, parts)
    gram = summed(gram_keep + other_core(gram_send))
    return tuple(factors(scale, place, gram, other_core(gram), sketch))


def core_sums(place, got):
    to_core, own = slot_sums(place, got)
    width = own.shape[-1]
    own, from_core = own.reshape(2 * SIDE, -1, width), other_core(to_core).reshape(SIDE, -1, width)
    leaving = [(own[d] + from_core[d].astype(F32)).astype(BF16) for d in (1, 3, 2)]
    return [own[0], from_core[0]], leaving


def sent_along_z(leaving):
    return [ahead(value, (2, 2), d) for d, value in zip((1, 3, 2), leaving)]


def solution(mesh):
    rows_total = mesh.shape["row"] * mesh.shape["col"] * RB_DEV * BS
    return jax.shard_map(
        functools.partial(body, float(rows_total) ** 0.5),
        mesh=mesh,
        in_specs=(
            P(("row", "col"), None, None, None),
            P("col", None),
            P(("row", "col"), None),
            P(("row", "col")),
            P(("row", "col"), None),
        ),
        out_specs=(P(("row", "col"), None), P()),
        check_vma=False,
    )
```

time: 1290 us -> 145 us (0.11)
  other arithmetic: 881 us -> 1.86 us
  local copies, waits for them, and re-layouts: 104 us -> 0.26 us
  matrix products: 94.2 us -> 0 us
  waiting for transfers between devices: 135 us -> 53.1 us
  between operations: 37.3 us -> 0.89 us
  starting transfers between devices: 25.1 us -> 57.9 us
  Pallas kernels: 0 us -> 31.1 us
    another operation x144 -> x7, other arithmetic: 872 us -> 0.5 us  [the longest x6 0.42 us: body(): across = [jnp.stack([part[d] for part in near]) for d in (1, 3, 2)]]
    dot_general x70 -> x0, matrix products: 70.9 us -> none  [the longest x68 49.3 us: product(): jnp.dot(left, right, precision=lax.Precision.HIGHEST, preferred_element_t...]
    another operation x145 -> x0, local copies, waits for them, and re-layouts: 64.4 us -> none  [the longest x113 63.8 us: upper_factor(): inverse = jax.scipy.linalg.solve_triangular(lower, identity, lower=True)]
    all_to_all x2 -> x0, waiting for transfers between devices: 59.3 us -> none  [the longest x1 59.3 us: body(): lax.all_to_all(send_values, 'row', split_axis=0, concat_axis=0, tiled=True)]
    reduce_scatter x1 -> x0, waiting for transfers between devices: 53.9 us -> none  [body(): lax.psum_scatter(term.reshape(count, sketch_width), 'col', scatter_dimens...]
    ppermute x7 -> x31, starting transfers between devices: 10.7 us -> 57.9 us  [the longest x27 45.6 us: moved(): return lax.ppermute(value, ('row', 'col'), pairs)]
    ppermute x7 -> x31, waiting for transfers between devices: 21.8 us -> 53.1 us  [the longest x27 51.1 us: moved(): return lax.ppermute(value, ('row', 'col'), pairs)]
    pallas_call x0 -> x5, Pallas kernels: none -> 31.1 us  [the longest x1 13 us: factors(): pl.pallas_call(functools.partial(factor_kernel, scale), in_specs=[SCALARS...]
  transfers between devices with their start and end apart: 10 -> 31, of which waited for: 8 -> 18; matrix products, arithmetic and copies ran while one was open for 6% -> 1% of each run, Pallas kernels for 0% -> 3%
where the time goes in v2:
time: 145 us
  starting transfers between devices  57.9 us (40%)
  waiting for transfers between devices  53.1 us (37%)
  Pallas kernels  31.1 us (21%)
  other arithmetic  1.86 us (1%)
    ppermute x27, waiting for transfers between devices, moved(): return lax.ppermute(value, ('row', 'col'), pairs)  51.1 us
    ppermute x27, starting transfers between devices, moved(): return lax.ppermute(value, ('row', 'col'), pairs)  45.6 us
    pallas_call x1, Pallas kernels, factors(): pl.pallas_call(functools.partial(factor_kernel, scale), in_specs=[SCALARS...  13 us
    ppermute x4, starting transfers between devices, other_core(): return lax.ppermute(value, 'col', [(i, i ^ 1) for i in range(2 * SIDE)])  12.4 us
    pallas_call x1, Pallas kernels, partials(): pl.pallas_call(partial_kernel, in_specs=[SCALARS] * 2 + [IN_HBM] * 2, out...  11.8 us
    pallas_call x2, Pallas kernels, slot_sums(): pl.pallas_call(slot_sum_kernel, in_specs=[SCALARS] + [WHOLE] * len(got),...  4.36 us
  transfers between devices with their start and end apart: 31, of which 18 were waited for; matrix products, arithmetic and copies ran while one was open for 1% of the time, Pallas kernels for 3%

profile of v2, /device:TPU:1, one launch (start us, length us, event | category | flops | bytes accessed | tf_op | source)
XLA Modules:
  0.0 145.1 jit_solution(4940214493292956114)
XLA Ops:
  1.5 11.8 %partials.1 = (bf16[4,528,128]{2,1,0:T(8,128)(2,1)S(1)}, bf16[4,528,128]{2,1,0:T(8,128)(2,1)S(1)}, bf16[4,528,128]{2,1,0:T(8,128)(2,1)S(1)}, bf16[4,528,128]{2,1...) custom-call(s32[18,32]{1,0:T(8,128)S(1)} %pad_add_fusion.index_ref, ...), custom_call_target="tpu_custom_call" | custom-call | tf_op jit(solution)/shard_map/partials/pallas_call | solution.py:138
  13.3 2.1 %collective-permute-start.10 = (bf16[4,528,128]{2,1,0:T(8,128)(2,1)S(1)}, bf16[4,528,128]{2,1,0:T(8,128)(2,1)S(1)}, u32[]{:S(2)}, u32[]{:S(2)}) collective-permute-start(bf16[4,528,128]{2,1,0:T(8,128)(2,1)S(1)} %get-tuple-element.24), channel_id=1, source_target_pairs={{0,32},{1,9},{2,34},{3,11},{4,36},{5,13},{6,38},{7,15},{8,40},{9,1... | collective-permute-start | bytes 1622024 | tf_op jit(solution)/shard_map/ppermute | solution.py:367
  15.4 1.4 collective-permute-start.11
  16.7 1.6 %collective-permute-start.12 = (bf16[4,528,128]{2,1,0:T(8,128)(2,1)S(1)}, bf16[4,528,128]{2,1,0:T(8,128)(2,1)S(1)}, u32[]{:S(2)}, u32[]{:S(2)}) collective-permute-start(bf16[4,528,128]{2,1,0:T(8,128)(2,1)S(1)} %get-tuple-element.26), channel_id=1, source_target_pairs={{0,64},{1,17},{2,66},{3,19},{4,68},{5,21},{6,70},{7,23},{8,72},{9,... | collective-permute-start | bytes 1622024 | tf_op jit(solution)/shard_map/ppermute | solution.py:367
  18.7 2.4 %collective-permute-start.1 = (bf16[4,528,128]{2,1,0:T(8,128)(2,1)S(1)}, bf16[4,528,128]{2,1,0:T(8,128)(2,1)S(1)}, u32[]{:S(2)}, u32[]{:S(2)}) collective-permute-start(bf16[4,528,128]{2,1,0:T(8,128)(2,1)S(1)} %get-tuple-element.19), channel_id=1, source_target_pairs={{0,96},{1,25},{2,98},{3,27},{4,100},{5,29},{6,102},{7,31},{8,104},... | collective-permute-start | bytes 1622024 | tf_op jit(solution)/shard_map/ppermute | solution.py:367
  21.1 2.6 %collective-permute-done.10.refs_1_ = bf16[4,528,128]{2,1,0:T(8,128)(2,1)S(1)} collective-permute-done((bf16[4,528,128]{2,1,0:T(8,128)(2,1)S(1)}, bf16[4,528,128]{2,1,0:T(8,128)(2,1)S(1)}, u32[]{:S(2)}, u32[]{:S(2)}) %collective-permute-start.10) | collective-permute-done | bytes 540704 | tf_op jit(solution)/shard_map/ppermute | solution.py:367
  23.7 1.7 %collective-permute-start.2 = (bf16[4,528,128]{2,1,0:T(8,128)(2,1)S(1)}, bf16[4,528,128]{2,1,0:T(8,128)(2,1)S(1)}, u32[]{:S(2)}, u32[]{:S(2)}) collective-permute-start(bf16[4,528,128]{2,1,0:T(8,128)(2,1)S(1)} %get-tuple-element.20), channel_id=1, source_target_pairs={{0,64},{1,17},{2,66},{3,19},{4,68},{5,21},{6,70},{7,23},{8,72},{9,... | collective-permute-start | bytes 1622024 | tf_op jit(solution)/shard_map/ppermute | solution.py:367
  25.5 5.2 %collective-permute-done.12.refs_3_ = bf16[4,528,128]{2,1,0:T(8,128)(2,1)S(1)} collective-permute-done((bf16[4,528,128]{2,1,0:T(8,128)(2,1)S(1)}, bf16[4,528,128]{2,1,0:T(8,128)(2,1)S(1)}, u32[]{:S(2)}, u32[]{:S(2)}) %collective-permute-start.12) | collective-permute-done | bytes 540704 | tf_op jit(solution)/shard_map/ppermute | solution.py:367
  30.8 1.1 collective-permute-start.13
  32.0 1.8 %collective-permute-start.14 = (bf16[4,528,128]{2,1,0:T(8,128)(2,1)S(1)}, bf16[4,528,128]{2,1,0:T(8,128)(2,1)S(1)}, u32[]{:S(2)}, u32[]{:S(2)}) collective-permute-start(bf16[4,528,128]{2,1,0:T(8,128)(2,1)S(1)} %pad_maximum_fusion.4), channel_id=1, source_target_pairs={{0,24},{1,97},{2,26},{3,99},{4,28},{5,101},{6,30},{7,103},{8,0},{9... | collective-permute-start | bytes 1622024 | tf_op jit(solution)/shard_map/ppermute | solution.py:367
  33.8 1.4 collective-permute-done.refs_1_
  35.3 3.9 %collective-permute-start.15 = (bf16[4,528,128]{2,1,0:T(8,128)(2,1)S(1)}, bf16[4,528,128]{2,1,0:T(8,128)(2,1)S(1)}, u32[]{:S(2)}, u32[]{:S(2)}) collective-permute-start(bf16[4,528,128]{2,1,0:T(8,128)(2,1)S(1)} %pad_maximum_fusion.5), channel_id=1, source_target_pairs={{0,16},{1,65},{2,18},{3,67},{4,20},{5,69},{6,22},{7,71},{8,24},{9,... | collective-permute-start | bytes 1622024 | tf_op jit(solution)/shard_map/ppermute | solution.py:367
  39.2 7.2 %collective-permute-done.2.refs_3_ = bf16[4,528,128]{2,1,0:T(8,128)(2,1)S(1)} collective-permute-done((bf16[4,528,128]{2,1,0:T(8,128)(2,1)S(1)}, bf16[4,528,128]{2,1,0:T(8,128)(2,1)S(1)}, u32[]{:S(2)}, u32[]{:S(2)}) %collective-permute-start.2) | collective-permute-done | bytes 540704 | tf_op jit(solution)/shard_map/ppermute | solution.py:367
  46.5 5.5 %collective-permute-start.5 = (bf16[4,528,128]{2,1,0:T(8,128)(2,1)S(1)}, bf16[4,528,128]{2,1,0:T(8,128)(2,1)S(1)}, u32[]{:S(2)}, u32[]{:S(2)}) collective-permute-start(bf16[4,528,128]{2,1,0:T(8,128)(2,1)S(1)} %pad_maximum_fusion.2), channel_id=1, source_target_pairs={{0,16},{1,65},{2,18},{3,67},{4,20},{5,69},{6,22},{7,71},{8,24},{9,... | collective-permute-start | bytes 1622024 | tf_op jit(solution)/shard_map/ppermute | solution.py:367
  52.3 1.5 %collective-permute-start.3 = (bf16[4,528,128]{2,1,0:T(8,128)(2,1)S(1)}, bf16[4,528,128]{2,1,0:T(8,128)(2,1)S(1)}, u32[]{:S(2)}, u32[]{:S(2)}) collective-permute-start(bf16[4,528,128]{2,1,0:T(8,128)(2,1)S(1)} %pad_maximum_fusion), channel_id=1, source_target_pairs={{0,8},{1,33},{2,10},{3,35},{4,12},{5,37},{6,14},{7,39},{8,16},{9,4... | collective-permute-start | bytes 1622024 | tf_op jit(solution)/shard_map/ppermute | solution.py:367
  53.8 1.1 collective-permute-done.15.refs_6_
  55.0 2.2 %slot_sums.3 = (bf16[32,128,128]{2,1,0:T(8,128)(2,1)S(1)}, f32[64,128,128]{2,1,0:T(8,128)S(1)}) custom-call(s32[4]{0:T(128)S(1)} %pad_add_fusion.1.place_ref, bf16[4,528,128]{2,1,0:T(8,128)(2,1)S(1)} %get-tuple-element.23.refs_0_, bf16[4,528,128]{2,1,0:T(8,128)(2,1)S(1)} %collective-permute-done.10.refs_1_, ...), custom_call_target="tpu_custom_call" | custom-call | tf_op jit(solution)/shard_map/slot_sums/pallas_call | solution.py:198
  57.2 4.5 %collective-permute-start.16 = (bf16[32,128,128]{2,1,0:T(8,128)(2,1)S(1)}, bf16[32,128,128]{2,1,0:T(8,128)(2,1)S(1)}, u32[]{:S(2)}, u32[]{:S(2)}) collective-permute-start(bf16[32,128,128]{2,1,0:T(8,128)(2,1)S(1)} %get-tuple-element.28), channel_id=1, source_target_pairs={{0,1},{1,0},{2,3},{3,2},{4,5},{5,4},{6,7},{7,6},{8,9},{9,8},{10,11... | collective-permute-start | bytes 3145736 | tf_op jit(solution)/shard_map/ppermute | solution.py:355
  61.7 4.4 %collective-permute-done.4.refs_5_ = bf16[4,528,128]{2,1,0:T(8,128)(2,1)S(1)} collective-permute-done((bf16[4,528,128]{2,1,0:T(8,128)(2,1)S(1)}, bf16[4,528,128]{2,1,0:T(8,128)(2,1)S(1)}, u32[]{:S(2)}, u32[]{:S(2)}) %collective-permute-start.4) | collective-permute-done | bytes 540704 | tf_op jit(solution)/shard_map/ppermute | solution.py:367
  66.0 0.8 collective-permute-done.3.refs_4_
  66.8 2.2 %slot_sums.2 = (bf16[32,128,128]{2,1,0:T(8,128)(2,1)S(1)}, f32[64,128,128]{2,1,0:T(8,128)S(1)}) custom-call(s32[4]{0:T(128)S(1)} %pad_add_fusion.1.place_ref, bf16[4,528,128]{2,1,0:T(8,128)(2,1)S(1)} %get-tuple-element.17.refs_0_, bf16[4,528,128]{2,1,0:T(8,128)(2,1)S(1)} %collective-permute-done.refs_1_, ...), custom_call_target="tpu_custom_call" | custom-call | tf_op jit(solution)/shard_map/slot_sums/pallas_call | solution.py:198
  69.0 3.4 %collective-permute-start.6 = (bf16[32,128,128]{2,1,0:T(8,128)(2,1)S(1)}, bf16[32,128,128]{2,1,0:T(8,128)(2,1)S(1)}, u32[]{:S(2)}, u32[]{:S(2)}) collective-permute-start(bf16[32,128,128]{2,1,0:T(8,128)(2,1)S(1)} %get-tuple-element.22), channel_id=1, source_target_pairs={{0,1},{1,0},{2,3},{3,2},{4,5},{5,4},{6,7},{7,6},{8,9},{9,8},{10,11... | collective-permute-start | bytes 3145736 | tf_op jit(solution)/shard_map/ppermute | solution.py:355
  72.7 1.7 %collective-permute-start.17 = (bf16[1024,128]{1,0:T(8,128)(2,1)S(1)}, bf16[1024,128]{1,0:T(8,128)(2,1)S(1)}, u32[]{:S(2)}, u32[]{:S(2)}) collective-permute-start(bf16[1024,128]{1,0:T(8,128)(2,1)S(1)} %bitcast.26), channel_id=1, source_target_pairs={{0,2},{1,3},{2,4},{3,5},{4,6},{5,7},{6,0},{7,1},{8,10},{9,11},{10,... | collective-permute-start | bytes 786440 | tf_op jit(solution)/shard_map/ppermute | solution.py:367
  74.4 2.2 %collective-permute-start.18 = (bf16[1024,128]{1,0:T(8,128)(2,1)S(1)}, bf16[1024,128]{1,0:T(8,128)(2,1)S(1)}, u32[]{:S(2)}, u32[]{:S(2)}) collective-permute-start(bf16[1024,128]{1,0:T(8,128)(2,1)S(1)} %bitcast.24), channel_id=1, source_target_pairs={{0,6},{1,7},{2,0},{3,1},{4,2},{5,3},{6,4},{7,5},{8,14},{9,15},{10,... | collective-permute-start | bytes 786440 | tf_op jit(solution)/shard_map/ppermute | solution.py:367
  76.6 1.2 collective-permute-start.19
  78.9 1.9 %collective-permute-start.8 = (bf16[1024,128]{1,0:T(8,128)(2,1)S(1)}, bf16[1024,128]{1,0:T(8,128)(2,1)S(1)}, u32[]{:S(2)}, u32[]{:S(2)}) collective-permute-start(bf16[1024,128]{1,0:T(8,128)(2,1)S(1)} %bitcast.27), channel_id=1, source_target_pairs={{0,6},{1,7},{2,0},{3,1},{4,2},{5,3},{6,4},{7,5},{8,14},{9,15},{10,... | collective-permute-start | bytes 786440 | tf_op jit(solution)/shard_map/ppermute | solution.py:367
  80.9 2.3 %collective-permute-done.17.refs_7_ = bf16[1024,128]{1,0:T(8,128)(2,1)S(1)} collective-permute-done((bf16[1024,128]{1,0:T(8,128)(2,1)S(1)}, bf16[1024,128]{1,0:T(8,128)(2,1)S(1)}, u32[]{:S(2)}, u32[]{:S(2)}) %collective-permute-start.17) | collective-permute-done | bytes 262176 | tf_op jit(solution)/shard_map/ppermute | solution.py:367
  83.2 1.5 %collective-permute-start.9 = (bf16[1024,128]{1,0:T(8,128)(2,1)S(1)}, bf16[1024,128]{1,0:T(8,128)(2,1)S(1)}, u32[]{:S(2)}, u32[]{:S(2)}) collective-permute-start(bf16[1024,128]{1,0:T(8,128)(2,1)S(1)} %bitcast.25), channel_id=1, source_target_pairs={{0,4},{1,5},{2,6},{3,7},{4,0},{5,1},{6,2},{7,3},{8,12},{9,13},{10,... | collective-permute-start | bytes 786440 | tf_op jit(solution)/shard_map/ppermute | solution.py:367
  84.8 5.1 %collective-permute-done.19.refs_9_ = bf16[1024,128]{1,0:T(8,128)(2,1)S(1)} collective-permute-done((bf16[1024,128]{1,0:T(8,128)(2,1)S(1)}, bf16[1024,128]{1,0:T(8,128)(2,1)S(1)}, u32[]{:S(2)}, u32[]{:S(2)}) %collective-permute-start.19) | collective-permute-done | bytes 262176 | tf_op jit(solution)/shard_map/ppermute | solution.py:367
  89.8 4.6 %collective-permute-done.7.refs_2_ = bf16[1024,128]{1,0:T(8,128)(2,1)S(1)} collective-permute-done((bf16[1024,128]{1,0:T(8,128)(2,1)S(1)}, bf16[1024,128]{1,0:T(8,128)(2,1)S(1)}, u32[]{:S(2)}, u32[]{:S(2)}) %collective-permute-start.7) | collective-permute-done | bytes 262176 | tf_op jit(solution)/shard_map/ppermute | solution.py:367
  94.4 6.6 %collective-permute-done.9.refs_4_ = bf16[1024,128]{1,0:T(8,128)(2,1)S(1)} collective-permute-done((bf16[1024,128]{1,0:T(8,128)(2,1)S(1)}, bf16[1024,128]{1,0:T(8,128)(2,1)S(1)}, u32[]{:S(2)}, u32[]{:S(2)}) %collective-permute-start.9) | collective-permute-done | bytes 262176 | tf_op jit(solution)/shard_map/ppermute | solution.py:367
  101.1 2.0 %sum_gram.1 = (f32[1024,256]{1,0:T(8,128)S(1)}, f32[128,256]{1,0:T(8,128)S(1)}, f32[128,256]{1,0:T(8,128)S(1)}) custom-call(s32[4]{0:T(128)S(1)} %pad_add_fusion.1.place_ref, f32[1024,128]{1,0:T(8,128)S(1)} %bitcast.19, bf16[1024,128]{1,0:T(8,128)(2,1)S(1)} %bitcast.21, bf16[1024,128]{1,0:T(8,128)(2,1)S(1)} %collective-permute-done.7.refs_2_, ...), custom_call_target="tpu_custom_call" | custom-call | tf_op jit(solution)/shard_map/sum_gram/pallas_call | solution.py:235
  103.0 0.9 collective-permute-start.20
  103.9 1.0 collective-permute-done.20
  105.4 1.9 %collective-permute-start.22 = (f32[128,256]{1,0:T(8,128)S(1)}, f32[128,256]{1,0:T(8,128)S(1)}, u32[]{:S(2)}, u32[]{:S(2)}) collective-permute-start(f32[128,256]{1,0:T(8,128)S(1)} %add.71), channel_id=1, source_target_pairs={{0,2},{1,33},{2,4},{3,35},{4,6},{5,37},{6,0},{7,39},{8,10},{9,41},... | collective-permute-start | bytes 393224 | tf_op jit(solution)/shard_map/ppermute | solution.py:367
  107.3 1.4 collective-permute-start.23
  108.7 1.9 %collective-permute-done.21 = f32[128,256]{1,0:T(8,128)S(1)} collective-permute-done((f32[128,256]{1,0:T(8,128)S(1)}, f32[128,256]{1,0:T(8,128)S(1)}, u32[]{:S(2)}, u32[]{:S(2)}) %collective-permute-start.21) | collective-permute-done | bytes 131104 | tf_op jit(solution)/shard_map/ppermute | solution.py:367
  110.6 1.4 collective-permute-done.22
  112.1 3.3 %collective-permute-start.24 = (f32[128,256]{1,0:T(8,128)S(1)}, f32[128,256]{1,0:T(8,128)S(1)}, u32[]{:S(2)}, u32[]{:S(2)}) collective-permute-start(f32[128,256]{1,0:T(8,128)S(1)} %add_add_fusion.2), channel_id=1, source_target_pairs={{0,64},{1,17},{2,66},{3,19},{4,68},{5,21},{6,70},{7,23},{8,72},{9,... | collective-permute-start | bytes 393224 | tf_op jit(solution)/shard_map/ppermute | solution.py:367
  115.3 2.7 %collective-permute-start.26 = (f32[128,256]{1,0:T(8,128)S(1)}, f32[128,256]{1,0:T(8,128)S(1)}, u32[]{:S(2)}, u32[]{:S(2)}) collective-permute-start(f32[128,256]{1,0:T(8,128)S(1)} %add_add_fusion.2), channel_id=1, source_target_pairs={{0,96},{1,25},{2,98},{3,27},{4,100},{5,29},{6,102},{7,31},{8,104},... | collective-permute-start | bytes 393224 | tf_op jit(solution)/shard_map/ppermute | solution.py:367
  118.0 2.6 %collective-permute-done.25 = f32[128,256]{1,0:T(8,128)S(1)} collective-permute-done((f32[128,256]{1,0:T(8,128)S(1)}, f32[128,256]{1,0:T(8,128)S(1)}, u32[]{:S(2)}, u32[]{:S(2)}) %collective-permute-start.25) | collective-permute-done | bytes 131104 | tf_op jit(solution)/shard_map/ppermute | solution.py:367
  120.8 2.1 %collective-permute-start.28 = (f32[128,256]{1,0:T(8,128)S(1)}, f32[128,256]{1,0:T(8,128)S(1)}, u32[]{:S(2)}, u32[]{:S(2)}) collective-permute-start(f32[128,256]{1,0:T(8,128)S(1)} %add_add_fusion.1), channel_id=1, source_target_pairs={{0,8},{1,3},{2,10},{3,5},{4,12},{5,7},{6,14},{7,1},{8,16},{9,11},{... | collective-permute-start | bytes 393224 | tf_op jit(solution)/shard_map/ppermute | solution.py:367
  122.9 0.8 collective-permute-start.29
  123.7 2.7 %collective-permute-done.27 = f32[128,256]{1,0:T(8,128)S(1)} collective-permute-done((f32[128,256]{1,0:T(8,128)S(1)}, f32[128,256]{1,0:T(8,128)S(1)}, u32[]{:S(2)}, u32[]{:S(2)}) %collective-permute-start.27) | collective-permute-done | bytes 131104 | tf_op jit(solution)/shard_map/ppermute | solution.py:367
  126.4 1.1 collective-permute-done.28
  127.5 3.6 %collective-permute-start.30 = (f32[128,256]{1,0:T(8,128)S(1)}, f32[128,256]{1,0:T(8,128)S(1)}, u32[]{:S(2)}, u32[]{:S(2)}) collective-permute-start(f32[128,256]{1,0:T(8,128)S(1)} %add_add_fusion.mine_ref), channel_id=1, source_target_pairs={{0,1},{1,0},{2,3},{3,2},{4,5},{5,4},{6,7},{7,6},{8,9},{9,8},{10,11... | collective-permute-start | bytes 393224 | tf_op jit(solution)/shard_map/ppermute | solution.py:355
  131.1 1.0 collective-permute-done.30.other_ref
  132.1 13.0 %factor_basis.1 = (f32[1024,256]{1,0:T(8,128)}, f32[256,256]{1,0:T(8,128)}) custom-call(s32[4]{0:T(128)S(1)} %pad_add_fusion.1.place_ref, f32[128,256]{1,0:T(8,128)S(1)} %add_add_fusion.mine_ref, f32[128,256]{1,0:T(8,128)S(1)} %collective-permute-done.30.other_ref, f32[1024,256]{1,0:T(8,128)S(1)} %get-tuple-element.31.sketch_ref), custom_call_target="tpu_custom_call" | custom-call | tf_op jit(solution)/shard_map/factor_basis/pallas_call | solution.py:340
  (43 shorter events, 3.9 us)
Async XLA Ops:
  13.3 10.4 %collective-permute-start.10 = (bf16[4,528,128]{2,1,0:T(8,128)(2,1)S(1)}, bf16[4,528,128]{2,1,0:T(8,128)(2,1)S(1)}, u32[]{:S(2)}, u32[]{:S(2)}) collective-permute-start(bf16[4,528,128]{2,1,0:T(8,128)(2,1)S(1)} %get-tuple-element.24), channel_id=1, source_target_pairs={{0,32},{1,9},{2,34},{3,11},{4,36},{5,13},{6,38},{7,15},{8,40},{9,1... | collective-permute-start | bytes 1622024 | tf_op jit(solution)/shard_map/ppermute | solution.py:367
  15.4 10.1 %collective-permute-start.11 = (bf16[4,528,128]{2,1,0:T(8,128)(2,1)S(1)}, bf16[4,528,128]{2,1,0:T(8,128)(2,1)S(1)}, u32[]{:S(2)}, u32[]{:S(2)}) collective-permute-start(bf16[4,528,128]{2,1,0:T(8,128)(2,1)S(1)} %get-tuple-element.25), channel_id=1, source_target_pairs={{0,96},{1,25},{2,98},{3,27},{4,100},{5,29},{6,102},{7,31},{8,104},... | collective-permute-start | bytes 1622024 | tf_op jit(solution)/shard_map/ppermute | solution.py:367
  16.7 14.0 %collective-permute-start.12 = (bf16[4,528,128]{2,1,0:T(8,128)(2,1)S(1)}, bf16[4,528,128]{2,1,0:T(8,128)(2,1)S(1)}, u32[]{:S(2)}, u32[]{:S(2)}) collective-permute-start(bf16[4,528,128]{2,1,0:T(8,128)(2,1)S(1)} %get-tuple-element.26), channel_id=1, source_target_pairs={{0,64},{1,17},{2,66},{3,19},{4,68},{5,21},{6,70},{7,23},{8,72},{9,... | collective-permute-start | bytes 1622024 | tf_op jit(solution)/shard_map/ppermute | solution.py:367
  18.4 16.9 %collective-permute-start = (bf16[4,528,128]{2,1,0:T(8,128)(2,1)S(1)}, bf16[4,528,128]{2,1,0:T(8,128)(2,1)S(1)}, u32[]{:S(2)}, u32[]{:S(2)}) collective-permute-start(bf16[4,528,128]{2,1,0:T(8,128)(2,1)S(1)} %get-tuple-element.18), channel_id=1, source_target_pairs={{0,32},{1,9},{2,34},{3,11},{4,36},{5,13},{6,38},{7,15},{8,40},{9,1... | collective-permute-start | bytes 1622024 | tf_op jit(solution)/shard_map/ppermute | solution.py:367
  18.7 20.5 %collective-permute-start.1 = (bf16[4,528,128]{2,1,0:T(8,128)(2,1)S(1)}, bf16[4,528,128]{2,1,0:T(8,128)(2,1)S(1)}, u32[]{:S(2)}, u32[]{:S(2)}) collective-permute-start(bf16[4,528,128]{2,1,0:T(8,128)(2,1)S(1)} %get-tuple-element.19), channel_id=1, source_target_pairs={{0,96},{1,25},{2,98},{3,27},{4,100},{5,29},{6,102},{7,31},{8,104},... | collective-permute-start | bytes 1622024 | tf_op jit(solution)/shard_map/ppermute | solution.py:367
  23.7 22.7 %collective-permute-start.2 = (bf16[4,528,128]{2,1,0:T(8,128)(2,1)S(1)}, bf16[4,528,128]{2,1,0:T(8,128)(2,1)S(1)}, u32[]{:S(2)}, u32[]{:S(2)}) collective-permute-start(bf16[4,528,128]{2,1,0:T(8,128)(2,1)S(1)} %get-tuple-element.20), channel_id=1, source_target_pairs={{0,64},{1,17},{2,66},{3,19},{4,68},{5,21},{6,70},{7,23},{8,72},{9,... | collective-permute-start | bytes 1622024 | tf_op jit(solution)/shard_map/ppermute | solution.py:367
  30.8 21.5 %collective-permute-start.13 = (bf16[4,528,128]{2,1,0:T(8,128)(2,1)S(1)}, bf16[4,528,128]{2,1,0:T(8,128)(2,1)S(1)}, u32[]{:S(2)}, u32[]{:S(2)}) collective-permute-start(bf16[4,528,128]{2,1,0:T(8,128)(2,1)S(1)} %pad_maximum_fusion.3), channel_id=1, source_target_pairs={{0,8},{1,33},{2,10},{3,35},{4,12},{5,37},{6,14},{7,39},{8,16},{9,4... | collective-permute-start | bytes 1622024 | tf_op jit(solution)/shard_map/ppermute | solution.py:367
  32.0 21.8 %collective-permute-start.14 = (bf16[4,528,128]{2,1,0:T(8,128)(2,1)S(1)}, bf16[4,528,128]{2,1,0:T(8,128)(2,1)S(1)}, u32[]{:S(2)}, u32[]{:S(2)}) collective-permute-start(bf16[4,528,128]{2,1,0:T(8,128)(2,1)S(1)} %pad_maximum_fusion.4), channel_id=1, source_target_pairs={{0,24},{1,97},{2,26},{3,99},{4,28},{5,101},{6,30},{7,103},{8,0},{9... | collective-permute-start | bytes 1622024 | tf_op jit(solution)/shard_map/ppermute | solution.py:367
  35.3 19.7 %collective-permute-start.15 = (bf16[4,528,128]{2,1,0:T(8,128)(2,1)S(1)}, bf16[4,528,128]{2,1,0:T(8,128)(2,1)S(1)}, u32[]{:S(2)}, u32[]{:S(2)}) collective-permute-start(bf16[4,528,128]{2,1,0:T(8,128)(2,1)S(1)} %pad_maximum_fusion.5), channel_id=1, source_target_pairs={{0,16},{1,65},{2,18},{3,67},{4,20},{5,69},{6,22},{7,71},{8,24},{9,... | collective-permute-start | bytes 1622024 | tf_op jit(solution)/shard_map/ppermute | solution.py:367
  46.5 15.1 %collective-permute-start.5 = (bf16[4,528,128]{2,1,0:T(8,128)(2,1)S(1)}, bf16[4,528,128]{2,1,0:T(8,128)(2,1)S(1)}, u32[]{:S(2)}, u32[]{:S(2)}) collective-permute-start(bf16[4,528,128]{2,1,0:T(8,128)(2,1)S(1)} %pad_maximum_fusion.2), channel_id=1, source_target_pairs={{0,16},{1,65},{2,18},{3,67},{4,20},{5,69},{6,22},{7,71},{8,24},{9,... | collective-permute-start | bytes 1622024 | tf_op jit(solution)/shard_map/ppermute | solution.py:367
  52.1 13.9 %collective-permute-start.4 = (bf16[4,528,128]{2,1,0:T(8,128)(2,1)S(1)}, bf16[4,528,128]{2,1,0:T(8,128)(2,1)S(1)}, u32[]{:S(2)}, u32[]{:S(2)}) collective-permute-start(bf16[4,528,128]{2,1,0:T(8,128)(2,1)S(1)} %pad_maximum_fusion.1), channel_id=1, source_target_pairs={{0,24},{1,97},{2,26},{3,99},{4,28},{5,101},{6,30},{7,103},{8,0},{9... | collective-permute-start | bytes 1622024 | tf_op jit(solution)/shard_map/ppermute | solution.py:367
  52.3 14.5 %collective-permute-start.3 = (bf16[4,528,128]{2,1,0:T(8,128)(2,1)S(1)}, bf16[4,528,128]{2,1,0:T(8,128)(2,1)S(1)}, u32[]{:S(2)}, u32[]{:S(2)}) collective-permute-start(bf16[4,528,128]{2,1,0:T(8,128)(2,1)S(1)} %pad_maximum_fusion), channel_id=1, source_target_pairs={{0,8},{1,33},{2,10},{3,35},{4,12},{5,37},{6,14},{7,39},{8,16},{9,4... | collective-permute-start | bytes 1622024 | tf_op jit(solution)/shard_map/ppermute | solution.py:367
  57.2 15.3 %collective-permute-start.16 = (bf16[32,128,128]{2,1,0:T(8,128)(2,1)S(1)}, bf16[32,128,128]{2,1,0:T(8,128)(2,1)S(1)}, u32[]{:S(2)}, u32[]{:S(2)}) collective-permute-start(bf16[32,128,128]{2,1,0:T(8,128)(2,1)S(1)} %get-tuple-element.28), channel_id=1, source_target_pairs={{0,1},{1,0},{2,3},{3,2},{4,5},{5,4},{6,7},{7,6},{8,9},{9,8},{10,11... | collective-permute-start | bytes 3145736 | tf_op jit(solution)/shard_map/ppermute | solution.py:355
  69.0 8.8 %collective-permute-start.6 = (bf16[32,128,128]{2,1,0:T(8,128)(2,1)S(1)}, bf16[32,128,128]{2,1,0:T(8,128)(2,1)S(1)}, u32[]{:S(2)}, u32[]{:S(2)}) collective-permute-start(bf16[32,128,128]{2,1,0:T(8,128)(2,1)S(1)} %get-tuple-element.22), channel_id=1, source_target_pairs={{0,1},{1,0},{2,3},{3,2},{4,5},{5,4},{6,7},{7,6},{8,9},{9,8},{10,11... | collective-permute-start | bytes 3145736 | tf_op jit(solution)/shard_map/ppermute | solution.py:355
  72.7 10.5 %collective-permute-start.17 = (bf16[1024,128]{1,0:T(8,128)(2,1)S(1)}, bf16[1024,128]{1,0:T(8,128)(2,1)S(1)}, u32[]{:S(2)}, u32[]{:S(2)}) collective-permute-start(bf16[1024,128]{1,0:T(8,128)(2,1)S(1)} %bitcast.26), channel_id=1, source_target_pairs={{0,2},{1,3},{2,4},{3,5},{4,6},{5,7},{6,0},{7,1},{8,10},{9,11},{10,... | collective-permute-start | bytes 786440 | tf_op jit(solution)/shard_map/ppermute | solution.py:367
  74.4 10.3 %collective-permute-start.18 = (bf16[1024,128]{1,0:T(8,128)(2,1)S(1)}, bf16[1024,128]{1,0:T(8,128)(2,1)S(1)}, u32[]{:S(2)}, u32[]{:S(2)}) collective-permute-start(bf16[1024,128]{1,0:T(8,128)(2,1)S(1)} %bitcast.24), channel_id=1, source_target_pairs={{0,6},{1,7},{2,0},{3,1},{4,2},{5,3},{6,4},{7,5},{8,14},{9,15},{10,... | collective-permute-start | bytes 786440 | tf_op jit(solution)/shard_map/ppermute | solution.py:367
  76.6 13.2 %collective-permute-start.19 = (bf16[1024,128]{1,0:T(8,128)(2,1)S(1)}, bf16[1024,128]{1,0:T(8,128)(2,1)S(1)}, u32[]{:S(2)}, u32[]{:S(2)}) collective-permute-start(bf16[1024,128]{1,0:T(8,128)(2,1)S(1)} %bitcast.23), channel_id=1, source_target_pairs={{0,4},{1,5},{2,6},{3,7},{4,0},{5,1},{6,2},{7,3},{8,12},{9,13},{10,... | collective-permute-start | bytes 786440 | tf_op jit(solution)/shard_map/ppermute | solution.py:367
  78.1 16.3 %collective-permute-start.7 = (bf16[1024,128]{1,0:T(8,128)(2,1)S(1)}, bf16[1024,128]{1,0:T(8,128)(2,1)S(1)}, u32[]{:S(2)}, u32[]{:S(2)}) collective-permute-start(bf16[1024,128]{1,0:T(8,128)(2,1)S(1)} %bitcast.28), channel_id=1, source_target_pairs={{0,2},{1,3},{2,4},{3,5},{4,6},{5,7},{6,0},{7,1},{8,10},{9,11},{10,... | collective-permute-start | bytes 786440 | tf_op jit(solution)/shard_map/ppermute | solution.py:367
  78.9 15.5 %collective-permute-start.8 = (bf16[1024,128]{1,0:T(8,128)(2,1)S(1)}, bf16[1024,128]{1,0:T(8,128)(2,1)S(1)}, u32[]{:S(2)}, u32[]{:S(2)}) collective-permute-start(bf16[1024,128]{1,0:T(8,128)(2,1)S(1)} %bitcast.27), channel_id=1, source_target_pairs={{0,6},{1,7},{2,0},{3,1},{4,2},{5,3},{6,4},{7,5},{8,14},{9,15},{10,... | collective-permute-start | bytes 786440 | tf_op jit(solution)/shard_map/ppermute | solution.py:367
  83.2 17.9 %collective-permute-start.9 = (bf16[1024,128]{1,0:T(8,128)(2,1)S(1)}, bf16[1024,128]{1,0:T(8,128)(2,1)S(1)}, u32[]{:S(2)}, u32[]{:S(2)}) collective-permute-start(bf16[1024,128]{1,0:T(8,128)(2,1)S(1)} %bitcast.25), channel_id=1, source_target_pairs={{0,4},{1,5},{2,6},{3,7},{4,0},{5,1},{6,2},{7,3},{8,12},{9,13},{10,... | collective-permute-start | bytes 786440 | tf_op jit(solution)/shard_map/ppermute | solution.py:367
  103.0 1.9 %collective-permute-start.20 = (f32[128,256]{1,0:T(8,128)S(1)}, f32[128,256]{1,0:T(8,128)S(1)}, u32[]{:S(2)}, u32[]{:S(2)}) collective-permute-start(f32[128,256]{1,0:T(8,128)S(1)} %get-tuple-element.30), channel_id=1, source_target_pairs={{0,1},{1,0},{2,3},{3,2},{4,5},{5,4},{6,7},{7,6},{8,9},{9,8},{10,11... | collective-permute-start | bytes 393224 | tf_op jit(solution)/shard_map/ppermute | solution.py:355
  104.9 5.7 %collective-permute-start.21 = (f32[128,256]{1,0:T(8,128)S(1)}, f32[128,256]{1,0:T(8,128)S(1)}, u32[]{:S(2)}, u32[]{:S(2)}) collective-permute-start(f32[128,256]{1,0:T(8,128)S(1)} %add.71), channel_id=1, source_target_pairs={{0,4},{1,65},{2,6},{3,67},{4,0},{5,69},{6,2},{7,71},{8,12},{9,73},... | collective-permute-start | bytes 393224 | tf_op jit(solution)/shard_map/ppermute | solution.py:367
  105.4 6.7 %collective-permute-start.22 = (f32[128,256]{1,0:T(8,128)S(1)}, f32[128,256]{1,0:T(8,128)S(1)}, u32[]{:S(2)}, u32[]{:S(2)}) collective-permute-start(f32[128,256]{1,0:T(8,128)S(1)} %add.71), channel_id=1, source_target_pairs={{0,2},{1,33},{2,4},{3,35},{4,6},{5,37},{6,0},{7,39},{8,10},{9,41},... | collective-permute-start | bytes 393224 | tf_op jit(solution)/shard_map/ppermute | solution.py:367
  107.3 4.8 %collective-permute-start.23 = (f32[128,256]{1,0:T(8,128)S(1)}, f32[128,256]{1,0:T(8,128)S(1)}, u32[]{:S(2)}, u32[]{:S(2)}) collective-permute-start(f32[128,256]{1,0:T(8,128)S(1)} %add.71), channel_id=1, source_target_pairs={{0,6},{1,97},{2,0},{3,99},{4,2},{5,101},{6,4},{7,103},{8,14},{9,10... | collective-permute-start | bytes 393224 | tf_op jit(solution)/shard_map/ppermute | solution.py:367
  112.1 5.9 %collective-permute-start.24 = (f32[128,256]{1,0:T(8,128)S(1)}, f32[128,256]{1,0:T(8,128)S(1)}, u32[]{:S(2)}, u32[]{:S(2)}) collective-permute-start(f32[128,256]{1,0:T(8,128)S(1)} %add_add_fusion.2), channel_id=1, source_target_pairs={{0,64},{1,17},{2,66},{3,19},{4,68},{5,21},{6,70},{7,23},{8,72},{9,... | collective-permute-start | bytes 393224 | tf_op jit(solution)/shard_map/ppermute | solution.py:367
  115.3 5.3 %collective-permute-start.25 = (f32[128,256]{1,0:T(8,128)S(1)}, f32[128,256]{1,0:T(8,128)S(1)}, u32[]{:S(2)}, u32[]{:S(2)}) collective-permute-start(f32[128,256]{1,0:T(8,128)S(1)} %add_add_fusion.2), channel_id=1, source_target_pairs={{0,32},{1,9},{2,34},{3,11},{4,36},{5,13},{6,38},{7,15},{8,40},{9,1... | collective-permute-start | bytes 393224 | tf_op jit(solution)/shard_map/ppermute | solution.py:367
  115.3 5.3 %collective-permute-start.26 = (f32[128,256]{1,0:T(8,128)S(1)}, f32[128,256]{1,0:T(8,128)S(1)}, u32[]{:S(2)}, u32[]{:S(2)}) collective-permute-start(f32[128,256]{1,0:T(8,128)S(1)} %add_add_fusion.2), channel_id=1, source_target_pairs={{0,96},{1,25},{2,98},{3,27},{4,100},{5,29},{6,102},{7,31},{8,104},... | collective-permute-start | bytes 393224 | tf_op jit(solution)/shard_map/ppermute | solution.py:367
  120.7 5.7 %collective-permute-start.27 = (f32[128,256]{1,0:T(8,128)S(1)}, f32[128,256]{1,0:T(8,128)S(1)}, u32[]{:S(2)}, u32[]{:S(2)}) collective-permute-start(f32[128,256]{1,0:T(8,128)S(1)} %add_add_fusion.1), channel_id=1, source_target_pairs={{0,16},{1,5},{2,18},{3,7},{4,20},{5,1},{6,22},{7,3},{8,24},{9,13},... | collective-permute-start | bytes 393224 | tf_op jit(solution)/shard_map/ppermute | solution.py:367
  120.8 6.7 %collective-permute-start.28 = (f32[128,256]{1,0:T(8,128)S(1)}, f32[128,256]{1,0:T(8,128)S(1)}, u32[]{:S(2)}, u32[]{:S(2)}) collective-permute-start(f32[128,256]{1,0:T(8,128)S(1)} %add_add_fusion.1), channel_id=1, source_target_pairs={{0,8},{1,3},{2,10},{3,5},{4,12},{5,7},{6,14},{7,1},{8,16},{9,11},{... | collective-permute-start | bytes 393224 | tf_op jit(solution)/shard_map/ppermute | solution.py:367
  122.9 4.6 %collective-permute-start.29 = (f32[128,256]{1,0:T(8,128)S(1)}, f32[128,256]{1,0:T(8,128)S(1)}, u32[]{:S(2)}, u32[]{:S(2)}) collective-permute-start(f32[128,256]{1,0:T(8,128)S(1)} %add_add_fusion.1), channel_id=1, source_target_pairs={{0,24},{1,7},{2,26},{3,1},{4,28},{5,3},{6,30},{7,5},{8,0},{9,15},{... | collective-permute-start | bytes 393224 | tf_op jit(solution)/shard_map/ppermute | solution.py:367
  127.5 4.6 %collective-permute-start.30 = (f32[128,256]{1,0:T(8,128)S(1)}, f32[128,256]{1,0:T(8,128)S(1)}, u32[]{:S(2)}, u32[]{:S(2)}) collective-permute-start(f32[128,256]{1,0:T(8,128)S(1)} %add_add_fusion.mine_ref), channel_id=1, source_target_pairs={{0,1},{1,0},{2,3},{3,2},{4,5},{5,4},{6,7},{7,6},{8,9},{9,8},{10,11... | collective-permute-start | bytes 393224 | tf_op jit(solution)/shard_map/ppermute | solution.py:355

commit v3 on v2

--- a/solution.py
+++ b/solution.py
@@ -224,9 +224,14 @@
     gram[...] = lax.dot_general(
         sketch, sketch, (((0,), (0,)), ((), ())), precision=HIGHEST, preferred_element_type=F32
     )
-    half = send_ref.shape[0]
-    send_ref[...] = gram[pl.ds(pl.multiple_of((1 - core) * half, half), half), :]
-    keep_ref[...] = gram[pl.ds(pl.multiple_of(core * half, half), half), :]
+    for side, (upper_ref, lower_ref) in enumerate(((keep_ref, send_ref), (send_ref, keep_ref))):
+
+        @pl.when(core == side)
+        def _():
+            upper_ref[0:BS, :] = gram[0:BS, 0:BS]
+            upper_ref[BS:, :] = gram[0 : BS // 2, BS:]
+            lower_ref[0:BS, :] = gram[BS:, BS:]
+            lower_ref[BS:, :] = gram[BS // 2 : BS, BS:]
 
 
 def gram_halves(place, parts):
@@ -238,8 +243,8 @@
         out_specs=[WHOLE] * 3,
         out_shape=[
             jax.ShapeDtypeStruct((rows, width), F32),
-            jax.ShapeDtypeStruct((width // 2, width), F32),
-            jax.ShapeDtypeStruct((width // 2, width), F32),
+            jax.ShapeDtypeStruct((BS + BS // 2, BS), F32),
+            jax.ShapeDtypeStruct((BS + BS // 2, BS), F32),
         ],
         scratch_shapes=[pltpu.VMEM((width, width), F32)],
         compiler_params=pltpu.CompilerParams(vmem_limit_bytes=20 * MIB),
@@ -273,7 +278,7 @@
     return jnp.broadcast_to(value, (8, BS))
 
 
-def factor_panel(panel, lane):
+def factor_panel(panel, lane, meanwhile):
     sub = lax.broadcasted_iota(jnp.int32, (8, BS), 0)
     for g in range(len(panel)):
         at = lane + 8 * g
@@ -293,6 +298,8 @@
             done.append(total)
         panel[g] = done
         done_rows = [[wide(tile[k : k + 1, :]) for k in range(8)] for tile in done]
+        if g == 0:
+            meanwhile()
         for h in range(g + 1, len(panel)):
             cols = [wide(panel[h][0][:, at + c : at + c + 1]) for c in range(8)]
             for k in range(8):
@@ -305,29 +312,41 @@
 
 def factor_kernel(scale, place_ref, mine_ref, other_ref, sketch_ref, basis_ref, factor_ref, work):
     core = place_ref[1]
-    n = mine_ref.shape[1]
-    half = n // 2
-    work[pl.ds(pl.multiple_of(core * half, half), half), 0:n] = mine_ref[...]
-    work[pl.ds(pl.multiple_of((1 - core) * half, half), half), 0:n] = other_ref[...]
+    n = factor_ref.shape[1]
+    work[BS:, 0:BS] = jnp.zeros((BS, BS), F32)
+    for side, (upper_ref, lower_ref) in enumerate(((mine_ref, other_ref), (other_ref, mine_ref))):
+
+        @pl.when(core == side)
+        def _():
+            work[0:BS, 0:BS] = upper_ref[0:BS, :]
+            work[0 : BS // 2, BS:n] = upper_ref[BS:, :]
+            work[BS:n, BS:n] = lower_ref[0:BS, :]
+            work[BS // 2 : BS, BS:n] = lower_ref[BS:, :]
+
     down = lax.broadcasted_iota(jnp.int32, (n, n), 0)
     across = lax.broadcasted_iota(jnp.int32, (n, n), 1)
     work[:, n : 2 * n] = (down == across).astype(F32)
-    for j in range(0, n, PANEL):
-        first, last = (j // BS) * BS, n + (j // BS) * BS + BS
-        tiles = range(first, last, BS)
-        panel = [[work[i : i + 8, t : t + BS] for t in tiles] for i in range(j, j + PANEL, 8)]
-        factor_panel(panel, j - first)
-        for g, group in enumerate(panel):
-            for t, tile in zip(tiles, group):
-                work[j + 8 * g : j + 8 * g + 8, t : t + BS] = tile
-        if j + PANEL < n:
-            work[j + PANEL : n, first:last] -= lax.dot_general(
-                work[j : j + PANEL, j + PANEL : n],
+
+    def update(j, low, high):
+        if low < high:
+            first, last = (j // BS) * BS, n + (j // BS) * BS + BS
+            work[low:high, first:last] -= lax.dot_general(
+                work[j : j + PANEL, low:high],
                 work[j : j + PANEL, first:last],
                 (((0,), (0,)), ((), ())),
                 precision=HIGHEST,
                 preferred_element_type=F32,
             )
+
+    for j in range(0, n, PANEL):
+        first, last = (j // BS) * BS, n + (j // BS) * BS + BS
+        tiles = range(first, last, BS)
+        panel = [[work[i : i + 8, t : t + BS] for t in tiles] for i in range(j, j + PANEL, 8)]
+        factor_panel(panel, j - first, functools.partial(update, j - PANEL, j + PANEL, n if j else 0))
+        for g, group in enumerate(panel):
+            for t, tile in zip(tiles, group):
+                work[j + 8 * g : j + 8 * g + 8, t : t + BS] = tile
+        update(j, j + PANEL, min(j + 2 * PANEL, n))
     factor_ref[...] = jnp.where(down <= across, work[:, 0:n], 0.0) * (1.0 / scale)
     inverse = work[:, n : 2 * n] * scale
     basis_ref[...] = lax.dot_general(

time: 145 us -> 143 us (0.986)
  waiting for transfers between devices: 53.1 us -> 50.7 us
    ppermute x27, waiting for transfers between devices: 51.1 us -> 48.8 us  [moved(): return lax.ppermute(value, ('row', 'col'), pairs)]
  transfers between devices with their start and end apart: 31 -> 31, of which waited for: 18 -> 19; matrix products, arithmetic and copies ran while one was open for 1% -> 1% of each run, Pallas kernels for 3% -> 3%
where the time goes in v3:
time: 143 us
  starting transfers between devices  59.1 us (41%)
  waiting for transfers between devices  50.7 us (35%)
  Pallas kernels  30.2 us (21%)
  other arithmetic  1.82 us (1%)
    ppermute x27, waiting for transfers between devices, moved(): return lax.ppermute(value, ('row', 'col'), pairs)  48.8 us
    ppermute x27, starting transfers between devices, moved(): return lax.ppermute(value, ('row', 'col'), pairs)  46.5 us
    ppermute x4, starting transfers between devices, other_core(): return lax.ppermute(value, 'col', [(i, i ^ 1) for i in range(2 * SIDE)])  12.6 us
    pallas_call x1, Pallas kernels, factors(): pl.pallas_call(functools.partial(factor_kernel, scale), in_specs=[SCALARS...  12.3 us
    pallas_call x1, Pallas kernels, partials(): pl.pallas_call(partial_kernel, in_specs=[SCALARS] * 2 + [IN_HBM] * 2, out...  11.8 us
    pallas_call x2, Pallas kernels, slot_sums(): pl.pallas_call(slot_sum_kernel, in_specs=[SCALARS] + [WHOLE] * len(got),...  4.2 us
  transfers between devices with their start and end apart: 31, of which 19 were waited for; matrix products, arithmetic and copies ran while one was open for 1% of the time, Pallas kernels for 3%

profile of v3, /device:TPU:1, one launch (start us, length us, event | category | flops | bytes accessed | tf_op | source)
XLA Modules:
  0.0 143.0 jit_solution(10778149905552549381)
XLA Ops:
  1.5 11.8 %partials.1 = (bf16[4,528,128]{2,1,0:T(8,128)(2,1)S(1)}, bf16[4,528,128]{2,1,0:T(8,128)(2,1)S(1)}, bf16[4,528,128]{2,1,0:T(8,128)(2,1)S(1)}, bf16[4,528,128]{2,1...) custom-call(s32[18,32]{1,0:T(8,128)S(1)} %pad_add_fusion.index_ref, ...), custom_call_target="tpu_custom_call" | custom-call | tf_op jit(solution)/shard_map/partials/pallas_call | solution.py:138
  13.3 2.1 %collective-permute-start.10 = (bf16[4,528,128]{2,1,0:T(8,128)(2,1)S(1)}, bf16[4,528,128]{2,1,0:T(8,128)(2,1)S(1)}, u32[]{:S(2)}, u32[]{:S(2)}) collective-permute-start(bf16[4,528,128]{2,1,0:T(8,128)(2,1)S(1)} %get-tuple-element.24), channel_id=1, source_target_pairs={{0,32},{1,9},{2,34},{3,11},{4,36},{5,13},{6,38},{7,15},{8,40},{9,1... | collective-permute-start | bytes 1622024 | tf_op jit(solution)/shard_map/ppermute | solution.py:386
  15.4 1.3 collective-permute-start.11
  16.7 1.6 %collective-permute-start.12 = (bf16[4,528,128]{2,1,0:T(8,128)(2,1)S(1)}, bf16[4,528,128]{2,1,0:T(8,128)(2,1)S(1)}, u32[]{:S(2)}, u32[]{:S(2)}) collective-permute-start(bf16[4,528,128]{2,1,0:T(8,128)(2,1)S(1)} %get-tuple-element.26), channel_id=1, source_target_pairs={{0,64},{1,17},{2,66},{3,19},{4,68},{5,21},{6,70},{7,23},{8,72},{9,... | collective-permute-start | bytes 1622024 | tf_op jit(solution)/shard_map/ppermute | solution.py:386
  18.7 2.4 %collective-permute-start.1 = (bf16[4,528,128]{2,1,0:T(8,128)(2,1)S(1)}, bf16[4,528,128]{2,1,0:T(8,128)(2,1)S(1)}, u32[]{:S(2)}, u32[]{:S(2)}) collective-permute-start(bf16[4,528,128]{2,1,0:T(8,128)(2,1)S(1)} %get-tuple-element.19), channel_id=1, source_target_pairs={{0,96},{1,25},{2,98},{3,27},{4,100},{5,29},{6,102},{7,31},{8,104},... | collective-permute-start | bytes 1622024 | tf_op jit(solution)/shard_map/ppermute | solution.py:386
  21.1 2.6 %collective-permute-done.10.refs_1_ = bf16[4,528,128]{2,1,0:T(8,128)(2,1)S(1)} collective-permute-done((bf16[4,528,128]{2,1,0:T(8,128)(2,1)S(1)}, bf16[4,528,128]{2,1,0:T(8,128)(2,1)S(1)}, u32[]{:S(2)}, u32[]{:S(2)}) %collective-permute-start.10) | collective-permute-done | bytes 540704 | tf_op jit(solution)/shard_map/ppermute | solution.py:386
  23.7 1.7 %collective-permute-start.2 = (bf16[4,528,128]{2,1,0:T(8,128)(2,1)S(1)}, bf16[4,528,128]{2,1,0:T(8,128)(2,1)S(1)}, u32[]{:S(2)}, u32[]{:S(2)}) collective-permute-start(bf16[4,528,128]{2,1,0:T(8,128)(2,1)S(1)} %get-tuple-element.20), channel_id=1, source_target_pairs={{0,64},{1,17},{2,66},{3,19},{4,68},{5,21},{6,70},{7,23},{8,72},{9,... | collective-permute-start | bytes 1622024 | tf_op jit(solution)/shard_map/ppermute | solution.py:386
  25.5 5.2 %collective-permute-done.12.refs_3_ = bf16[4,528,128]{2,1,0:T(8,128)(2,1)S(1)} collective-permute-done((bf16[4,528,128]{2,1,0:T(8,128)(2,1)S(1)}, bf16[4,528,128]{2,1,0:T(8,128)(2,1)S(1)}, u32[]{:S(2)}, u32[]{:S(2)}) %collective-permute-start.12) | collective-permute-done | bytes 540704 | tf_op jit(solution)/shard_map/ppermute | solution.py:386
  30.8 1.1 collective-permute-start.13
  32.0 1.8 %collective-permute-start.14 = (bf16[4,528,128]{2,1,0:T(8,128)(2,1)S(1)}, bf16[4,528,128]{2,1,0:T(8,128)(2,1)S(1)}, u32[]{:S(2)}, u32[]{:S(2)}) collective-permute-start(bf16[4,528,128]{2,1,0:T(8,128)(2,1)S(1)} %pad_maximum_fusion.4), channel_id=1, source_target_pairs={{0,24},{1,97},{2,26},{3,99},{4,28},{5,101},{6,30},{7,103},{8,0},{9... | collective-permute-start | bytes 1622024 | tf_op jit(solution)/shard_map/ppermute | solution.py:386
  33.8 1.4 collective-permute-done.refs_1_
  35.3 3.8 %collective-permute-start.15 = (bf16[4,528,128]{2,1,0:T(8,128)(2,1)S(1)}, bf16[4,528,128]{2,1,0:T(8,128)(2,1)S(1)}, u32[]{:S(2)}, u32[]{:S(2)}) collective-permute-start(bf16[4,528,128]{2,1,0:T(8,128)(2,1)S(1)} %pad_maximum_fusion.5), channel_id=1, source_target_pairs={{0,16},{1,65},{2,18},{3,67},{4,20},{5,69},{6,22},{7,71},{8,24},{9,... | collective-permute-start | bytes 1622024 | tf_op jit(solution)/shard_map/ppermute | solution.py:386
  39.2 6.5 %collective-permute-done.2.refs_3_ = bf16[4,528,128]{2,1,0:T(8,128)(2,1)S(1)} collective-permute-done((bf16[4,528,128]{2,1,0:T(8,128)(2,1)S(1)}, bf16[4,528,128]{2,1,0:T(8,128)(2,1)S(1)}, u32[]{:S(2)}, u32[]{:S(2)}) %collective-permute-start.2) | collective-permute-done | bytes 540704 | tf_op jit(solution)/shard_map/ppermute | solution.py:386
  45.8 6.2 %collective-permute-start.5 = (bf16[4,528,128]{2,1,0:T(8,128)(2,1)S(1)}, bf16[4,528,128]{2,1,0:T(8,128)(2,1)S(1)}, u32[]{:S(2)}, u32[]{:S(2)}) collective-permute-start(bf16[4,528,128]{2,1,0:T(8,128)(2,1)S(1)} %pad_maximum_fusion.2), channel_id=1, source_target_pairs={{0,16},{1,65},{2,18},{3,67},{4,20},{5,69},{6,22},{7,71},{8,24},{9,... | collective-permute-start | bytes 1622024 | tf_op jit(solution)/shard_map/ppermute | solution.py:386
  52.2 1.5 %collective-permute-start.3 = (bf16[4,528,128]{2,1,0:T(8,128)(2,1)S(1)}, bf16[4,528,128]{2,1,0:T(8,128)(2,1)S(1)}, u32[]{:S(2)}, u32[]{:S(2)}) collective-permute-start(bf16[4,528,128]{2,1,0:T(8,128)(2,1)S(1)} %pad_maximum_fusion), channel_id=1, source_target_pairs={{0,8},{1,33},{2,10},{3,35},{4,12},{5,37},{6,14},{7,39},{8,16},{9,4... | collective-permute-start | bytes 1622024 | tf_op jit(solution)/shard_map/ppermute | solution.py:386
  53.7 1.2 collective-permute-done.15.refs_6_
  55.0 2.1 %slot_sums.3 = (bf16[32,128,128]{2,1,0:T(8,128)(2,1)S(1)}, f32[64,128,128]{2,1,0:T(8,128)S(1)}) custom-call(s32[4]{0:T(128)S(1)} %pad_add_fusion.1.place_ref, bf16[4,528,128]{2,1,0:T(8,128)(2,1)S(1)} %get-tuple-element.23.refs_0_, bf16[4,528,128]{2,1,0:T(8,128)(2,1)S(1)} %collective-permute-done.10.refs_1_, ...), custom_call_target="tpu_custom_call" | custom-call | tf_op jit(solution)/shard_map/slot_sums/pallas_call | solution.py:198
  57.1 4.5 %collective-permute-start.16 = (bf16[32,128,128]{2,1,0:T(8,128)(2,1)S(1)}, bf16[32,128,128]{2,1,0:T(8,128)(2,1)S(1)}, u32[]{:S(2)}, u32[]{:S(2)}) collective-permute-start(bf16[32,128,128]{2,1,0:T(8,128)(2,1)S(1)} %get-tuple-element.28), channel_id=1, source_target_pairs={{0,1},{1,0},{2,3},{3,2},{4,5},{5,4},{6,7},{7,6},{8,9},{9,8},{10,11... | collective-permute-start | bytes 3145736 | tf_op jit(solution)/shard_map/ppermute | solution.py:374
  61.6 4.4 %collective-permute-done.4.refs_5_ = bf16[4,528,128]{2,1,0:T(8,128)(2,1)S(1)} collective-permute-done((bf16[4,528,128]{2,1,0:T(8,128)(2,1)S(1)}, bf16[4,528,128]{2,1,0:T(8,128)(2,1)S(1)}, u32[]{:S(2)}, u32[]{:S(2)}) %collective-permute-start.4) | collective-permute-done | bytes 540704 | tf_op jit(solution)/shard_map/ppermute | solution.py:386
  66.9 2.1 %slot_sums.2 = (bf16[32,128,128]{2,1,0:T(8,128)(2,1)S(1)}, f32[64,128,128]{2,1,0:T(8,128)S(1)}) custom-call(s32[4]{0:T(128)S(1)} %pad_add_fusion.1.place_ref, bf16[4,528,128]{2,1,0:T(8,128)(2,1)S(1)} %get-tuple-element.17.refs_0_, bf16[4,528,128]{2,1,0:T(8,128)(2,1)S(1)} %collective-permute-done.refs_1_, ...), custom_call_target="tpu_custom_call" | custom-call | tf_op jit(solution)/shard_map/slot_sums/pallas_call | solution.py:198
  69.0 3.4 %collective-permute-start.6 = (bf16[32,128,128]{2,1,0:T(8,128)(2,1)S(1)}, bf16[32,128,128]{2,1,0:T(8,128)(2,1)S(1)}, u32[]{:S(2)}, u32[]{:S(2)}) collective-permute-start(bf16[32,128,128]{2,1,0:T(8,128)(2,1)S(1)} %get-tuple-element.22), channel_id=1, source_target_pairs={{0,1},{1,0},{2,3},{3,2},{4,5},{5,4},{6,7},{7,6},{8,9},{9,8},{10,11... | collective-permute-start | bytes 3145736 | tf_op jit(solution)/shard_map/ppermute | solution.py:374
  72.6 1.7 %collective-permute-start.17 = (bf16[1024,128]{1,0:T(8,128)(2,1)S(1)}, bf16[1024,128]{1,0:T(8,128)(2,1)S(1)}, u32[]{:S(2)}, u32[]{:S(2)}) collective-permute-start(bf16[1024,128]{1,0:T(8,128)(2,1)S(1)} %bitcast.26), channel_id=1, source_target_pairs={{0,2},{1,3},{2,4},{3,5},{4,6},{5,7},{6,0},{7,1},{8,10},{9,11},{10,... | collective-permute-start | bytes 786440 | tf_op jit(solution)/shard_map/ppermute | solution.py:386
  74.4 2.2 %collective-permute-start.18 = (bf16[1024,128]{1,0:T(8,128)(2,1)S(1)}, bf16[1024,128]{1,0:T(8,128)(2,1)S(1)}, u32[]{:S(2)}, u32[]{:S(2)}) collective-permute-start(bf16[1024,128]{1,0:T(8,128)(2,1)S(1)} %bitcast.24), channel_id=1, source_target_pairs={{0,6},{1,7},{2,0},{3,1},{4,2},{5,3},{6,4},{7,5},{8,14},{9,15},{10,... | collective-permute-start | bytes 786440 | tf_op jit(solution)/shard_map/ppermute | solution.py:386
  76.6 1.2 collective-permute-start.19
  78.9 1.9 %collective-permute-start.8 = (bf16[1024,128]{1,0:T(8,128)(2,1)S(1)}, bf16[1024,128]{1,0:T(8,128)(2,1)S(1)}, u32[]{:S(2)}, u32[]{:S(2)}) collective-permute-start(bf16[1024,128]{1,0:T(8,128)(2,1)S(1)} %bitcast.27), channel_id=1, source_target_pairs={{0,6},{1,7},{2,0},{3,1},{4,2},{5,3},{6,4},{7,5},{8,14},{9,15},{10,... | collective-permute-start | bytes 786440 | tf_op jit(solution)/shard_map/ppermute | solution.py:386
  80.8 2.4 %collective-permute-done.17.refs_7_ = bf16[1024,128]{1,0:T(8,128)(2,1)S(1)} collective-permute-done((bf16[1024,128]{1,0:T(8,128)(2,1)S(1)}, bf16[1024,128]{1,0:T(8,128)(2,1)S(1)}, u32[]{:S(2)}, u32[]{:S(2)}) %collective-permute-start.17) | collective-permute-done | bytes 262176 | tf_op jit(solution)/shard_map/ppermute | solution.py:386
  83.2 1.5 %collective-permute-start.9 = (bf16[1024,128]{1,0:T(8,128)(2,1)S(1)}, bf16[1024,128]{1,0:T(8,128)(2,1)S(1)}, u32[]{:S(2)}, u32[]{:S(2)}) collective-permute-start(bf16[1024,128]{1,0:T(8,128)(2,1)S(1)} %bitcast.25), channel_id=1, source_target_pairs={{0,4},{1,5},{2,6},{3,7},{4,0},{5,1},{6,2},{7,3},{8,12},{9,13},{10,... | collective-permute-start | bytes 786440 | tf_op jit(solution)/shard_map/ppermute | solution.py:386
  84.7 2.6 %collective-permute-done.18.refs_8_ = bf16[1024,128]{1,0:T(8,128)(2,1)S(1)} collective-permute-done((bf16[1024,128]{1,0:T(8,128)(2,1)S(1)}, bf16[1024,128]{1,0:T(8,128)(2,1)S(1)}, u32[]{:S(2)}, u32[]{:S(2)}) %collective-permute-start.18) | collective-permute-done | bytes 262176 | tf_op jit(solution)/shard_map/ppermute | solution.py:386
  87.3 2.5 %collective-permute-done.19.refs_9_ = bf16[1024,128]{1,0:T(8,128)(2,1)S(1)} collective-permute-done((bf16[1024,128]{1,0:T(8,128)(2,1)S(1)}, bf16[1024,128]{1,0:T(8,128)(2,1)S(1)}, u32[]{:S(2)}, u32[]{:S(2)}) %collective-permute-start.19) | collective-permute-done | bytes 262176 | tf_op jit(solution)/shard_map/ppermute | solution.py:386
  89.8 4.6 %collective-permute-done.7.refs_2_ = bf16[1024,128]{1,0:T(8,128)(2,1)S(1)} collective-permute-done((bf16[1024,128]{1,0:T(8,128)(2,1)S(1)}, bf16[1024,128]{1,0:T(8,128)(2,1)S(1)}, u32[]{:S(2)}, u32[]{:S(2)}) %collective-permute-start.7) | collective-permute-done | bytes 262176 | tf_op jit(solution)/shard_map/ppermute | solution.py:386
  94.4 6.6 %collective-permute-done.9.refs_4_ = bf16[1024,128]{1,0:T(8,128)(2,1)S(1)} collective-permute-done((bf16[1024,128]{1,0:T(8,128)(2,1)S(1)}, bf16[1024,128]{1,0:T(8,128)(2,1)S(1)}, u32[]{:S(2)}, u32[]{:S(2)}) %collective-permute-start.9) | collective-permute-done | bytes 262176 | tf_op jit(solution)/shard_map/ppermute | solution.py:386
  101.0 2.0 %sum_gram.1 = (f32[1024,256]{1,0:T(8,128)S(1)}, f32[192,128]{1,0:T(8,128)S(1)}, f32[192,128]{1,0:T(8,128)S(1)}) custom-call(s32[4]{0:T(128)S(1)} %pad_add_fusion.1.place_ref, f32[1024,128]{1,0:T(8,128)S(1)} %bitcast.19, bf16[1024,128]{1,0:T(8,128)(2,1)S(1)} %bitcast.21, bf16[1024,128]{1,0:T(8,128)(2,1)S(1)} %collective-permute-done.7.refs_2_, ...), custom_call_target="tpu_custom_call" | custom-call | tf_op jit(solution)/shard_map/sum_gram/pallas_call | solution.py:240
  103.0 0.9 collective-permute-start.20
  103.9 0.9 collective-permute-done.20
  105.4 1.9 %collective-permute-start.22 = (f32[192,128]{1,0:T(8,128)S(1)}, f32[192,128]{1,0:T(8,128)S(1)}, u32[]{:S(2)}, u32[]{:S(2)}) collective-permute-start(f32[192,128]{1,0:T(8,128)S(1)} %add.71), channel_id=1, source_target_pairs={{0,2},{1,33},{2,4},{3,35},{4,6},{5,37},{6,0},{7,39},{8,10},{9,41},... | collective-permute-start | bytes 294920 | tf_op jit(solution)/shard_map/ppermute | solution.py:386
  107.2 1.5 %collective-permute-start.23 = (f32[192,128]{1,0:T(8,128)S(1)}, f32[192,128]{1,0:T(8,128)S(1)}, u32[]{:S(2)}, u32[]{:S(2)}) collective-permute-start(f32[192,128]{1,0:T(8,128)S(1)} %add.71), channel_id=1, source_target_pairs={{0,6},{1,97},{2,0},{3,99},{4,2},{5,101},{6,4},{7,103},{8,14},{9,10... | collective-permute-start | bytes 294920 | tf_op jit(solution)/shard_map/ppermute | solution.py:386
  108.7 1.5 %collective-permute-done.21 = f32[192,128]{1,0:T(8,128)S(1)} collective-permute-done((f32[192,128]{1,0:T(8,128)S(1)}, f32[192,128]{1,0:T(8,128)S(1)}, u32[]{:S(2)}, u32[]{:S(2)}) %collective-permute-start.21) | collective-permute-done | bytes 98336 | tf_op jit(solution)/shard_map/ppermute | solution.py:386
  110.2 1.1 collective-permute-done.22
  111.2 3.3 %collective-permute-start.24 = (f32[192,128]{1,0:T(8,128)S(1)}, f32[192,128]{1,0:T(8,128)S(1)}, u32[]{:S(2)}, u32[]{:S(2)}) collective-permute-start(f32[192,128]{1,0:T(8,128)S(1)} %add_add_fusion.2), channel_id=1, source_target_pairs={{0,64},{1,17},{2,66},{3,19},{4,68},{5,21},{6,70},{7,23},{8,72},{9,... | collective-permute-start | bytes 294920 | tf_op jit(solution)/shard_map/ppermute | solution.py:386
  114.6 2.7 %collective-permute-start.26 = (f32[192,128]{1,0:T(8,128)S(1)}, f32[192,128]{1,0:T(8,128)S(1)}, u32[]{:S(2)}, u32[]{:S(2)}) collective-permute-start(f32[192,128]{1,0:T(8,128)S(1)} %add_add_fusion.2), channel_id=1, source_target_pairs={{0,96},{1,25},{2,98},{3,27},{4,100},{5,29},{6,102},{7,31},{8,104},... | collective-permute-start | bytes 294920 | tf_op jit(solution)/shard_map/ppermute | solution.py:386
  117.3 2.2 %collective-permute-done.25 = f32[192,128]{1,0:T(8,128)S(1)} collective-permute-done((f32[192,128]{1,0:T(8,128)S(1)}, f32[192,128]{1,0:T(8,128)S(1)}, u32[]{:S(2)}, u32[]{:S(2)}) %collective-permute-start.25) | collective-permute-done | bytes 98336 | tf_op jit(solution)/shard_map/ppermute | solution.py:386
  119.6 2.0 %collective-permute-start.28 = (f32[192,128]{1,0:T(8,128)S(1)}, f32[192,128]{1,0:T(8,128)S(1)}, u32[]{:S(2)}, u32[]{:S(2)}) collective-permute-start(f32[192,128]{1,0:T(8,128)S(1)} %add_add_fusion.1), channel_id=1, source_target_pairs={{0,8},{1,3},{2,10},{3,5},{4,12},{5,7},{6,14},{7,1},{8,16},{9,11},{... | collective-permute-start | bytes 294920 | tf_op jit(solution)/shard_map/ppermute | solution.py:386
  121.5 1.1 collective-permute-start.29
  122.7 1.9 %collective-permute-done.27 = f32[192,128]{1,0:T(8,128)S(1)} collective-permute-done((f32[192,128]{1,0:T(8,128)S(1)}, f32[192,128]{1,0:T(8,128)S(1)}, u32[]{:S(2)}, u32[]{:S(2)}) %collective-permute-start.27) | collective-permute-done | bytes 98336 | tf_op jit(solution)/shard_map/ppermute | solution.py:386
  124.6 1.3 collective-permute-done.28
  125.9 3.8 %collective-permute-start.30 = (f32[192,128]{1,0:T(8,128)S(1)}, f32[192,128]{1,0:T(8,128)S(1)}, u32[]{:S(2)}, u32[]{:S(2)}) collective-permute-start(f32[192,128]{1,0:T(8,128)S(1)} %add_add_fusion.mine_ref), channel_id=1, source_target_pairs={{0,1},{1,0},{2,3},{3,2},{4,5},{5,4},{6,7},{7,6},{8,9},{9,8},{10,11... | collective-permute-start | bytes 294920 | tf_op jit(solution)/shard_map/ppermute | solution.py:374
  129.7 0.9 collective-permute-done.30.other_ref
  130.7 12.3 %factor_basis.1 = (f32[1024,256]{1,0:T(8,128)}, f32[256,256]{1,0:T(8,128)}) custom-call(s32[4]{0:T(128)S(1)} %pad_add_fusion.1.place_ref, f32[192,128]{1,0:T(8,128)S(1)} %add_add_fusion.mine_ref, f32[192,128]{1,0:T(8,128)S(1)} %collective-permute-done.30.other_ref, f32[1024,256]{1,0:T(8,128)S(1)} %get-tuple-element.31.sketch_ref), custom_call_target="tpu_custom_call" | custom-call | tf_op jit(solution)/shard_map/factor_basis/pallas_call | solution.py:359
  (43 shorter events, 4.8 us)
Async XLA Ops:
  13.3 10.4 %collective-permute-start.10 = (bf16[4,528,128]{2,1,0:T(8,128)(2,1)S(1)}, bf16[4,528,128]{2,1,0:T(8,128)(2,1)S(1)}, u32[]{:S(2)}, u32[]{:S(2)}) collective-permute-start(bf16[4,528,128]{2,1,0:T(8,128)(2,1)S(1)} %get-tuple-element.24), channel_id=1, source_target_pairs={{0,32},{1,9},{2,34},{3,11},{4,36},{5,13},{6,38},{7,15},{8,40},{9,1... | collective-permute-start | bytes 1622024 | tf_op jit(solution)/shard_map/ppermute | solution.py:386
  15.4 10.1 %collective-permute-start.11 = (bf16[4,528,128]{2,1,0:T(8,128)(2,1)S(1)}, bf16[4,528,128]{2,1,0:T(8,128)(2,1)S(1)}, u32[]{:S(2)}, u32[]{:S(2)}) collective-permute-start(bf16[4,528,128]{2,1,0:T(8,128)(2,1)S(1)} %get-tuple-element.25), channel_id=1, source_target_pairs={{0,96},{1,25},{2,98},{3,27},{4,100},{5,29},{6,102},{7,31},{8,104},... | collective-permute-start | bytes 1622024 | tf_op jit(solution)/shard_map/ppermute | solution.py:386
  16.7 14.0 %collective-permute-start.12 = (bf16[4,528,128]{2,1,0:T(8,128)(2,1)S(1)}, bf16[4,528,128]{2,1,0:T(8,128)(2,1)S(1)}, u32[]{:S(2)}, u32[]{:S(2)}) collective-permute-start(bf16[4,528,128]{2,1,0:T(8,128)(2,1)S(1)} %get-tuple-element.26), channel_id=1, source_target_pairs={{0,64},{1,17},{2,66},{3,19},{4,68},{5,21},{6,70},{7,23},{8,72},{9,... | collective-permute-start | bytes 1622024 | tf_op jit(solution)/shard_map/ppermute | solution.py:386
  18.4 16.9 %collective-permute-start = (bf16[4,528,128]{2,1,0:T(8,128)(2,1)S(1)}, bf16[4,528,128]{2,1,0:T(8,128)(2,1)S(1)}, u32[]{:S(2)}, u32[]{:S(2)}) collective-permute-start(bf16[4,528,128]{2,1,0:T(8,128)(2,1)S(1)} %get-tuple-element.18), channel_id=1, source_target_pairs={{0,32},{1,9},{2,34},{3,11},{4,36},{5,13},{6,38},{7,15},{8,40},{9,1... | collective-permute-start | bytes 1622024 | tf_op jit(solution)/shard_map/ppermute | solution.py:386
  18.7 20.5 %collective-permute-start.1 = (bf16[4,528,128]{2,1,0:T(8,128)(2,1)S(1)}, bf16[4,528,128]{2,1,0:T(8,128)(2,1)S(1)}, u32[]{:S(2)}, u32[]{:S(2)}) collective-permute-start(bf16[4,528,128]{2,1,0:T(8,128)(2,1)S(1)} %get-tuple-element.19), channel_id=1, source_target_pairs={{0,96},{1,25},{2,98},{3,27},{4,100},{5,29},{6,102},{7,31},{8,104},... | collective-permute-start | bytes 1622024 | tf_op jit(solution)/shard_map/ppermute | solution.py:386
  23.7 22.0 %collective-permute-start.2 = (bf16[4,528,128]{2,1,0:T(8,128)(2,1)S(1)}, bf16[4,528,128]{2,1,0:T(8,128)(2,1)S(1)}, u32[]{:S(2)}, u32[]{:S(2)}) collective-permute-start(bf16[4,528,128]{2,1,0:T(8,128)(2,1)S(1)} %get-tuple-element.20), channel_id=1, source_target_pairs={{0,64},{1,17},{2,66},{3,19},{4,68},{5,21},{6,70},{7,23},{8,72},{9,... | collective-permute-start | bytes 1622024 | tf_op jit(solution)/shard_map/ppermute | solution.py:386
  30.8 21.4 %collective-permute-start.13 = (bf16[4,528,128]{2,1,0:T(8,128)(2,1)S(1)}, bf16[4,528,128]{2,1,0:T(8,128)(2,1)S(1)}, u32[]{:S(2)}, u32[]{:S(2)}) collective-permute-start(bf16[4,528,128]{2,1,0:T(8,128)(2,1)S(1)} %pad_maximum_fusion.3), channel_id=1, source_target_pairs={{0,8},{1,33},{2,10},{3,35},{4,12},{5,37},{6,14},{7,39},{8,16},{9,4... | collective-permute-start | bytes 1622024 | tf_op jit(solution)/shard_map/ppermute | solution.py:386
  32.0 21.7 %collective-permute-start.14 = (bf16[4,528,128]{2,1,0:T(8,128)(2,1)S(1)}, bf16[4,528,128]{2,1,0:T(8,128)(2,1)S(1)}, u32[]{:S(2)}, u32[]{:S(2)}) collective-permute-start(bf16[4,528,128]{2,1,0:T(8,128)(2,1)S(1)} %pad_maximum_fusion.4), channel_id=1, source_target_pairs={{0,24},{1,97},{2,26},{3,99},{4,28},{5,101},{6,30},{7,103},{8,0},{9... | collective-permute-start | bytes 1622024 | tf_op jit(solution)/shard_map/ppermute | solution.py:386
  35.3 19.7 %collective-permute-start.15 = (bf16[4,528,128]{2,1,0:T(8,128)(2,1)S(1)}, bf16[4,528,128]{2,1,0:T(8,128)(2,1)S(1)}, u32[]{:S(2)}, u32[]{:S(2)}) collective-permute-start(bf16[4,528,128]{2,1,0:T(8,128)(2,1)S(1)} %pad_maximum_fusion.5), channel_id=1, source_target_pairs={{0,16},{1,65},{2,18},{3,67},{4,20},{5,69},{6,22},{7,71},{8,24},{9,... | collective-permute-start | bytes 1622024 | tf_op jit(solution)/shard_map/ppermute | solution.py:386
  45.8 15.8 %collective-permute-start.5 = (bf16[4,528,128]{2,1,0:T(8,128)(2,1)S(1)}, bf16[4,528,128]{2,1,0:T(8,128)(2,1)S(1)}, u32[]{:S(2)}, u32[]{:S(2)}) collective-permute-start(bf16[4,528,128]{2,1,0:T(8,128)(2,1)S(1)} %pad_maximum_fusion.2), channel_id=1, source_target_pairs={{0,16},{1,65},{2,18},{3,67},{4,20},{5,69},{6,22},{7,71},{8,24},{9,... | collective-permute-start | bytes 1622024 | tf_op jit(solution)/shard_map/ppermute | solution.py:386
  52.1 14.0 %collective-permute-start.4 = (bf16[4,528,128]{2,1,0:T(8,128)(2,1)S(1)}, bf16[4,528,128]{2,1,0:T(8,128)(2,1)S(1)}, u32[]{:S(2)}, u32[]{:S(2)}) collective-permute-start(bf16[4,528,128]{2,1,0:T(8,128)(2,1)S(1)} %pad_maximum_fusion.1), channel_id=1, source_target_pairs={{0,24},{1,97},{2,26},{3,99},{4,28},{5,101},{6,30},{7,103},{8,0},{9... | collective-permute-start | bytes 1622024 | tf_op jit(solution)/shard_map/ppermute | solution.py:386
  52.2 14.6 %collective-permute-start.3 = (bf16[4,528,128]{2,1,0:T(8,128)(2,1)S(1)}, bf16[4,528,128]{2,1,0:T(8,128)(2,1)S(1)}, u32[]{:S(2)}, u32[]{:S(2)}) collective-permute-start(bf16[4,528,128]{2,1,0:T(8,128)(2,1)S(1)} %pad_maximum_fusion), channel_id=1, source_target_pairs={{0,8},{1,33},{2,10},{3,35},{4,12},{5,37},{6,14},{7,39},{8,16},{9,4... | collective-permute-start | bytes 1622024 | tf_op jit(solution)/shard_map/ppermute | solution.py:386
  57.1 15.3 %collective-permute-start.16 = (bf16[32,128,128]{2,1,0:T(8,128)(2,1)S(1)}, bf16[32,128,128]{2,1,0:T(8,128)(2,1)S(1)}, u32[]{:S(2)}, u32[]{:S(2)}) collective-permute-start(bf16[32,128,128]{2,1,0:T(8,128)(2,1)S(1)} %get-tuple-element.28), channel_id=1, source_target_pairs={{0,1},{1,0},{2,3},{3,2},{4,5},{5,4},{6,7},{7,6},{8,9},{9,8},{10,11... | collective-permute-start | bytes 3145736 | tf_op jit(solution)/shard_map/ppermute | solution.py:374
  69.0 8.8 %collective-permute-start.6 = (bf16[32,128,128]{2,1,0:T(8,128)(2,1)S(1)}, bf16[32,128,128]{2,1,0:T(8,128)(2,1)S(1)}, u32[]{:S(2)}, u32[]{:S(2)}) collective-permute-start(bf16[32,128,128]{2,1,0:T(8,128)(2,1)S(1)} %get-tuple-element.22), channel_id=1, source_target_pairs={{0,1},{1,0},{2,3},{3,2},{4,5},{5,4},{6,7},{7,6},{8,9},{9,8},{10,11... | collective-permute-start | bytes 3145736 | tf_op jit(solution)/shard_map/ppermute | solution.py:374
  72.6 10.5 %collective-permute-start.17 = (bf16[1024,128]{1,0:T(8,128)(2,1)S(1)}, bf16[1024,128]{1,0:T(8,128)(2,1)S(1)}, u32[]{:S(2)}, u32[]{:S(2)}) collective-permute-start(bf16[1024,128]{1,0:T(8,128)(2,1)S(1)} %bitcast.26), channel_id=1, source_target_pairs={{0,2},{1,3},{2,4},{3,5},{4,6},{5,7},{6,0},{7,1},{8,10},{9,11},{10,... | collective-permute-start | bytes 786440 | tf_op jit(solution)/shard_map/ppermute | solution.py:386
  74.4 12.9 %collective-permute-start.18 = (bf16[1024,128]{1,0:T(8,128)(2,1)S(1)}, bf16[1024,128]{1,0:T(8,128)(2,1)S(1)}, u32[]{:S(2)}, u32[]{:S(2)}) collective-permute-start(bf16[1024,128]{1,0:T(8,128)(2,1)S(1)} %bitcast.24), channel_id=1, source_target_pairs={{0,6},{1,7},{2,0},{3,1},{4,2},{5,3},{6,4},{7,5},{8,14},{9,15},{10,... | collective-permute-start | bytes 786440 | tf_op jit(solution)/shard_map/ppermute | solution.py:386
  76.6 13.2 %collective-permute-start.19 = (bf16[1024,128]{1,0:T(8,128)(2,1)S(1)}, bf16[1024,128]{1,0:T(8,128)(2,1)S(1)}, u32[]{:S(2)}, u32[]{:S(2)}) collective-permute-start(bf16[1024,128]{1,0:T(8,128)(2,1)S(1)} %bitcast.23), channel_id=1, source_target_pairs={{0,4},{1,5},{2,6},{3,7},{4,0},{5,1},{6,2},{7,3},{8,12},{9,13},{10,... | collective-permute-start | bytes 786440 | tf_op jit(solution)/shard_map/ppermute | solution.py:386
  78.0 16.3 %collective-permute-start.7 = (bf16[1024,128]{1,0:T(8,128)(2,1)S(1)}, bf16[1024,128]{1,0:T(8,128)(2,1)S(1)}, u32[]{:S(2)}, u32[]{:S(2)}) collective-permute-start(bf16[1024,128]{1,0:T(8,128)(2,1)S(1)} %bitcast.28), channel_id=1, source_target_pairs={{0,2},{1,3},{2,4},{3,5},{4,6},{5,7},{6,0},{7,1},{8,10},{9,11},{10,... | collective-permute-start | bytes 786440 | tf_op jit(solution)/shard_map/ppermute | solution.py:386
  78.9 15.5 %collective-permute-start.8 = (bf16[1024,128]{1,0:T(8,128)(2,1)S(1)}, bf16[1024,128]{1,0:T(8,128)(2,1)S(1)}, u32[]{:S(2)}, u32[]{:S(2)}) collective-permute-start(bf16[1024,128]{1,0:T(8,128)(2,1)S(1)} %bitcast.27), channel_id=1, source_target_pairs={{0,6},{1,7},{2,0},{3,1},{4,2},{5,3},{6,4},{7,5},{8,14},{9,15},{10,... | collective-permute-start | bytes 786440 | tf_op jit(solution)/shard_map/ppermute | solution.py:386
  83.2 17.9 %collective-permute-start.9 = (bf16[1024,128]{1,0:T(8,128)(2,1)S(1)}, bf16[1024,128]{1,0:T(8,128)(2,1)S(1)}, u32[]{:S(2)}, u32[]{:S(2)}) collective-permute-start(bf16[1024,128]{1,0:T(8,128)(2,1)S(1)} %bitcast.25), channel_id=1, source_target_pairs={{0,4},{1,5},{2,6},{3,7},{4,0},{5,1},{6,2},{7,3},{8,12},{9,13},{10,... | collective-permute-start | bytes 786440 | tf_op jit(solution)/shard_map/ppermute | solution.py:386
  103.0 1.8 %collective-permute-start.20 = (f32[192,128]{1,0:T(8,128)S(1)}, f32[192,128]{1,0:T(8,128)S(1)}, u32[]{:S(2)}, u32[]{:S(2)}) collective-permute-start(f32[192,128]{1,0:T(8,128)S(1)} %get-tuple-element.30), channel_id=1, source_target_pairs={{0,1},{1,0},{2,3},{3,2},{4,5},{5,4},{6,7},{7,6},{8,9},{9,8},{10,11... | collective-permute-start | bytes 294920 | tf_op jit(solution)/shard_map/ppermute | solution.py:374
  104.8 5.3 %collective-permute-start.21 = (f32[192,128]{1,0:T(8,128)S(1)}, f32[192,128]{1,0:T(8,128)S(1)}, u32[]{:S(2)}, u32[]{:S(2)}) collective-permute-start(f32[192,128]{1,0:T(8,128)S(1)} %add.71), channel_id=1, source_target_pairs={{0,4},{1,65},{2,6},{3,67},{4,0},{5,69},{6,2},{7,71},{8,12},{9,73},... | collective-permute-start | bytes 294920 | tf_op jit(solution)/shard_map/ppermute | solution.py:386
  105.4 5.9 %collective-permute-start.22 = (f32[192,128]{1,0:T(8,128)S(1)}, f32[192,128]{1,0:T(8,128)S(1)}, u32[]{:S(2)}, u32[]{:S(2)}) collective-permute-start(f32[192,128]{1,0:T(8,128)S(1)} %add.71), channel_id=1, source_target_pairs={{0,2},{1,33},{2,4},{3,35},{4,6},{5,37},{6,0},{7,39},{8,10},{9,41},... | collective-permute-start | bytes 294920 | tf_op jit(solution)/shard_map/ppermute | solution.py:386
  107.2 4.0 %collective-permute-start.23 = (f32[192,128]{1,0:T(8,128)S(1)}, f32[192,128]{1,0:T(8,128)S(1)}, u32[]{:S(2)}, u32[]{:S(2)}) collective-permute-start(f32[192,128]{1,0:T(8,128)S(1)} %add.71), channel_id=1, source_target_pairs={{0,6},{1,97},{2,0},{3,99},{4,2},{5,101},{6,4},{7,103},{8,14},{9,10... | collective-permute-start | bytes 294920 | tf_op jit(solution)/shard_map/ppermute | solution.py:386
  111.2 6.0 %collective-permute-start.24 = (f32[192,128]{1,0:T(8,128)S(1)}, f32[192,128]{1,0:T(8,128)S(1)}, u32[]{:S(2)}, u32[]{:S(2)}) collective-permute-start(f32[192,128]{1,0:T(8,128)S(1)} %add_add_fusion.2), channel_id=1, source_target_pairs={{0,64},{1,17},{2,66},{3,19},{4,68},{5,21},{6,70},{7,23},{8,72},{9,... | collective-permute-start | bytes 294920 | tf_op jit(solution)/shard_map/ppermute | solution.py:386
  114.6 4.8 %collective-permute-start.25 = (f32[192,128]{1,0:T(8,128)S(1)}, f32[192,128]{1,0:T(8,128)S(1)}, u32[]{:S(2)}, u32[]{:S(2)}) collective-permute-start(f32[192,128]{1,0:T(8,128)S(1)} %add_add_fusion.2), channel_id=1, source_target_pairs={{0,32},{1,9},{2,34},{3,11},{4,36},{5,13},{6,38},{7,15},{8,40},{9,1... | collective-permute-start | bytes 294920 | tf_op jit(solution)/shard_map/ppermute | solution.py:386
  114.6 4.8 %collective-permute-start.26 = (f32[192,128]{1,0:T(8,128)S(1)}, f32[192,128]{1,0:T(8,128)S(1)}, u32[]{:S(2)}, u32[]{:S(2)}) collective-permute-start(f32[192,128]{1,0:T(8,128)S(1)} %add_add_fusion.2), channel_id=1, source_target_pairs={{0,96},{1,25},{2,98},{3,27},{4,100},{5,29},{6,102},{7,31},{8,104},... | collective-permute-start | bytes 294920 | tf_op jit(solution)/shard_map/ppermute | solution.py:386
  119.5 5.1 %collective-permute-start.27 = (f32[192,128]{1,0:T(8,128)S(1)}, f32[192,128]{1,0:T(8,128)S(1)}, u32[]{:S(2)}, u32[]{:S(2)}) collective-permute-start(f32[192,128]{1,0:T(8,128)S(1)} %add_add_fusion.1), channel_id=1, source_target_pairs={{0,16},{1,5},{2,18},{3,7},{4,20},{5,1},{6,22},{7,3},{8,24},{9,13},... | collective-permute-start | bytes 294920 | tf_op jit(solution)/shard_map/ppermute | solution.py:386
  119.6 6.3 %collective-permute-start.28 = (f32[192,128]{1,0:T(8,128)S(1)}, f32[192,128]{1,0:T(8,128)S(1)}, u32[]{:S(2)}, u32[]{:S(2)}) collective-permute-start(f32[192,128]{1,0:T(8,128)S(1)} %add_add_fusion.1), channel_id=1, source_target_pairs={{0,8},{1,3},{2,10},{3,5},{4,12},{5,7},{6,14},{7,1},{8,16},{9,11},{... | collective-permute-start | bytes 294920 | tf_op jit(solution)/shard_map/ppermute | solution.py:386
  121.5 4.3 %collective-permute-start.29 = (f32[192,128]{1,0:T(8,128)S(1)}, f32[192,128]{1,0:T(8,128)S(1)}, u32[]{:S(2)}, u32[]{:S(2)}) collective-permute-start(f32[192,128]{1,0:T(8,128)S(1)} %add_add_fusion.1), channel_id=1, source_target_pairs={{0,24},{1,7},{2,26},{3,1},{4,28},{5,3},{6,30},{7,5},{8,0},{9,15},{... | collective-permute-start | bytes 294920 | tf_op jit(solution)/shard_map/ppermute | solution.py:386
  125.9 4.8 %collective-permute-start.30 = (f32[192,128]{1,0:T(8,128)S(1)}, f32[192,128]{1,0:T(8,128)S(1)}, u32[]{:S(2)}, u32[]{:S(2)}) collective-permute-start(f32[192,128]{1,0:T(8,128)S(1)} %add_add_fusion.mine_ref), channel_id=1, source_target_pairs={{0,1},{1,0},{2,3},{3,2},{4,5},{5,4},{6,7},{7,6},{8,9},{9,8},{10,11... | collective-permute-start | bytes 294920 | tf_op jit(solution)/shard_map/ppermute | solution.py:374

commit v4 on v3

--- a/solution.py
+++ b/solution.py
@@ -13,6 +13,7 @@
 META = 16
 SLOT_ROWS = CAP * BS + META
 CHUNKS = 2
+CARRIER = CHUNKS - 1
 PANEL = 32
 UNROLL = 4
 AHEAD = 3
@@ -110,10 +111,9 @@
     tails = [
         pltpu.make_async_copy(
             meta.at[pl.ds(d * SIDE, SIDE)],
-            outs[c * SIDE + d].at[:, pl.ds(CAP * BS, META), :],
-            meta_sems.at[c, d],
+            outs[CARRIER * SIDE + d].at[:, pl.ds(CAP * BS, META), :],
+            meta_sems.at[d],
         )
-        for c in range(CHUNKS)
         for d in range(SIDE)
     ]
     for tail in tails:
@@ -134,12 +134,16 @@
     width = omega.shape[1]
     slab = omega.reshape(-1, BS, width)
     indices = jnp.concatenate([col_target.T, route_dest.T, row_target[None, :]])
-    out = jax.ShapeDtypeStruct((SIDE, SLOT_ROWS, width // CHUNKS), BF16)
+    out_shape = [
+        jax.ShapeDtypeStruct((SIDE, SLOT_ROWS if c == CARRIER else CAP * BS, width // CHUNKS), BF16)
+        for c in range(CHUNKS)
+        for _ in range(SIDE)
+    ]
     outs = pl.pallas_call(
         partial_kernel,
         in_specs=[SCALARS] * 2 + [IN_HBM] * 2,
         out_specs=[pl.BlockSpec(memory_space=pl.ANY)] * (CHUNKS * SIDE),
-        out_shape=[out] * (CHUNKS * SIDE),
+        out_shape=out_shape,
         scratch_shapes=[
             pltpu.VMEM(a_blocks.shape, BF16),
             pltpu.VMEM(slab.shape, BF16),
@@ -150,7 +154,7 @@
             pltpu.SemaphoreType.DMA((targets // UNROLL,)),
             pltpu.SemaphoreType.DMA,
             pltpu.SemaphoreType.DMA((CHUNKS, targets)),
-            pltpu.SemaphoreType.DMA((CHUNKS, SIDE)),
+            pltpu.SemaphoreType.DMA((SIDE,)),
         ],
         compiler_params=pltpu.CompilerParams(vmem_limit_bytes=48 * MIB),
         name="partials",
@@ -158,11 +162,10 @@
     return [outs[c * SIDE : (c + 1) * SIDE] for c in range(CHUNKS)]
 
 
-def slot_sum_kernel(place_ref, *refs):
+def carrier_sum_kernel(place_ref, *refs):
     got, (send_ref, acc, ints, rows, sem) = refs[: 2 * SIDE - 1], refs[2 * SIDE - 1 :]
     z, core = place_ref[0], place_ref[1]
-    pieces = [(ref, 0) for ref in got[:SIDE]] + [(ref, i) for ref in got[SIDE:] for i in range(SIDE)]
-    for s, (ref, i) in enumerate(pieces):
+    for s, (ref, i) in enumerate(slots_of(got)):
         tile = ref[i, CAP * BS : SLOT_ROWS, 0:BS].astype(F32)
         row = tile[0:1, :].astype(jnp.int32)
         side = (row // RB_DEV) & 1
@@ -171,14 +174,26 @@
         ints[s : s + 1, :] = jnp.where(row < 0, row, place)
     copy = pltpu.make_async_copy(ints, rows, sem)
     copy.start()
-
+    copy.wait()
+    add_slots(rows, got, send_ref, acc)
+
+
+def slot_sum_kernel(rows, *refs):
+    got, (send_ref, acc) = refs[: 2 * SIDE - 1], refs[2 * SIDE - 1 :]
+    add_slots(rows, got, send_ref, acc)
+
+
+def slots_of(got):
+    return [(ref, 0) for ref in got[:SIDE]] + [(ref, i) for ref in got[SIDE:] for i in range(SIDE)]
+
+
+def add_slots(rows, got, send_ref, acc):
     def clear(b, carry):
         acc[b] = jnp.zeros(acc.shape[1:], F32)
         return carry
 
     lax.fori_loop(0, 2 * HALF, clear, 0, unroll=2)
-    copy.wait()
-    for s, (ref, i) in enumerate(pieces):
+    for s, (ref, i) in enumerate(slots_of(got)):
         for r in range(CAP):
             place = rows[s, r]
 
@@ -193,24 +208,24 @@
     lax.fori_loop(0, HALF, write, 0, unroll=2)
 
 
-def slot_sums(place, got):
+def slot_sums(place, got, rows):
     width = got[0].shape[2]
-    return pl.pallas_call(
-        slot_sum_kernel,
+    carrier = rows is None
+    out_shape = [
+        jax.ShapeDtypeStruct((HALF, BS, width), BF16),
+        jax.ShapeDtypeStruct((2 * HALF, BS, width), F32),
+        jax.ShapeDtypeStruct((OWNERS, BS), jnp.int32),
+    ]
+    outs = pl.pallas_call(
+        carrier_sum_kernel if carrier else slot_sum_kernel,
         in_specs=[SCALARS] + [WHOLE] * len(got),
-        out_specs=[WHOLE] * 2,
-        out_shape=[
-            jax.ShapeDtypeStruct((HALF, BS, width), BF16),
-            jax.ShapeDtypeStruct((2 * HALF, BS, width), F32),
-        ],
-        scratch_shapes=[
-            pltpu.VMEM((OWNERS, BS), jnp.int32),
-            pltpu.SMEM((OWNERS, BS), jnp.int32),
-            pltpu.SemaphoreType.DMA,
-        ],
+        out_specs=[WHOLE] * (3 if carrier else 2),
+        out_shape=out_shape if carrier else out_shape[:2],
+        scratch_shapes=[pltpu.SMEM((OWNERS, BS), jnp.int32), pltpu.SemaphoreType.DMA] if carrier else [],
         compiler_params=pltpu.CompilerParams(vmem_limit_bytes=22 * MIB),
-        name="slot_sums",
-    )(place, *got)
+        name="carrier_sums" if carrier else "slot_sums",
+    )(place if carrier else rows, *got)
+    return outs if carrier else [*outs, rows]
 
 
 def gram_kernel(place_ref, *refs):
@@ -409,23 +424,24 @@
     place = jnp.stack([col // 2, col % 2, row // SIDE, row % SIDE]).astype(jnp.int32)
     sends = partials(a_blocks, omega, route_dest, row_target, col_target, place)
     parts = []
-    for c, send in enumerate(sends):
+    rows = None
+    for send in sends[::-1]:
         near = [send[0]] + [ahead(send[d], (0, 1), d) for d in (1, 3, 2)]
         across = [jnp.stack([part[d] for part in near]) for d in (1, 3, 2)]
         far = [ahead(value, (1, 0), d) for d, value in zip((1, 3, 2), across)]
-        kept, leaving = core_sums(place, near + far)
-        parts = parts + kept + sent_along_z(leaving)
+        kept, leaving, rows = core_sums(place, near + far, rows)
+        parts = kept + sent_along_z(leaving) + parts
     sketch, gram_send, gram_keep = gram_halves(place, parts)
     gram = summed(gram_keep + other_core(gram_send))
     return tuple(factors(scale, place, gram, other_core(gram), sketch))
 
 
-def core_sums(place, got):
-    to_core, own = slot_sums(place, got)
+def core_sums(place, got, rows):
+    to_core, own, rows = slot_sums(place, got, rows)
     width = own.shape[-1]
     own, from_core = own.reshape(2 * SIDE, -1, width), other_core(to_core).reshape(SIDE, -1, width)
     leaving = [(own[d] + from_core[d].astype(F32)).astype(BF16) for d in (1, 3, 2)]
-    return [own[0], from_core[0]], leaving
+    return [own[0], from_core[0]], leaving, rows
 
 
 def sent_along_z(leaving):

time: 143 us -> 146 us (1.021)
  waiting for transfers between devices: 50.7 us -> 62.6 us
  starting transfers between devices: 59.1 us -> 49.8 us
    ppermute x27, waiting for transfers between devices: 48.8 us -> 60.8 us  [moved(): return lax.ppermute(value, ('row', 'col'), pairs)]
    ppermute x27, starting transfers between devices: 46.5 us -> 39.1 us  [moved(): return lax.ppermute(value, ('row', 'col'), pairs)]
    ppermute x4, starting transfers between devices: 12.6 us -> 10.7 us  [other_core(): return lax.ppermute(value, 'col', [(i, i ^ 1) for i in range(2 * SIDE)])]
  transfers between devices with their start and end apart: 31 -> 31, of which waited for: 19 -> 20; matrix products, arithmetic and copies ran while one was open for 1% -> 1% of each run, Pallas kernels for 3% -> 3%
where the time goes in v4:
time: 146 us
  waiting for transfers between devices  62.6 us (43%)
  starting transfers between devices  49.8 us (34%)
  Pallas kernels  30.2 us (21%)
  other arithmetic  1.85 us (1%)
    ppermute x27, waiting for transfers between devices, moved(): return lax.ppermute(value, ('row', 'col'), pairs)  60.8 us
    ppermute x27, starting transfers between devices, moved(): return lax.ppermute(value, ('row', 'col'), pairs)  39.1 us
    pallas_call x1, Pallas kernels, factors(): pl.pallas_call(functools.partial(factor_kernel, scale), in_specs=[SCALARS...  12.3 us
    pallas_call x1, Pallas kernels, partials(): pl.pallas_call(partial_kernel, in_specs=[SCALARS] * 2 + [IN_HBM] * 2, out...  11.7 us
    ppermute x4, starting transfers between devices, other_core(): return lax.ppermute(value, 'col', [(i, i ^ 1) for i in range(2 * SIDE)])  10.7 us
    pallas_call x2, Pallas kernels, slot_sums(): pl.pallas_call(carrier_sum_kernel if carrier else slot_sum_kernel, in_spe...  4.21 us
  transfers between devices with their start and end apart: 31, of which 20 were waited for; matrix products, arithmetic and copies ran while one was open for 1% of the time, Pallas kernels for 3%

profile of v4, /device:TPU:1, one launch (start us, length us, event | category | flops | bytes accessed | tf_op | source)
XLA Modules:
  0.0 145.6 jit_solution(13263625830509023466)
XLA Ops:
  1.5 11.7 %partials.1 = (bf16[4,512,128]{2,1,0:T(8,128)(2,1)S(1)}, bf16[4,512,128]{2,1,0:T(8,128)(2,1)S(1)}, bf16[4,512,128]{2,1,0:T(8,128)(2,1)S(1)}, bf16[4,512,128]{2,1...) custom-call(s32[18,32]{1,0:T(8,128)S(1)} %pad_add_fusion.index_ref, ...), custom_call_target="tpu_custom_call" | custom-call | tf_op jit(solution)/shard_map/partials/pallas_call | solution.py:142
  13.2 2.1 %collective-permute-start.6 = (bf16[4,512,128]{2,1,0:T(8,128)(2,1)S(1)}, bf16[4,512,128]{2,1,0:T(8,128)(2,1)S(1)}, u32[]{:S(2)}, u32[]{:S(2)}) collective-permute-start(bf16[4,512,128]{2,1,0:T(8,128)(2,1)S(1)} %get-tuple-element.24), channel_id=1, source_target_pairs={{0,32},{1,9},{2,34},{3,11},{4,36},{5,13},{6,38},{7,15},{8,40},{9,1... | collective-permute-start | bytes 1572872 | tf_op jit(solution)/shard_map/ppermute | solution.py:401
  15.3 1.2 collective-permute-start
  16.5 1.5 %collective-permute-start.1 = (bf16[4,528,128]{2,1,0:T(8,128)(2,1)S(1)}, bf16[4,528,128]{2,1,0:T(8,128)(2,1)S(1)}, u32[]{:S(2)}, u32[]{:S(2)}) collective-permute-start(bf16[4,528,128]{2,1,0:T(8,128)(2,1)S(1)} %get-tuple-element.20), channel_id=1, source_target_pairs={{0,96},{1,25},{2,98},{3,27},{4,100},{5,29},{6,102},{7,31},{8,104},... | collective-permute-start | bytes 1622024 | tf_op jit(solution)/shard_map/ppermute | solution.py:401
  18.1 1.6 %collective-permute-start.8 = (bf16[4,512,128]{2,1,0:T(8,128)(2,1)S(1)}, bf16[4,512,128]{2,1,0:T(8,128)(2,1)S(1)}, u32[]{:S(2)}, u32[]{:S(2)}) collective-permute-start(bf16[4,512,128]{2,1,0:T(8,128)(2,1)S(1)} %get-tuple-element.26), channel_id=1, source_target_pairs={{0,64},{1,17},{2,66},{3,19},{4,68},{5,21},{6,70},{7,23},{8,72},{9,... | collective-permute-start | bytes 1572872 | tf_op jit(solution)/shard_map/ppermute | solution.py:401
  19.8 3.6 %collective-permute-done.6.refs_1_ = bf16[4,512,128]{2,1,0:T(8,128)(2,1)S(1)} collective-permute-done((bf16[4,512,128]{2,1,0:T(8,128)(2,1)S(1)}, bf16[4,512,128]{2,1,0:T(8,128)(2,1)S(1)}, u32[]{:S(2)}, u32[]{:S(2)}) %collective-permute-start.6) | collective-permute-done | bytes 524320 | tf_op jit(solution)/shard_map/ppermute | solution.py:401
  23.5 1.7 %collective-permute-start.2 = (bf16[4,528,128]{2,1,0:T(8,128)(2,1)S(1)}, bf16[4,528,128]{2,1,0:T(8,128)(2,1)S(1)}, u32[]{:S(2)}, u32[]{:S(2)}) collective-permute-start(bf16[4,528,128]{2,1,0:T(8,128)(2,1)S(1)} %get-tuple-element.21), channel_id=1, source_target_pairs={{0,64},{1,17},{2,66},{3,19},{4,68},{5,21},{6,70},{7,23},{8,72},{9,... | collective-permute-start | bytes 1622024 | tf_op jit(solution)/shard_map/ppermute | solution.py:401
  25.2 5.4 %collective-permute-done.7.refs_2_ = bf16[4,512,128]{2,1,0:T(8,128)(2,1)S(1)} collective-permute-done((bf16[4,512,128]{2,1,0:T(8,128)(2,1)S(1)}, bf16[4,512,128]{2,1,0:T(8,128)(2,1)S(1)}, u32[]{:S(2)}, u32[]{:S(2)}) %collective-permute-start.7) | collective-permute-done | bytes 524320 | tf_op jit(solution)/shard_map/ppermute | solution.py:401
  30.7 5.4 %collective-permute-done.8.refs_3_ = bf16[4,512,128]{2,1,0:T(8,128)(2,1)S(1)} collective-permute-done((bf16[4,512,128]{2,1,0:T(8,128)(2,1)S(1)}, bf16[4,512,128]{2,1,0:T(8,128)(2,1)S(1)}, u32[]{:S(2)}, u32[]{:S(2)}) %collective-permute-start.8) | collective-permute-done | bytes 524320 | tf_op jit(solution)/shard_map/ppermute | solution.py:401
  36.2 5.7 %collective-permute-done.2.refs_3_ = bf16[4,528,128]{2,1,0:T(8,128)(2,1)S(1)} collective-permute-done((bf16[4,528,128]{2,1,0:T(8,128)(2,1)S(1)}, bf16[4,528,128]{2,1,0:T(8,128)(2,1)S(1)}, u32[]{:S(2)}, u32[]{:S(2)}) %collective-permute-start.2) | collective-permute-done | bytes 540704 | tf_op jit(solution)/shard_map/ppermute | solution.py:401
  41.9 2.7 %collective-permute-start.5 = (bf16[4,528,128]{2,1,0:T(8,128)(2,1)S(1)}, bf16[4,528,128]{2,1,0:T(8,128)(2,1)S(1)}, u32[]{:S(2)}, u32[]{:S(2)}) collective-permute-start(bf16[4,528,128]{2,1,0:T(8,128)(2,1)S(1)} %pad_maximum_fusion.2), channel_id=1, source_target_pairs={{0,16},{1,65},{2,18},{3,67},{4,20},{5,69},{6,22},{7,71},{8,24},{9,... | collective-permute-start | bytes 1622024 | tf_op jit(solution)/shard_map/ppermute | solution.py:401
  44.7 0.8 collective-permute-start.4
  46.5 1.1 collective-permute-start.11
  47.6 2.1 %collective-permute-start.10 = (bf16[4,512,128]{2,1,0:T(8,128)(2,1)S(1)}, bf16[4,512,128]{2,1,0:T(8,128)(2,1)S(1)}, u32[]{:S(2)}, u32[]{:S(2)}) collective-permute-start(bf16[4,512,128]{2,1,0:T(8,128)(2,1)S(1)} %pad_maximum_fusion.4), channel_id=1, source_target_pairs={{0,24},{1,97},{2,26},{3,99},{4,28},{5,101},{6,30},{7,103},{8,0},{9... | collective-permute-start | bytes 1572872 | tf_op jit(solution)/shard_map/ppermute | solution.py:401
  49.8 2.2 %collective-permute-done.5.refs_6_ = bf16[4,528,128]{2,1,0:T(8,128)(2,1)S(1)} collective-permute-done((bf16[4,528,128]{2,1,0:T(8,128)(2,1)S(1)}, bf16[4,528,128]{2,1,0:T(8,128)(2,1)S(1)}, u32[]{:S(2)}, u32[]{:S(2)}) %collective-permute-start.5) | collective-permute-done | bytes 540704 | tf_op jit(solution)/shard_map/ppermute | solution.py:401
  52.1 1.0 collective-permute-start.9
  53.1 5.1 %collective-permute-done.4.refs_5_ = bf16[4,528,128]{2,1,0:T(8,128)(2,1)S(1)} collective-permute-done((bf16[4,528,128]{2,1,0:T(8,128)(2,1)S(1)}, bf16[4,528,128]{2,1,0:T(8,128)(2,1)S(1)}, u32[]{:S(2)}, u32[]{:S(2)}) %collective-permute-start.4) | collective-permute-done | bytes 540704 | tf_op jit(solution)/shard_map/ppermute | solution.py:401
  58.2 2.4 %carrier_sums.1 = (bf16[32,128,128]{2,1,0:T(8,128)(2,1)S(1)}, f32[64,128,128]{2,1,0:T(8,128)S(1)}, s32[16,128]{1,0:T(8,128)S(1)}) custom-call(s32[4]{0:T(128)S(1)} %pad_add_fusion.1.place_ref, bf16[4,528,128]{2,1,0:T(8,128)(2,1)S(1)} %get-tuple-element.18.refs_0_, bf16[4,528,128]{2,1,0:T(8,128)(2,1)S(1)} %collective-permute-done.refs_1_, ...), custom_call_target="tpu_custom_call" | custom-call | tf_op jit(solution)/shard_map/carrier_sums/pallas_call | solution.py:219
  60.6 2.5 %collective-permute-start.16 = (bf16[32,128,128]{2,1,0:T(8,128)(2,1)S(1)}, bf16[32,128,128]{2,1,0:T(8,128)(2,1)S(1)}, u32[]{:S(2)}, u32[]{:S(2)}) collective-permute-start(bf16[32,128,128]{2,1,0:T(8,128)(2,1)S(1)} %get-tuple-element.30), channel_id=1, source_target_pairs={{0,1},{1,0},{2,3},{3,2},{4,5},{5,4},{6,7},{7,6},{8,9},{9,8},{10,11... | collective-permute-start | bytes 3145736 | tf_op jit(solution)/shard_map/ppermute | solution.py:389
  63.5 6.0 %collective-permute-done.10.refs_5_ = bf16[4,512,128]{2,1,0:T(8,128)(2,1)S(1)} collective-permute-done((bf16[4,512,128]{2,1,0:T(8,128)(2,1)S(1)}, bf16[4,512,128]{2,1,0:T(8,128)(2,1)S(1)}, u32[]{:S(2)}, u32[]{:S(2)}) %collective-permute-start.10) | collective-permute-done | bytes 524320 | tf_op jit(solution)/shard_map/ppermute | solution.py:401
  69.5 1.8 %slot_sums.1 = (bf16[32,128,128]{2,1,0:T(8,128)(2,1)S(1)}, f32[64,128,128]{2,1,0:T(8,128)S(1)}) custom-call(s32[16,128]{1,0:T(8,128)S(1)} %get-tuple-element.22.rows, bf16[4,512,128]{2,1,0:T(8,128)(2,1)S(1)} %get-tuple-element.23.refs_0_, bf16[4,512,128]{2,1,0:T(8,128)(2,1)S(1)} %collective-permute-done.6.refs_1_, ...), custom_call_target="tpu_custom_call" | custom-call | tf_op jit(solution)/shard_map/slot_sums/pallas_call | solution.py:219
  71.3 2.5 %collective-permute-start.12 = (bf16[32,128,128]{2,1,0:T(8,128)(2,1)S(1)}, bf16[32,128,128]{2,1,0:T(8,128)(2,1)S(1)}, u32[]{:S(2)}, u32[]{:S(2)}) collective-permute-start(bf16[32,128,128]{2,1,0:T(8,128)(2,1)S(1)} %get-tuple-element.28), channel_id=1, source_target_pairs={{0,1},{1,0},{2,3},{3,2},{4,5},{5,4},{6,7},{7,6},{8,9},{9,8},{10,11... | collective-permute-start | bytes 3145736 | tf_op jit(solution)/shard_map/ppermute | solution.py:389
  74.0 1.7 %collective-permute-start.17 = (bf16[1024,128]{1,0:T(8,128)(2,1)S(1)}, bf16[1024,128]{1,0:T(8,128)(2,1)S(1)}, u32[]{:S(2)}, u32[]{:S(2)}) collective-permute-start(bf16[1024,128]{1,0:T(8,128)(2,1)S(1)} %bitcast.26), channel_id=1, source_target_pairs={{0,2},{1,3},{2,4},{3,5},{4,6},{5,7},{6,0},{7,1},{8,10},{9,11},{10,... | collective-permute-start | bytes 786440 | tf_op jit(solution)/shard_map/ppermute | solution.py:401
  75.7 2.2 %collective-permute-start.18 = (bf16[1024,128]{1,0:T(8,128)(2,1)S(1)}, bf16[1024,128]{1,0:T(8,128)(2,1)S(1)}, u32[]{:S(2)}, u32[]{:S(2)}) collective-permute-start(bf16[1024,128]{1,0:T(8,128)(2,1)S(1)} %bitcast.24), channel_id=1, source_target_pairs={{0,6},{1,7},{2,0},{3,1},{4,2},{5,3},{6,4},{7,5},{8,14},{9,15},{10,... | collective-permute-start | bytes 786440 | tf_op jit(solution)/shard_map/ppermute | solution.py:401
  78.0 1.2 collective-permute-start.19
  80.3 1.9 %collective-permute-start.14 = (bf16[1024,128]{1,0:T(8,128)(2,1)S(1)}, bf16[1024,128]{1,0:T(8,128)(2,1)S(1)}, u32[]{:S(2)}, u32[]{:S(2)}) collective-permute-start(bf16[1024,128]{1,0:T(8,128)(2,1)S(1)} %bitcast.27), channel_id=1, source_target_pairs={{0,6},{1,7},{2,0},{3,1},{4,2},{5,3},{6,4},{7,5},{8,14},{9,15},{10,... | collective-permute-start | bytes 786440 | tf_op jit(solution)/shard_map/ppermute | solution.py:401
  82.2 2.3 %collective-permute-done.17.refs_7_ = bf16[1024,128]{1,0:T(8,128)(2,1)S(1)} collective-permute-done((bf16[1024,128]{1,0:T(8,128)(2,1)S(1)}, bf16[1024,128]{1,0:T(8,128)(2,1)S(1)}, u32[]{:S(2)}, u32[]{:S(2)}) %collective-permute-start.17) | collective-permute-done | bytes 262176 | tf_op jit(solution)/shard_map/ppermute | solution.py:401
  84.5 1.5 %collective-permute-start.15 = (bf16[1024,128]{1,0:T(8,128)(2,1)S(1)}, bf16[1024,128]{1,0:T(8,128)(2,1)S(1)}, u32[]{:S(2)}, u32[]{:S(2)}) collective-permute-start(bf16[1024,128]{1,0:T(8,128)(2,1)S(1)} %bitcast.25), channel_id=1, source_target_pairs={{0,4},{1,5},{2,6},{3,7},{4,0},{5,1},{6,2},{7,3},{8,12},{9,13},{10,... | collective-permute-start | bytes 786440 | tf_op jit(solution)/shard_map/ppermute | solution.py:401
  86.1 5.1 %collective-permute-done.19.refs_9_ = bf16[1024,128]{1,0:T(8,128)(2,1)S(1)} collective-permute-done((bf16[1024,128]{1,0:T(8,128)(2,1)S(1)}, bf16[1024,128]{1,0:T(8,128)(2,1)S(1)}, u32[]{:S(2)}, u32[]{:S(2)}) %collective-permute-start.19) | collective-permute-done | bytes 262176 | tf_op jit(solution)/shard_map/ppermute | solution.py:401
  91.2 4.6 %collective-permute-done.13.refs_2_ = bf16[1024,128]{1,0:T(8,128)(2,1)S(1)} collective-permute-done((bf16[1024,128]{1,0:T(8,128)(2,1)S(1)}, bf16[1024,128]{1,0:T(8,128)(2,1)S(1)}, u32[]{:S(2)}, u32[]{:S(2)}) %collective-permute-start.13) | collective-permute-done | bytes 262176 | tf_op jit(solution)/shard_map/ppermute | solution.py:401
  95.8 6.6 %collective-permute-done.15.refs_4_ = bf16[1024,128]{1,0:T(8,128)(2,1)S(1)} collective-permute-done((bf16[1024,128]{1,0:T(8,128)(2,1)S(1)}, bf16[1024,128]{1,0:T(8,128)(2,1)S(1)}, u32[]{:S(2)}, u32[]{:S(2)}) %collective-permute-start.15) | collective-permute-done | bytes 262176 | tf_op jit(solution)/shard_map/ppermute | solution.py:401
  102.4 2.0 %sum_gram.1 = (f32[1024,256]{1,0:T(8,128)S(1)}, f32[192,128]{1,0:T(8,128)S(1)}, f32[192,128]{1,0:T(8,128)S(1)}) custom-call(s32[4]{0:T(128)S(1)} %pad_add_fusion.1.place_ref, f32[1024,128]{1,0:T(8,128)S(1)} %bitcast.19, bf16[1024,128]{1,0:T(8,128)(2,1)S(1)} %bitcast.20, bf16[1024,128]{1,0:T(8,128)(2,1)S(1)} %collective-permute-done.13.refs_2_, ...), custom_call_target="tpu_custom_call" | custom-call | tf_op jit(solution)/shard_map/sum_gram/pallas_call | solution.py:255
  104.4 1.1 collective-permute-start.20
  105.4 0.9 collective-permute-done.20
  106.4 1.6 %collective-permute-start.21 = (f32[192,128]{1,0:T(8,128)S(1)}, f32[192,128]{1,0:T(8,128)S(1)}, u32[]{:S(2)}, u32[]{:S(2)}) collective-permute-start(f32[192,128]{1,0:T(8,128)S(1)} %add.71), channel_id=1, source_target_pairs={{0,4},{1,65},{2,6},{3,67},{4,0},{5,69},{6,2},{7,71},{8,12},{9,73},... | collective-permute-start | bytes 294920 | tf_op jit(solution)/shard_map/ppermute | solution.py:401
  108.0 2.5 %collective-permute-start.22 = (f32[192,128]{1,0:T(8,128)S(1)}, f32[192,128]{1,0:T(8,128)S(1)}, u32[]{:S(2)}, u32[]{:S(2)}) collective-permute-start(f32[192,128]{1,0:T(8,128)S(1)} %add.71), channel_id=1, source_target_pairs={{0,2},{1,33},{2,4},{3,35},{4,6},{5,37},{6,0},{7,39},{8,10},{9,41},... | collective-permute-start | bytes 294920 | tf_op jit(solution)/shard_map/ppermute | solution.py:401
  110.8 1.0 collective-permute-done.21
  111.7 1.3 collective-permute-done.22
  113.1 0.9 collective-permute-done.23
  114.0 2.7 %collective-permute-start.24 = (f32[192,128]{1,0:T(8,128)S(1)}, f32[192,128]{1,0:T(8,128)S(1)}, u32[]{:S(2)}, u32[]{:S(2)}) collective-permute-start(f32[192,128]{1,0:T(8,128)S(1)} %add_add_fusion.2), channel_id=1, source_target_pairs={{0,64},{1,17},{2,66},{3,19},{4,68},{5,21},{6,70},{7,23},{8,72},{9,... | collective-permute-start | bytes 294920 | tf_op jit(solution)/shard_map/ppermute | solution.py:401
  117.0 2.4 %collective-permute-start.26 = (f32[192,128]{1,0:T(8,128)S(1)}, f32[192,128]{1,0:T(8,128)S(1)}, u32[]{:S(2)}, u32[]{:S(2)}) collective-permute-start(f32[192,128]{1,0:T(8,128)S(1)} %add_add_fusion.2), channel_id=1, source_target_pairs={{0,96},{1,25},{2,98},{3,27},{4,100},{5,29},{6,102},{7,31},{8,104},... | collective-permute-start | bytes 294920 | tf_op jit(solution)/shard_map/ppermute | solution.py:401
  119.4 2.2 %collective-permute-done.25 = f32[192,128]{1,0:T(8,128)S(1)} collective-permute-done((f32[192,128]{1,0:T(8,128)S(1)}, f32[192,128]{1,0:T(8,128)S(1)}, u32[]{:S(2)}, u32[]{:S(2)}) %collective-permute-start.25) | collective-permute-done | bytes 98336 | tf_op jit(solution)/shard_map/ppermute | solution.py:401
  122.0 2.1 %collective-permute-start.28 = (f32[192,128]{1,0:T(8,128)S(1)}, f32[192,128]{1,0:T(8,128)S(1)}, u32[]{:S(2)}, u32[]{:S(2)}) collective-permute-start(f32[192,128]{1,0:T(8,128)S(1)} %add_add_fusion.1), channel_id=1, source_target_pairs={{0,8},{1,3},{2,10},{3,5},{4,12},{5,7},{6,14},{7,1},{8,16},{9,11},{... | collective-permute-start | bytes 294920 | tf_op jit(solution)/shard_map/ppermute | solution.py:401
  124.8 1.9 %collective-permute-done.27 = f32[192,128]{1,0:T(8,128)S(1)} collective-permute-done((f32[192,128]{1,0:T(8,128)S(1)}, f32[192,128]{1,0:T(8,128)S(1)}, u32[]{:S(2)}, u32[]{:S(2)}) %collective-permute-start.27) | collective-permute-done | bytes 98336 | tf_op jit(solution)/shard_map/ppermute | solution.py:401
  126.7 1.0 collective-permute-done.28
  127.7 4.7 %collective-permute-start.30 = (f32[192,128]{1,0:T(8,128)S(1)}, f32[192,128]{1,0:T(8,128)S(1)}, u32[]{:S(2)}, u32[]{:S(2)}) collective-permute-start(f32[192,128]{1,0:T(8,128)S(1)} %add_add_fusion.mine_ref), channel_id=1, source_target_pairs={{0,1},{1,0},{2,3},{3,2},{4,5},{5,4},{6,7},{7,6},{8,9},{9,8},{10,11... | collective-permute-start | bytes 294920 | tf_op jit(solution)/shard_map/ppermute | solution.py:389
  132.3 0.9 collective-permute-done.30.other_ref
  133.3 12.3 %factor_basis.1 = (f32[1024,256]{1,0:T(8,128)}, f32[256,256]{1,0:T(8,128)}) custom-call(s32[4]{0:T(128)S(1)} %pad_add_fusion.1.place_ref, f32[192,128]{1,0:T(8,128)S(1)} %add_add_fusion.mine_ref, f32[192,128]{1,0:T(8,128)S(1)} %collective-permute-done.30.other_ref, f32[1024,256]{1,0:T(8,128)S(1)} %get-tuple-element.33.sketch_ref), custom_call_target="tpu_custom_call" | custom-call | tf_op jit(solution)/shard_map/factor_basis/pallas_call | solution.py:374
  (43 shorter events, 6.0 us)
Async XLA Ops:
  13.2 10.2 %collective-permute-start.6 = (bf16[4,512,128]{2,1,0:T(8,128)(2,1)S(1)}, bf16[4,512,128]{2,1,0:T(8,128)(2,1)S(1)}, u32[]{:S(2)}, u32[]{:S(2)}) collective-permute-start(bf16[4,512,128]{2,1,0:T(8,128)(2,1)S(1)} %get-tuple-element.24), channel_id=1, source_target_pairs={{0,32},{1,9},{2,34},{3,11},{4,36},{5,13},{6,38},{7,15},{8,40},{9,1... | collective-permute-start | bytes 1572872 | tf_op jit(solution)/shard_map/ppermute | solution.py:401
  15.3 20.7 %collective-permute-start = (bf16[4,528,128]{2,1,0:T(8,128)(2,1)S(1)}, bf16[4,528,128]{2,1,0:T(8,128)(2,1)S(1)}, u32[]{:S(2)}, u32[]{:S(2)}) collective-permute-start(bf16[4,528,128]{2,1,0:T(8,128)(2,1)S(1)} %get-tuple-element.19), channel_id=1, source_target_pairs={{0,32},{1,9},{2,34},{3,11},{4,36},{5,13},{6,38},{7,15},{8,40},{9,1... | collective-permute-start | bytes 1622024 | tf_op jit(solution)/shard_map/ppermute | solution.py:401
  16.5 19.6 %collective-permute-start.1 = (bf16[4,528,128]{2,1,0:T(8,128)(2,1)S(1)}, bf16[4,528,128]{2,1,0:T(8,128)(2,1)S(1)}, u32[]{:S(2)}, u32[]{:S(2)}) collective-permute-start(bf16[4,528,128]{2,1,0:T(8,128)(2,1)S(1)} %get-tuple-element.20), channel_id=1, source_target_pairs={{0,96},{1,25},{2,98},{3,27},{4,100},{5,29},{6,102},{7,31},{8,104},... | collective-permute-start | bytes 1622024 | tf_op jit(solution)/shard_map/ppermute | solution.py:401
  18.0 12.6 %collective-permute-start.7 = (bf16[4,512,128]{2,1,0:T(8,128)(2,1)S(1)}, bf16[4,512,128]{2,1,0:T(8,128)(2,1)S(1)}, u32[]{:S(2)}, u32[]{:S(2)}) collective-permute-start(bf16[4,512,128]{2,1,0:T(8,128)(2,1)S(1)} %get-tuple-element.25), channel_id=1, source_target_pairs={{0,96},{1,25},{2,98},{3,27},{4,100},{5,29},{6,102},{7,31},{8,104},... | collective-permute-start | bytes 1572872 | tf_op jit(solution)/shard_map/ppermute | solution.py:401
  18.1 17.9 %collective-permute-start.8 = (bf16[4,512,128]{2,1,0:T(8,128)(2,1)S(1)}, bf16[4,512,128]{2,1,0:T(8,128)(2,1)S(1)}, u32[]{:S(2)}, u32[]{:S(2)}) collective-permute-start(bf16[4,512,128]{2,1,0:T(8,128)(2,1)S(1)} %get-tuple-element.26), channel_id=1, source_target_pairs={{0,64},{1,17},{2,66},{3,19},{4,68},{5,21},{6,70},{7,23},{8,72},{9,... | collective-permute-start | bytes 1572872 | tf_op jit(solution)/shard_map/ppermute | solution.py:401
  23.5 18.4 %collective-permute-start.2 = (bf16[4,528,128]{2,1,0:T(8,128)(2,1)S(1)}, bf16[4,528,128]{2,1,0:T(8,128)(2,1)S(1)}, u32[]{:S(2)}, u32[]{:S(2)}) collective-permute-start(bf16[4,528,128]{2,1,0:T(8,128)(2,1)S(1)} %get-tuple-element.21), channel_id=1, source_target_pairs={{0,64},{1,17},{2,66},{3,19},{4,68},{5,21},{6,70},{7,23},{8,72},{9,... | collective-permute-start | bytes 1622024 | tf_op jit(solution)/shard_map/ppermute | solution.py:401
  41.9 10.1 %collective-permute-start.5 = (bf16[4,528,128]{2,1,0:T(8,128)(2,1)S(1)}, bf16[4,528,128]{2,1,0:T(8,128)(2,1)S(1)}, u32[]{:S(2)}, u32[]{:S(2)}) collective-permute-start(bf16[4,528,128]{2,1,0:T(8,128)(2,1)S(1)} %pad_maximum_fusion.2), channel_id=1, source_target_pairs={{0,16},{1,65},{2,18},{3,67},{4,20},{5,69},{6,22},{7,71},{8,24},{9,... | collective-permute-start | bytes 1622024 | tf_op jit(solution)/shard_map/ppermute | solution.py:401
  44.7 13.5 %collective-permute-start.4 = (bf16[4,528,128]{2,1,0:T(8,128)(2,1)S(1)}, bf16[4,528,128]{2,1,0:T(8,128)(2,1)S(1)}, u32[]{:S(2)}, u32[]{:S(2)}) collective-permute-start(bf16[4,528,128]{2,1,0:T(8,128)(2,1)S(1)} %pad_maximum_fusion.1), channel_id=1, source_target_pairs={{0,24},{1,97},{2,26},{3,99},{4,28},{5,101},{6,30},{7,103},{8,0},{9... | collective-permute-start | bytes 1622024 | tf_op jit(solution)/shard_map/ppermute | solution.py:401
  45.6 12.6 %collective-permute-start.3 = (bf16[4,528,128]{2,1,0:T(8,128)(2,1)S(1)}, bf16[4,528,128]{2,1,0:T(8,128)(2,1)S(1)}, u32[]{:S(2)}, u32[]{:S(2)}) collective-permute-start(bf16[4,528,128]{2,1,0:T(8,128)(2,1)S(1)} %pad_maximum_fusion), channel_id=1, source_target_pairs={{0,8},{1,33},{2,10},{3,35},{4,12},{5,37},{6,14},{7,39},{8,16},{9,4... | collective-permute-start | bytes 1622024 | tf_op jit(solution)/shard_map/ppermute | solution.py:401
  46.5 17.1 %collective-permute-start.11 = (bf16[4,512,128]{2,1,0:T(8,128)(2,1)S(1)}, bf16[4,512,128]{2,1,0:T(8,128)(2,1)S(1)}, u32[]{:S(2)}, u32[]{:S(2)}) collective-permute-start(bf16[4,512,128]{2,1,0:T(8,128)(2,1)S(1)} %pad_maximum_fusion.5), channel_id=1, source_target_pairs={{0,16},{1,65},{2,18},{3,67},{4,20},{5,69},{6,22},{7,71},{8,24},{9,... | collective-permute-start | bytes 1572872 | tf_op jit(solution)/shard_map/ppermute | solution.py:401
  47.6 21.8 %collective-permute-start.10 = (bf16[4,512,128]{2,1,0:T(8,128)(2,1)S(1)}, bf16[4,512,128]{2,1,0:T(8,128)(2,1)S(1)}, u32[]{:S(2)}, u32[]{:S(2)}) collective-permute-start(bf16[4,512,128]{2,1,0:T(8,128)(2,1)S(1)} %pad_maximum_fusion.4), channel_id=1, source_target_pairs={{0,24},{1,97},{2,26},{3,99},{4,28},{5,101},{6,30},{7,103},{8,0},{9... | collective-permute-start | bytes 1572872 | tf_op jit(solution)/shard_map/ppermute | solution.py:401
  52.1 17.4 %collective-permute-start.9 = (bf16[4,512,128]{2,1,0:T(8,128)(2,1)S(1)}, bf16[4,512,128]{2,1,0:T(8,128)(2,1)S(1)}, u32[]{:S(2)}, u32[]{:S(2)}) collective-permute-start(bf16[4,512,128]{2,1,0:T(8,128)(2,1)S(1)} %pad_maximum_fusion.3), channel_id=1, source_target_pairs={{0,8},{1,33},{2,10},{3,35},{4,12},{5,37},{6,14},{7,39},{8,16},{9,4... | collective-permute-start | bytes 1572872 | tf_op jit(solution)/shard_map/ppermute | solution.py:401
  60.6 13.1 %collective-permute-start.16 = (bf16[32,128,128]{2,1,0:T(8,128)(2,1)S(1)}, bf16[32,128,128]{2,1,0:T(8,128)(2,1)S(1)}, u32[]{:S(2)}, u32[]{:S(2)}) collective-permute-start(bf16[32,128,128]{2,1,0:T(8,128)(2,1)S(1)} %get-tuple-element.30), channel_id=1, source_target_pairs={{0,1},{1,0},{2,3},{3,2},{4,5},{5,4},{6,7},{7,6},{8,9},{9,8},{10,11... | collective-permute-start | bytes 3145736 | tf_op jit(solution)/shard_map/ppermute | solution.py:389
  71.3 7.9 %collective-permute-start.12 = (bf16[32,128,128]{2,1,0:T(8,128)(2,1)S(1)}, bf16[32,128,128]{2,1,0:T(8,128)(2,1)S(1)}, u32[]{:S(2)}, u32[]{:S(2)}) collective-permute-start(bf16[32,128,128]{2,1,0:T(8,128)(2,1)S(1)} %get-tuple-element.28), channel_id=1, source_target_pairs={{0,1},{1,0},{2,3},{3,2},{4,5},{5,4},{6,7},{7,6},{8,9},{9,8},{10,11... | collective-permute-start | bytes 3145736 | tf_op jit(solution)/shard_map/ppermute | solution.py:389
  74.0 10.5 %collective-permute-start.17 = (bf16[1024,128]{1,0:T(8,128)(2,1)S(1)}, bf16[1024,128]{1,0:T(8,128)(2,1)S(1)}, u32[]{:S(2)}, u32[]{:S(2)}) collective-permute-start(bf16[1024,128]{1,0:T(8,128)(2,1)S(1)} %bitcast.26), channel_id=1, source_target_pairs={{0,2},{1,3},{2,4},{3,5},{4,6},{5,7},{6,0},{7,1},{8,10},{9,11},{10,... | collective-permute-start | bytes 786440 | tf_op jit(solution)/shard_map/ppermute | solution.py:401
  75.7 10.3 %collective-permute-start.18 = (bf16[1024,128]{1,0:T(8,128)(2,1)S(1)}, bf16[1024,128]{1,0:T(8,128)(2,1)S(1)}, u32[]{:S(2)}, u32[]{:S(2)}) collective-permute-start(bf16[1024,128]{1,0:T(8,128)(2,1)S(1)} %bitcast.24), channel_id=1, source_target_pairs={{0,6},{1,7},{2,0},{3,1},{4,2},{5,3},{6,4},{7,5},{8,14},{9,15},{10,... | collective-permute-start | bytes 786440 | tf_op jit(solution)/shard_map/ppermute | solution.py:401
  78.0 13.2 %collective-permute-start.19 = (bf16[1024,128]{1,0:T(8,128)(2,1)S(1)}, bf16[1024,128]{1,0:T(8,128)(2,1)S(1)}, u32[]{:S(2)}, u32[]{:S(2)}) collective-permute-start(bf16[1024,128]{1,0:T(8,128)(2,1)S(1)} %bitcast.23), channel_id=1, source_target_pairs={{0,4},{1,5},{2,6},{3,7},{4,0},{5,1},{6,2},{7,3},{8,12},{9,13},{10,... | collective-permute-start | bytes 786440 | tf_op jit(solution)/shard_map/ppermute | solution.py:401
  79.5 16.3 %collective-permute-start.13 = (bf16[1024,128]{1,0:T(8,128)(2,1)S(1)}, bf16[1024,128]{1,0:T(8,128)(2,1)S(1)}, u32[]{:S(2)}, u32[]{:S(2)}) collective-permute-start(bf16[1024,128]{1,0:T(8,128)(2,1)S(1)} %bitcast.28), channel_id=1, source_target_pairs={{0,2},{1,3},{2,4},{3,5},{4,6},{5,7},{6,0},{7,1},{8,10},{9,11},{10,... | collective-permute-start | bytes 786440 | tf_op jit(solution)/shard_map/ppermute | solution.py:401
  80.3 15.5 %collective-permute-start.14 = (bf16[1024,128]{1,0:T(8,128)(2,1)S(1)}, bf16[1024,128]{1,0:T(8,128)(2,1)S(1)}, u32[]{:S(2)}, u32[]{:S(2)}) collective-permute-start(bf16[1024,128]{1,0:T(8,128)(2,1)S(1)} %bitcast.27), channel_id=1, source_target_pairs={{0,6},{1,7},{2,0},{3,1},{4,2},{5,3},{6,4},{7,5},{8,14},{9,15},{10,... | collective-permute-start | bytes 786440 | tf_op jit(solution)/shard_map/ppermute | solution.py:401
  84.5 17.9 %collective-permute-start.15 = (bf16[1024,128]{1,0:T(8,128)(2,1)S(1)}, bf16[1024,128]{1,0:T(8,128)(2,1)S(1)}, u32[]{:S(2)}, u32[]{:S(2)}) collective-permute-start(bf16[1024,128]{1,0:T(8,128)(2,1)S(1)} %bitcast.25), channel_id=1, source_target_pairs={{0,4},{1,5},{2,6},{3,7},{4,0},{5,1},{6,2},{7,3},{8,12},{9,13},{10,... | collective-permute-start | bytes 786440 | tf_op jit(solution)/shard_map/ppermute | solution.py:401
  104.4 2.0 %collective-permute-start.20 = (f32[192,128]{1,0:T(8,128)S(1)}, f32[192,128]{1,0:T(8,128)S(1)}, u32[]{:S(2)}, u32[]{:S(2)}) collective-permute-start(f32[192,128]{1,0:T(8,128)S(1)} %get-tuple-element.32), channel_id=1, source_target_pairs={{0,1},{1,0},{2,3},{3,2},{4,5},{5,4},{6,7},{7,6},{8,9},{9,8},{10,11... | collective-permute-start | bytes 294920 | tf_op jit(solution)/shard_map/ppermute | solution.py:389
  106.4 5.3 %collective-permute-start.21 = (f32[192,128]{1,0:T(8,128)S(1)}, f32[192,128]{1,0:T(8,128)S(1)}, u32[]{:S(2)}, u32[]{:S(2)}) collective-permute-start(f32[192,128]{1,0:T(8,128)S(1)} %add.71), channel_id=1, source_target_pairs={{0,4},{1,65},{2,6},{3,67},{4,0},{5,69},{6,2},{7,71},{8,12},{9,73},... | collective-permute-start | bytes 294920 | tf_op jit(solution)/shard_map/ppermute | solution.py:401
  108.0 5.0 %collective-permute-start.22 = (f32[192,128]{1,0:T(8,128)S(1)}, f32[192,128]{1,0:T(8,128)S(1)}, u32[]{:S(2)}, u32[]{:S(2)}) collective-permute-start(f32[192,128]{1,0:T(8,128)S(1)} %add.71), channel_id=1, source_target_pairs={{0,2},{1,33},{2,4},{3,35},{4,6},{5,37},{6,0},{7,39},{8,10},{9,41},... | collective-permute-start | bytes 294920 | tf_op jit(solution)/shard_map/ppermute | solution.py:401
  110.5 3.5 %collective-permute-start.23 = (f32[192,128]{1,0:T(8,128)S(1)}, f32[192,128]{1,0:T(8,128)S(1)}, u32[]{:S(2)}, u32[]{:S(2)}) collective-permute-start(f32[192,128]{1,0:T(8,128)S(1)} %add.71), channel_id=1, source_target_pairs={{0,6},{1,97},{2,0},{3,99},{4,2},{5,101},{6,4},{7,103},{8,14},{9,10... | collective-permute-start | bytes 294920 | tf_op jit(solution)/shard_map/ppermute | solution.py:401
  114.0 5.3 %collective-permute-start.24 = (f32[192,128]{1,0:T(8,128)S(1)}, f32[192,128]{1,0:T(8,128)S(1)}, u32[]{:S(2)}, u32[]{:S(2)}) collective-permute-start(f32[192,128]{1,0:T(8,128)S(1)} %add_add_fusion.2), channel_id=1, source_target_pairs={{0,64},{1,17},{2,66},{3,19},{4,68},{5,21},{6,70},{7,23},{8,72},{9,... | collective-permute-start | bytes 294920 | tf_op jit(solution)/shard_map/ppermute | solution.py:401
  116.7 4.8 %collective-permute-start.25 = (f32[192,128]{1,0:T(8,128)S(1)}, f32[192,128]{1,0:T(8,128)S(1)}, u32[]{:S(2)}, u32[]{:S(2)}) collective-permute-start(f32[192,128]{1,0:T(8,128)S(1)} %add_add_fusion.2), channel_id=1, source_target_pairs={{0,32},{1,9},{2,34},{3,11},{4,36},{5,13},{6,38},{7,15},{8,40},{9,1... | collective-permute-start | bytes 294920 | tf_op jit(solution)/shard_map/ppermute | solution.py:401
  117.0 4.5 %collective-permute-start.26 = (f32[192,128]{1,0:T(8,128)S(1)}, f32[192,128]{1,0:T(8,128)S(1)}, u32[]{:S(2)}, u32[]{:S(2)}) collective-permute-start(f32[192,128]{1,0:T(8,128)S(1)} %add_add_fusion.2), channel_id=1, source_target_pairs={{0,96},{1,25},{2,98},{3,27},{4,100},{5,29},{6,102},{7,31},{8,104},... | collective-permute-start | bytes 294920 | tf_op jit(solution)/shard_map/ppermute | solution.py:401
  121.5 5.1 %collective-permute-start.27 = (f32[192,128]{1,0:T(8,128)S(1)}, f32[192,128]{1,0:T(8,128)S(1)}, u32[]{:S(2)}, u32[]{:S(2)}) collective-permute-start(f32[192,128]{1,0:T(8,128)S(1)} %add_add_fusion.1), channel_id=1, source_target_pairs={{0,16},{1,5},{2,18},{3,7},{4,20},{5,1},{6,22},{7,3},{8,24},{9,13},... | collective-permute-start | bytes 294920 | tf_op jit(solution)/shard_map/ppermute | solution.py:401
  122.0 5.6 %collective-permute-start.28 = (f32[192,128]{1,0:T(8,128)S(1)}, f32[192,128]{1,0:T(8,128)S(1)}, u32[]{:S(2)}, u32[]{:S(2)}) collective-permute-start(f32[192,128]{1,0:T(8,128)S(1)} %add_add_fusion.1), channel_id=1, source_target_pairs={{0,8},{1,3},{2,10},{3,5},{4,12},{5,7},{6,14},{7,1},{8,16},{9,11},{... | collective-permute-start | bytes 294920 | tf_op jit(solution)/shard_map/ppermute | solution.py:401
  124.1 3.5 %collective-permute-start.29 = (f32[192,128]{1,0:T(8,128)S(1)}, f32[192,128]{1,0:T(8,128)S(1)}, u32[]{:S(2)}, u32[]{:S(2)}) collective-permute-start(f32[192,128]{1,0:T(8,128)S(1)} %add_add_fusion.1), channel_id=1, source_target_pairs={{0,24},{1,7},{2,26},{3,1},{4,28},{5,3},{6,30},{7,5},{8,0},{9,15},{... | collective-permute-start | bytes 294920 | tf_op jit(solution)/shard_map/ppermute | solution.py:401
  127.7 5.6 %collective-permute-start.30 = (f32[192,128]{1,0:T(8,128)S(1)}, f32[192,128]{1,0:T(8,128)S(1)}, u32[]{:S(2)}, u32[]{:S(2)}) collective-permute-start(f32[192,128]{1,0:T(8,128)S(1)} %add_add_fusion.mine_ref), channel_id=1, source_target_pairs={{0,1},{1,0},{2,3},{3,2},{4,5},{5,4},{6,7},{7,6},{8,9},{9,8},{10,11... | collective-permute-start | bytes 294920 | tf_op jit(solution)/shard_map/ppermute | solution.py:389
